TPU v7x, 256 devices: a whole 4x4x8 slice. The times are simulated.
256 devices in a mesh: tile: 64 (over y, z_lo, x), head: 4 (over z_hi, core).
Axes of the slice: x: 4, y: 4, z: 8 (z_hi: 2, z_lo: 4; z = z_hi * 4 + z_lo), core: 2. Of those that a mesh axis runs over, the one named last changes fastest.
Arguments:
- tokens: bfloat16 [16384, 384], P('tile'), may hold values from -6 to 6
- ln_gain: float32 [384], replicated, may hold values from 0.1 to 1.9
- qkv_weight: bfloat16 [3, 768, 384], P(None, 'head'), may hold values from -0.3125 to 0.3125
- query_pool: bfloat16 [4, 768], P(None, 'head'), may hold values from -3 to 3
- key_pool: bfloat16 [16, 768], P(None, 'head'), may hold values from -1.5 to 1.5
- value_pool: bfloat16 [16, 768], P(None, 'head'), may hold values from -1.5 to 1.5
- proj_weight: bfloat16 [768, 768], P('head'), may hold values from -0.21875 to 0.21875
- skip_weight: bfloat16 [768, 384], P('head'), may hold values from -0.3125 to 0.3125
- cotangent: bfloat16 [4096, 768], P('tile', 'head'), may hold values from -6 to 6
Outputs:
- block_out: bfloat16 [4096, 768], P('tile', 'head')
- input_grad: bfloat16 [16384, 384], P('tile')
- qkv_grad: float32 [3, 768, 384], P(None, 'head')
- proj_grad: float32 [768, 768], P('head')
All inputs are finite; a program needn't handle non-finite values.
Results may differ from a plain program's by a relative error of at most 0.02.
Values may be sent and summed in bfloat16 or wider, within the bound.
No kernel may reach another device: no remote copies, remote signals or barrier semaphores. Data moves between devices by JAX's collectives and lax.ppermute only.
A program may use at most 64 MiB of HBM per device.

v0:
```python
import jax
import jax.numpy as jnp
from jax import lax
from jax.sharding import PartitionSpec as P

HEAD_DIM = 96
TILE_H = 8
TILE_W = 32


EPSILON = 1e-06


def normalize(tokens):
    values_in = tokens.astype(jnp.float32)
    center = values_in - jnp.mean(values_in, axis=-1, keepdims=True)
    inv_std = lax.rsqrt(jnp.mean(center * center, axis=-1, keepdims=True) + EPSILON)
    return (center * inv_std, inv_std)


def pool_field(feature, weight, stride):
    channels = feature.shape[-1]
    cells_grid = feature.reshape(-1, TILE_H // stride, stride, TILE_W // stride, stride, channels)
    kernel = weight.astype(jnp.float32).reshape(stride, stride, channels)
    return jnp.einsum("fiajbc,abc->fijc", cells_grid, kernel).reshape(-1, channels)


def spread_field(upstream, weight, stride):
    channels = upstream.shape[-1]
    cells_grid = upstream.reshape(-1, TILE_H // stride, TILE_W // stride, channels)
    kernel = weight.astype(jnp.float32).reshape(stride, stride, channels)
    return jnp.einsum("fijc,abc->fiajbc", cells_grid, kernel).reshape(-1, channels)


def mean_pool(tokens):
    channels = tokens.shape[-1]
    cells_grid = tokens.astype(jnp.float32).reshape(-1, TILE_H // 2, 2, TILE_W // 2, 2, channels)
    return jnp.sum(cells_grid, axis=(2, 4)).reshape(-1, channels) * 0.25


def expand_rows(upstream):
    channels = upstream.shape[-1]
    cells_grid = upstream.reshape(-1, TILE_H // 2, 1, TILE_W // 2, 1, channels)
    cells_grid = jnp.broadcast_to(
        cells_grid, (cells_grid.shape[0], TILE_H // 2, 2, TILE_W // 2, 2, channels)
    )
    return cells_grid.reshape(-1, channels)


def norm_back(upstream, unit_rows, inv_std, ln_gain):
    scaled = upstream * ln_gain
    return inv_std * (
        scaled
        - jnp.mean(scaled, axis=-1, keepdims=True)
        - unit_rows * jnp.mean(scaled * unit_rows, axis=-1, keepdims=True)
    )


def attend(operands):
    queries, grad_rows, key_rows, value_rows = operands
    scale = HEAD_DIM ** (-0.5)
    scores = jnp.dot(queries, key_rows.T, preferred_element_type=jnp.float32) * scale
    exp_scores = jnp.exp(scores)
    row_total = jnp.sum(exp_scores, axis=-1, keepdims=True)
    attn_probs = (exp_scores / row_total).astype(jnp.bfloat16)
    out_rows = (
        jnp.dot(attn_probs, value_rows, preferred_element_type=jnp.float32)
        + queries.astype(jnp.float32)
    ).astype(jnp.bfloat16)
    dprobs = jnp.dot(grad_rows, value_rows.T, preferred_element_type=jnp.float32)
    probs_wide = attn_probs.astype(jnp.float32)
    row_delta = jnp.sum(probs_wide * dprobs, axis=-1, keepdims=True)
    d_scores = (scale * probs_wide * (dprobs - row_delta)).astype(jnp.bfloat16)
    dquery = jnp.dot(d_scores, key_rows, preferred_element_type=jnp.float32) + grad_rows.astype(
        jnp.float32
    )
    key_grad = jnp.dot(d_scores.T, queries, preferred_element_type=jnp.float32)
    value_grad = jnp.dot(attn_probs.T, grad_rows, preferred_element_type=jnp.float32)
    return (out_rows, dquery, key_grad, value_grad, row_total[:, 0], row_delta[:, 0])


def split_heads(rows_in):
    return rows_in.reshape(rows_in.shape[0], -1, HEAD_DIM).transpose(1, 0, 2)


def join_heads(stacked):
    return stacked.transpose(1, 0, 2).reshape(stacked.shape[1], -1)


def local(
    tokens,
    ln_gain,
    qkv_weight,
    query_pool,
    key_pool,
    value_pool,
    proj_weight,
    skip_weight,
    cotangent,
):
    unit_rows, inv_std = normalize(tokens)
    normed = (unit_rows * ln_gain).astype(jnp.bfloat16)
    projected = [
        jnp.dot(normed, qkv_weight[which].T, preferred_element_type=jnp.float32)
        for which in range(3)
    ]
    query_pooled = pool_field(projected[0], query_pool, 2).astype(jnp.bfloat16)
    key_pooled = pool_field(projected[1], key_pool, 4).astype(jnp.bfloat16)
    value_pooled = pool_field(projected[2], value_pool, 4).astype(jnp.bfloat16)
    all_keys, all_values = (
        lax.all_gather(key_pooled, "tile", axis=0, tiled=True),
        lax.all_gather(value_pooled, "tile", axis=0, tiled=True),
    )
    full_cotangent = lax.all_gather(cotangent, "head", axis=1, tiled=True)
    d_attended = jnp.dot(full_cotangent, proj_weight.T, preferred_element_type=jnp.float32).astype(
        jnp.bfloat16
    )
    head_outs, query_grads, key_grads, value_grads, row_totals, row_deltas = lax.map(
        attend,
        (
            split_heads(query_pooled),
            split_heads(d_attended),
            split_heads(all_keys),
            split_heads(all_values),
        ),
    )
    attended = join_heads(head_outs)
    head_part = jnp.dot(attended, proj_weight, preferred_element_type=jnp.float32)
    summed = lax.psum_scatter(
        head_part.astype(jnp.bfloat16), "head", scatter_dimension=1, tiled=True
    ).astype(jnp.float32)
    pooled_input = mean_pool(tokens).astype(jnp.bfloat16)
    block_out = (
        summed + jnp.dot(pooled_input, skip_weight.T, preferred_element_type=jnp.float32)
    ).astype(jnp.bfloat16)
    proj_part = jnp.dot(attended.T, full_cotangent, preferred_element_type=jnp.float32)
    d_pooled_part = jnp.dot(cotangent, skip_weight, preferred_element_type=jnp.float32)
    own_keys, own_values = (
        lax.psum_scatter(key_grads, "tile", scatter_dimension=1, tiled=True),
        lax.psum_scatter(value_grads, "tile", scatter_dimension=1, tiled=True),
    )
    d_projected = jnp.stack(
        [
            spread_field(join_heads(query_grads), query_pool, 2),
            spread_field(join_heads(own_keys), key_pool, 4),
            spread_field(join_heads(own_values), value_pool, 4),
        ]
    ).astype(jnp.bfloat16)
    qkv_part = jnp.stack(
        [
            jnp.dot(d_projected[which].T, normed, preferred_element_type=jnp.float32)
            for which in range(3)
        ]
    )
    qkv_grad, proj_grad = lax.psum((qkv_part, proj_part), "tile")
    d_normed_part = jnp.dot(d_projected[0], qkv_weight[0], preferred_element_type=jnp.float32)
    d_normed_part = d_normed_part + jnp.dot(
        d_projected[1], qkv_weight[1], preferred_element_type=jnp.float32
    )
    d_normed_part = d_normed_part + jnp.dot(
        d_projected[2], qkv_weight[2], preferred_element_type=jnp.float32
    )
    d_normed, d_pooled = (
        lax.psum(d_normed_part.astype(jnp.bfloat16), "head").astype(jnp.float32),
        lax.psum(d_pooled_part.astype(jnp.bfloat16), "head").astype(jnp.float32),
    )
    input_grad = (
        norm_back(d_normed, unit_rows, inv_std, ln_gain) + expand_rows(d_pooled) * 0.25
    ).astype(jnp.bfloat16)
    return (block_out, input_grad, qkv_grad, proj_grad)


def solution(mesh):
    placed = (
        P("tile", None),
        P(),
        P(None, "head", None),
        P(None, "head"),
        P(None, "head"),
        P(None, "head"),
        P("head", None),
        P("head", None),
        P("tile", "head"),
    )
    return jax.shard_map(
        local,
        mesh=mesh,
        in_specs=placed,
        out_specs=(P("tile", "head"), P("tile", None), P(None, "head", None), P("head", None)),
        check_vma=False,
    )
```

profile of v0, /device:TPU:2, one launch (start us, length us, event | category | flops | bytes accessed | tf_op | source)
XLA Modules:
  0.0 1889.7 jit_solution(13723024882109514639)
XLA Ops:
  8.1 1.1 convert_reduce_fusion
  11.6 183.9 %all_gather.9 = bf16[1024,192]{1,0:T(8,128)(2,1)S(1)} all-gather(bf16[16,192]{1,0:T(8,128)(2,1)S(1)} %bitcast.258), channel_id=1, replica_groups=mesh['tile'=64,'head'=4] {'tile'}, dimensions={0}, use_global_device_ids=true | all-gather | bytes 399360 | tf_op jit(solution)/shard_map/all_gather | solution.py:111
  196.6 188.6 %all_gather.10 = bf16[1024,192]{1,0:T(8,128)(2,1)S(1)} all-gather(bf16[16,192]{1,0:T(8,128)(2,1)S(1)} %bitcast.257), channel_id=1, replica_groups=mesh['tile'=64,'head'=4] {'tile'}, dimensions={0}, use_global_device_ids=true | all-gather | bytes 399360 | tf_op jit(solution)/shard_map/all_gather | solution.py:112
  385.8 1.2 fusion.38
  387.1 9.5 all-gather
  397.2 3.2 while.16
  400.4 1.3 copy.39
  401.8 1.3 copy.40
  403.4 0.8 copy.65
  404.3 1.1 fusion.61
  407.1 0.7 copy-done.5
  408.0 22.7 %psum.29 = bf16[64,384]{1,0:T(8,128)(2,1)S(1)} all-reduce(bf16[64,384]{1,0:T(8,128)(2,1)S(1)} %convolution_convert_fusion.1), channel_id=1, replica_groups=mesh['tile'=64,'head'=4] {'head'}, use_global_device_ids=true, to_apply=%region_13.14 | all-reduce | flops 24576 | bytes 98304 | tf_op jit(solution)/shard_map/psum | solution.py:165
  432.6 685.0 %all-reduce.12.cloned.1.call-done = (f32[2,1024,96]{2,0,1:T(2,128)}, f32[2,1024,96]{2,0,1:T(2,128)}) async-done(((f32[2,1024,96]{2,0,1:T(2,128)}, f32[2,1024,96]{2,0,1:T(2,128)}), (f32[2,1024,96]{2,0,1:T(2,128)}, f32[2,1024,96]{2,0,1:T(2,128)})) %all-reduce.12.cloned.1.call-update) | async-done | bytes 1572880
  1117.6 0.7 dynamic-slice_bitcast_fusion
  1119.2 0.9 fusion.34
  1120.5 1.0 pad_maximum_fusion
  1122.2 0.9 copy.66
  1123.1 0.8 fusion.41
  1123.9 48.2 %all-reduce.8.cloned.1.call-done = bf16[256,384]{1,0:T(8,128)(2,1)} async-done(((bf16[256,384]{1,0:T(8,128)(2,1)}), bf16[256,384]{1,0:T(8,128)(2,1)}) %all-reduce.8.cloned.1.call-update) | async-done | bytes 196624 | tf_op jit(solution)/shard_map/psum | solution.py:164
  1172.1 1.2 fusion.42
  1173.4 0.9 add_convert_fusion
  1174.3 704.8 %all-reduce.10.cloned.1.call-done = (f32[3,192,384]{2,1,0:T(8,128)}, f32[192,768]{1,0:T(8,128)}) async-done(((f32[3,192,384]{2,1,0:T(8,128)}, f32[192,768]{1,0:T(8,128)}), (f32[3,192,384]{2,1,0:T(8,128)}, f32[192,768]{1,0:T(8,128)})) %all-reduce.10.cloned.1.call-update) | async-done | bytes 1474576 | tf_op jit(solution)/shard_map/psum | solution.py:155
  1879.1 2.2 copy.102
  1881.3 0.8 copy.103
  (105 shorter events, 13.3 us)
Async XLA Ops:
  8.0 388.8 %copy-start = (bf16[192,768]{1,0:T(8,128)(2,1)S(1)}, bf16[192,768]{1,0:T(8,128)(2,1)}, u32[]{:S(2)}) copy-start(bf16[192,768]{1,0:T(8,128)(2,1)} %param.17) | copy-start | bytes 884740
  8.0 1.2 copy-start.1
  8.0 1109.6 %all-reduce.12.cloned.1.call-start = ((), (), s32[]{:S(2)}) async-start(), calls=%async_computation.4 | async-start | bytes 4194304
  9.4 0.7 copy-start.9
  10.2 1.0 copy-start.6
  10.3 0.7 copy-start.10
  195.5 0.7 copy-start.11
  385.1 0.7 copy-start.12
  385.8 1.3 copy-start.8
  387.0 10.2 copy-start.2
  403.1 719.1 %reduce-scatter.4.cloned.1.call-start = ((), (), s32[]{:S(2)}) async-start(), calls=%async_computation.2 | async-start | bytes 245760
  404.3 767.8 %all-reduce.8.cloned.1.call-start = ((), (), s32[]{:S(2)}) async-start(), calls=%async_computation.1 | async-start | bytes 393216 | tf_op jit(solution)/shard_map/psum | solution.py:164
  405.7 1.0 copy-start.7
  406.9 0.9 copy-start.5
  430.7 0.7 copy-start.13
  1120.2 759.0 %all-reduce.10.cloned.1.call-start = ((), (), s32[]{:S(2)}) async-start(), calls=%async_computation.3 | async-start | bytes 2949120 | tf_op jit(solution)/shard_map/psum | solution.py:155
  1172.1 1.3 copy-start.3
  1879.1 2.2 copy-start.4
Sparse Core Ops, SparseCore 0:
  403.2 714.3 all-reduce.11
Sparse Core Ops, SparseCore 1:
  406.8 31.5 reduce-scatter.3
  1120.3 51.8 all-reduce.7
  1175.3 703.8 all-reduce.9
where the time goes:
time: 1890 us
  waiting for transfers between devices  1440 us (76%)
  blocking collectives  405 us (21%)
    psum x1, waiting for transfers between devices, local(): qkv_grad, proj_grad = lax.psum((qkv_part, proj_part), 'tile')  705 us
    unnamed x6, waiting for transfers between devices  685 us
    all_gather x1, blocking collectives, local(): lax.all_gather(value_pooled, 'tile', axis=0, tiled=True)  189 us
    all_gather x1, blocking collectives, local(): lax.all_gather(key_pooled, 'tile', axis=0, tiled=True)  184 us
    psum x1, waiting for transfers between devices, local(): lax.psum(d_normed_part.astype(jnp.bfloat16), 'head').astype(jnp.float32)  48.2 us
  transfers between devices with their start and end apart: 4, of which 3 were waited for; matrix products, arithmetic and copies ran while one was open for 1% of the time, Pallas kernels for 0%

commit v1 on v0

v1 whole, which is shorter than its diff:
```python
import numpy as np

import jax
import jax.numpy as jnp
from jax import lax
from jax.experimental import pallas as pl
from jax.experimental.pallas import tpu as pltpu
from jax.sharding import Mesh
from jax.sharding import PartitionSpec as P

HEAD_DIM = 96
EPSILON = 1e-06
F32 = jnp.float32
BF16 = jnp.bfloat16
TILE = ("y", "z", "x")
HEAD = ("half", "core")
PLANE = ("y", "x")


def shift(block, axis, step):
    return lax.ppermute(block, axis, [(i, (i + step) % 4) for i in range(4)])


def swap(block, axis):
    return lax.ppermute(block, axis, [(0, 1), (1, 0)])


def exchange_plane(blocks):
    return lax.all_to_all(blocks, PLANE, 0, 0, tiled=True)


def gather_plane(block):
    return exchange_plane(jnp.broadcast_to(block[None], (16, *block.shape)))


def sum_four(parts):
    wide = [p.astype(F32) for p in parts]
    return (wide[0] + wide[2]) + (wide[1] + wide[3])


def fuse(function, outs, name):
    def call(*operands):
        count = len(operands)

        def kernel(*refs):
            results = function(*[ref[...] for ref in refs[:count]])
            for ref, result in zip(refs[count:], results):
                ref[...] = result

        return pl.pallas_call(
            kernel,
            out_shape=[jax.ShapeDtypeStruct(shape, dtype) for shape, dtype in outs],
            compiler_params=pltpu.CompilerParams(vmem_limit_bytes=48 * 1024 * 1024),
            name=name,
        )(*operands)

    return call


def dot(a, b, contract):
    return lax.dot_general(a, b, (contract, ((), ())), preferred_element_type=F32)


def dot_nn(a, b):
    return dot(a, b, ((1,), (0,)))


def dot_nt(a, b):
    return dot(a, b, ((1,), (1,)))


def dot_tn(a, b):
    return dot(a, b, ((0,), (0,)))


def token_of(place):
    a, b, r, c = place >> 6, (place >> 4) & 3, (place >> 3) & 1, place & 7
    return (4 * r + a) * 32 + 4 * c + b


def query_of(place):
    a, b, r, c = place >> 5, (place >> 4) & 1, (place >> 3) & 1, place & 7
    return (2 * r + a) * 16 + 2 * c + b


def selector(count, source, transposed):
    rows = lax.broadcasted_iota(jnp.int32, (count, count), 0)
    columns = lax.broadcasted_iota(jnp.int32, (count, count), 1)
    hit = source(columns) == rows if transposed else source(rows) == columns
    return jnp.where(hit, 1.0, 0.0).astype(BF16)


def normalize(values_in):
    center = values_in - jnp.mean(values_in, axis=-1, keepdims=True)
    inv_std = lax.rsqrt(jnp.mean(center * center, axis=-1, keepdims=True) + EPSILON)
    return center * inv_std, inv_std


def pool_keys(feature, weight):
    wide = weight.astype(F32)
    total = wide[0:1] * feature[0:16]
    for k in range(1, 16):
        total = total + wide[k : k + 1] * feature[16 * k : 16 * k + 16]
    return total


def spread_keys(upstream, weight):
    wide = weight.astype(F32)
    return jnp.concatenate([wide[k : k + 1] * upstream for k in range(16)], axis=0)


def query_blocks():
    out = []
    for a2 in range(2):
        for b2 in range(2):
            out.append(
                [
                    (2 * a1 + b1, (2 * a2 + a1) * 4 + 2 * b2 + b1)
                    for a1 in range(2)
                    for b1 in range(2)
                ]
            )
    return out


def pool_queries(feature, weight):
    wide = weight.astype(F32)
    rows = []
    for members in query_blocks():
        total = None
        for tap, block in members:
            term = feature[16 * block : 16 * block + 16]
            if weight is not None:
                term = wide[tap : tap + 1] * term
            total = term if total is None else total + term
        rows.append(total)
    return jnp.concatenate(rows, axis=0)


def spread_queries(upstream, weight):
    wide = weight.astype(F32)
    blocks = [None] * 16
    for place, members in enumerate(query_blocks()):
        for tap, block in members:
            blocks[block] = wide[tap : tap + 1] * upstream[16 * place : 16 * place + 16]
    return jnp.concatenate(blocks, axis=0)


def front(tokens, ln_gain, weight_kv, key_pool, value_pool):
    held = dot_nn(selector(256, token_of, False), tokens)
    unit, _ = normalize(held)
    normed = (unit * ln_gain).astype(BF16)
    key_pooled = pool_keys(dot_nt(normed, weight_kv[1]), key_pool)
    value_pooled = pool_keys(dot_nt(normed, weight_kv[2]), value_pool)
    both = jnp.concatenate([key_pooled, value_pooled], axis=1).astype(BF16)
    return both, normed, held.astype(BF16)


def middle(normed, held, weight_q, query_pool, full_cotangent, cotangent, proj_weight, skip_weight):
    query_pooled = pool_queries(dot_nt(normed, weight_q[0]), query_pool).astype(BF16)
    to_held = selector(64, query_of, False)
    held_cotangent = dot_nn(to_held, full_cotangent).astype(BF16)
    d_attended = dot_nt(held_cotangent, proj_weight).astype(BF16)
    ones = jnp.ones((4, held.shape[1]), F32)
    pooled_input = (pool_queries(held.astype(F32), ones) * 0.25).astype(BF16)
    natural = dot_nn(selector(64, query_of, True), pooled_input).astype(BF16)
    skipped = dot_nt(natural, skip_weight)
    own_cotangent = dot_nn(to_held, cotangent).astype(BF16)
    d_pooled = dot_nn(own_cotangent, skip_weight).astype(BF16)
    return query_pooled, d_attended, held_cotangent, skipped, d_pooled


def attend(rows_kv, query_pooled, d_attended):
    rows_kv = rows_kv.reshape(1024, 384)
    scale = HEAD_DIM ** (-0.5)
    lanes = lax.broadcasted_iota(jnp.int32, (64, 192), 1)
    first = lanes < HEAD_DIM
    nothing = jnp.zeros((64, 192), BF16)

    def masked(rows_in):
        wide = rows_in.astype(F32)
        return jnp.concatenate(
            [jnp.where(first, wide, 0.0), jnp.where(first, 0.0, wide)], axis=0
        ).astype(BF16)

    blank = jnp.concatenate([nothing, nothing], axis=0)
    packed = jnp.concatenate(
        [
            jnp.concatenate([masked(query_pooled), blank], axis=1),
            jnp.concatenate([blank, masked(d_attended)], axis=1),
        ],
        axis=0,
    )
    products = dot_nt(packed, rows_kv)
    exp_scores = jnp.exp(products[:128] * scale)
    row_total = jnp.sum(exp_scores, axis=-1, keepdims=True)
    attn_probs = (exp_scores / row_total).astype(BF16)
    dprobs = products[128:]
    probs_wide = attn_probs.astype(F32)
    row_delta = jnp.sum(probs_wide * dprobs, axis=-1, keepdims=True)
    d_scores = (scale * probs_wide * (dprobs - row_delta)).astype(BF16)
    both = jnp.concatenate([d_scores, attn_probs], axis=0)
    rows_grad = dot_tn(both, packed).astype(BF16).reshape(16, 64, 384)
    mixed = dot_nn(both, rows_kv)
    from_keys, from_values = mixed[:128, :192], mixed[128:, 192:]
    query_grad = jnp.where(first, from_keys[:64], from_keys[64:]) + d_attended.astype(F32)
    attended = (
        jnp.where(first, from_values[:64], from_values[64:]) + query_pooled.astype(F32)
    ).astype(BF16)
    return rows_grad, query_grad, attended


def cut(rows_in):
    return [rows_in[:, i : i + 128] for i in range(0, rows_in.shape[1], 128)]


def after(query_grad, attended, normed, query_pool, held_cotangent, proj_weight):
    d_queries = spread_queries(query_grad, query_pool).astype(BF16)
    pieces = cut(dot_tn(d_queries, normed)) + cut(dot_tn(attended, held_cotangent))
    natural = dot_nn(selector(64, query_of, True), attended).astype(BF16)
    head_part = dot_nn(natural, proj_weight).astype(BF16)
    return jnp.stack(pieces).astype(BF16), d_queries, head_part


def weights(parts, normed, d_queries, key_pool, value_pool, qkv_weight, pieces):
    total = sum_four([parts[k] for k in range(4)])
    d_keys = spread_keys(total[:, :192], key_pool).astype(BF16)
    d_values = spread_keys(total[:, 192:], value_pool).astype(BF16)
    more = jnp.stack(cut(dot_tn(d_keys, normed)) + cut(dot_tn(d_values, normed))).astype(BF16)
    blank = jnp.zeros((1, 192, 128), BF16)
    d_normed = dot_nn(d_queries, qkv_weight[0])
    d_normed = d_normed + dot_nn(d_keys, qkv_weight[1])
    d_normed = d_normed + dot_nn(d_values, qkv_weight[2])
    return jnp.concatenate([pieces, more, blank], axis=0), d_normed.astype(BF16)


def finish(pieces):
    wide = pieces.astype(F32)

    def join(start, count):
        return jnp.concatenate([wide[start + i] for i in range(count)], axis=1)

    qkv_grad = jnp.stack([join(0, 3), join(9, 3), join(12, 3)])
    return qkv_grad, join(3, 6)


def back(sum_a, sum_b, held, ln_gain):
    total = sum_a.astype(F32) + sum_b.astype(F32)
    unit, inv_std = normalize(held.astype(F32))
    scaled = total[:128] * ln_gain
    grad = inv_std * (
        scaled
        - jnp.mean(scaled, axis=-1, keepdims=True)
        - unit * jnp.mean(scaled * unit, axis=-1, keepdims=True)
    )
    pooled = total[128:160] * 0.25
    spread = []
    for block in range(8):
        place = (block % 4) // 2
        spread.append(pooled[16 * place : 16 * place + 16])
    return ((grad + jnp.concatenate(spread, axis=0)).astype(BF16),)


def unpermute(rows_in):
    return (dot_nn(selector(256, token_of, True), rows_in).astype(BF16),)


def local(
    tokens,
    ln_gain,
    qkv_weight,
    query_pool,
    key_pool,
    value_pool,
    proj_weight,
    skip_weight,
    cotangent,
):
    core, half = lax.axis_index("core"), lax.axis_index("half")
    gain = ln_gain.reshape(1, -1)

    def pick(stacked, place, axis=0):
        return lax.dynamic_index_in_dim(stacked, place, axis, keepdims=False)

    other = swap(cotangent, "core")
    pair = jnp.where(
        core == 0,
        jnp.concatenate([cotangent, other], axis=1),
        jnp.concatenate([other, cotangent], axis=1),
    )
    far = swap(pair, "half")
    full_cotangent = jnp.where(
        half == 0, jnp.concatenate([pair, far], axis=1), jnp.concatenate([far, pair], axis=1)
    )

    own_kv, normed, held = fuse(
        front, [((16, 384), BF16), ((256, 384), BF16), ((256, 384), BF16)], "front"
    )(tokens, gain, qkv_weight, key_pool, value_pool)
    line_kv = jnp.concatenate([own_kv] + [shift(own_kv, "z", k) for k in (1, 2, 3)], axis=0)
    rows_kv = gather_plane(line_kv)

    query_pooled, d_attended, held_cotangent, skipped, d_pooled = fuse(
        middle,
        [
            ((64, 192), BF16),
            ((64, 192), BF16),
            ((64, 768), BF16),
            ((64, 192), F32),
            ((64, 384), BF16),
        ],
        "middle",
    )(normed, held, qkv_weight, query_pool, full_cotangent, cotangent, proj_weight, skip_weight)

    rows_grad, query_grad, attended = fuse(
        attend, [((16, 64, 384), BF16), ((64, 192), F32), ((64, 192), BF16)], "attend"
    )(rows_kv, query_pooled, d_attended)

    arrived = exchange_plane(rows_grad)
    line = jnp.sum(arrived.astype(F32), axis=0).astype(BF16).reshape(4, 16, 384)
    parts = jnp.stack([line[0]] + [shift(line[k], "z", -k) for k in (1, 2, 3)])

    pieces, d_queries, head_part = fuse(
        after, [((9, 192, 128), BF16), ((256, 192), BF16), ((64, 768), BF16)], "after"
    )(query_grad, attended, normed, query_pool, held_cotangent, proj_weight)

    pieces, d_normed = fuse(weights, [((16, 192, 128), BF16), ((256, 384), BF16)], "weights")(
        parts, normed, d_queries, key_pool, value_pool, qkv_weight, pieces
    )

    quarters = head_part.reshape(64, 2, 2, 192)

    def for_core(place):
        rows_out = pick(quarters, place, 2).reshape(64, 384)
        return jnp.concatenate(
            [
                pick(d_normed.reshape(2, 128, 384), place),
                pick(d_pooled.reshape(2, 32, 384), place),
                rows_out,
            ],
            axis=0,
        )

    both = (
        for_core(core).astype(F32) + swap(for_core(1 - core), "core").astype(F32)
    ).astype(BF16)
    rows_out = both[160:].reshape(64, 2, 192)
    sent = jnp.concatenate(
        [both[:160], pick(rows_out, 1 - half, 1).reshape(32, 384)], axis=0
    )
    taken = swap(sent, "half")

    reduced = jnp.sum(exchange_plane(pieces).astype(F32), axis=0).astype(BF16)
    reduced = sum_four([reduced] + [shift(reduced, "z", k) for k in (1, 2, 3)]).astype(BF16)
    qkv_grad, proj_grad = fuse(finish, [((3, 192, 384), F32), ((192, 768), F32)], "finish")(
        gather_plane(reduced)
    )

    summed = pick(rows_out, half, 1).astype(F32) + taken[160:].reshape(64, 192).astype(F32)
    block_out = (summed + skipped).astype(BF16)
    (own_rows,) = fuse(back, [((128, 384), BF16)], "back")(
        both[:160], taken[:160], pick(held.reshape(2, 128, 384), core), gain
    )
    other_rows = swap(own_rows, "core")
    ordered = jnp.where(
        core == 0,
        jnp.concatenate([own_rows, other_rows]),
        jnp.concatenate([other_rows, own_rows]),
    )
    (input_grad,) = fuse(unpermute, [((256, 384), BF16)], "unpermute")(ordered)
    return (block_out, input_grad, qkv_grad, proj_grad)


def solution(mesh):
    grid = Mesh(
        np.asarray(mesh.devices).reshape(4, 4, 4, 2, 2), ("y", "z", "x", "half", "core")
    )
    placed = (
        P(TILE, None),
        P(),
        P(None, HEAD, None),
        P(None, HEAD),
        P(None, HEAD),
        P(None, HEAD),
        P(HEAD, None),
        P(HEAD, None),
        P(TILE, HEAD),
    )
    return jax.shard_map(
        local,
        mesh=grid,
        in_specs=placed,
        out_specs=(P(TILE, HEAD), P(TILE, None), P(None, HEAD, None), P(HEAD, None)),
        check_vma=False,
    )
```

time: 1890 us -> 110 us (0.06)
  waiting for transfers between devices: 1440 us -> 28.4 us
  blocking collectives: 405 us -> 18.5 us
  starting transfers between devices: 0.17 us -> 42.8 us
    psum x2 -> x0, waiting for transfers between devices: 753 us -> none  [the longest x1 705 us: local(): qkv_grad, proj_grad = lax.psum((qkv_part, proj_part), 'tile')]
    unnamed x6 -> x0, waiting for transfers between devices: 685 us -> none
    all_gather x3 -> x0, blocking collectives: 382 us -> none  [the longest x1 189 us: local(): lax.all_gather(value_pooled, 'tile', axis=0, tiled=True)]
    ppermute x0 -> x14, starting transfers between devices: none -> 25.5 us  [the longest x9 13.7 us: shift(): return lax.ppermute(block, axis, [(i, (i + step) % 4) for i in range(4)])]
    psum x1 -> x0, blocking collectives: 22.7 us -> none  [local(): lax.psum(d_pooled_part.astype(jnp.bfloat16), 'head').astype(jnp.float32)]
    ppermute x0 -> x14, waiting for transfers between devices: none -> 20.3 us  [the longest x9 11.1 us: shift(): return lax.ppermute(block, axis, [(i, (i + step) % 4) for i in range(4)])]
  transfers between devices with their start and end apart: 4 -> 17, of which waited for: 3 -> 14; matrix products, arithmetic and copies ran while one was open for 1% -> 3% of each run, Pallas kernels for 0% -> 2%
where the time goes in v1:
time: 110 us; the launch traced here: 108 us
  starting transfers between devices  42.8 us (39%)
  waiting for transfers between devices  28.4 us (26%)
  blocking collectives  18.5 us (17%)
  local copies, waits for them, and re-layouts  9.34 us (8%)
  Pallas kernels  7.02 us (6%)
  other arithmetic  1.14 us (1%)
    all_to_all x1, blocking collectives, exchange_plane(): return lax.all_to_all(blocks, PLANE, 0, 0, tiled=True)  18.5 us
    all_to_all x3, starting transfers between devices, exchange_plane(): return lax.all_to_all(blocks, PLANE, 0, 0, tiled=True)  17.3 us
    ppermute x9, starting transfers between devices, shift(): return lax.ppermute(block, axis, [(i, (i + step) % 4) for i in range(4)])  13.7 us
    ppermute x5, starting transfers between devices, swap(): return lax.ppermute(block, axis, [(0, 1), (1, 0)])  11.8 us
    ppermute x9, waiting for transfers between devices, shift(): return lax.ppermute(block, axis, [(i, (i + step) % 4) for i in range(4)])  11.1 us
    ppermute x5, waiting for transfers between devices, swap(): return lax.ppermute(block, axis, [(0, 1), (1, 0)])  9.2 us
    all_to_all x3, waiting for transfers between devices, exchange_plane(): return lax.all_to_all(blocks, PLANE, 0, 0, tiled=True)  8.12 us
    pallas_call x8, Pallas kernels, call(): pl.pallas_call(kernel, out_shape=[jax.ShapeDtypeStruct(shape, dtype) for...  7.02 us
  transfers between devices with their start and end apart: 17, of which 14 were waited for; matrix products, arithmetic and copies ran while one was open for 3% of the time, Pallas kernels for 2%

profile of v1, /device:TPU:2, one launch (start us, length us, event | category | flops | bytes accessed | tf_op | source)
XLA Modules:
  0.0 108.1 jit_solution(4747980746508623293)
XLA Ops:
  1.3 1.0 copy-done
  5.4 4.6 %collective-permute-start.2 = (bf16[16,384]{1,0:T(8,128)(2,1)S(1)}, bf16[16,384]{1,0:T(8,128)(2,1)S(1)}, u32[]{:S(2)}, u32[]{:S(2)}) collective-permute-start(bf16[16,384]{1,0:T(8,128)(2,1)S(1)} %get-tuple-element.22), channel_id=1, source_target_pairs={{0,48},{16,0},{32,16},{48,32},{1,49},{17,1},{33,17},{49,33},{2,50}... | collective-permute-start | bytes 36872 | tf_op jit(solution)/shard_map/ppermute | solution.py:21
  11.4 3.2 %collective-permute-done.1 = bf16[16,384]{1,0:T(8,128)(2,1)S(1)} collective-permute-done((bf16[16,384]{1,0:T(8,128)(2,1)S(1)}, bf16[16,384]{1,0:T(8,128)(2,1)S(1)}, u32[]{:S(2)}, u32[]{:S(2)}) %collective-permute-start.1) | collective-permute-done | bytes 12320 | tf_op jit(solution)/shard_map/ppermute | solution.py:21
  15.5 1.0 broadcast_in_dim.4
  16.5 7.6 %all-to-all-start = ((bf16[16,64,384]{2,1,0:T(8,128)(2,1)}), bf16[16,64,384]{2,1,0:T(8,128)(2,1)S(1)}, u32[]{:S(2)}, u32[]{:S(2)}) async-start(bf16[16,64,384]{2,1,0:T(8,128)(2,1)} %broadcast_in_dim.4), calls=%async_computation | async-start | bytes 1572864 | tf_op jit(solution)/shard_map/all_to_all | solution.py:29
  24.2 1.2 %collective-permute-done.3 = bf16[64,192]{1,0:T(8,128)(2,1)S(1)} collective-permute-done((bf16[64,192]{1,0:T(8,128)(2,1)S(1)}, bf16[64,192]{1,0:T(8,128)(2,1)S(1)}, u32[]{:S(2)}, u32[]{:S(2)}) %collective-permute-start.3) | collective-permute-done | bytes 24608 | tf_op jit(solution)/shard_map/ppermute | solution.py:25
  25.5 5.1 %collective-permute-start.4 = (bf16[64,384]{1,0:T(8,128)(2,1)S(1)}, bf16[64,384]{1,0:T(8,128)(2,1)S(1)}, u32[]{:S(2)}, u32[]{:S(2)}) collective-permute-start(bf16[64,384]{1,0:T(8,128)(2,1)S(1)} %maximum_select_fusion.2), channel_id=1, source_target_pairs={{0,2},{2,0},{1,3},{3,1},{4,6},{6,4},{5,7},{7,5},{8,10},{10,8},{9,1... | collective-permute-start | bytes 147464 | tf_op jit(solution)/shard_map/ppermute | solution.py:25
  30.6 3.0 %collective-permute-done.4 = bf16[64,384]{1,0:T(8,128)(2,1)S(1)} collective-permute-done((bf16[64,384]{1,0:T(8,128)(2,1)S(1)}, bf16[64,384]{1,0:T(8,128)(2,1)S(1)}, u32[]{:S(2)}, u32[]{:S(2)}) %collective-permute-start.4) | collective-permute-done | bytes 49184 | tf_op jit(solution)/shard_map/ppermute | solution.py:25
  35.8 1.5 %attend.1 = (bf16[16,64,384]{2,1,0:T(8,128)(2,1)S(1)}, f32[64,192]{1,0:T(8,128)S(1)}, bf16[64,192]{1,0:T(8,128)(2,1)S(1)}) custom-call(bf16[16,64,384]{2,1,0:T(8,128)(2,1)S(1)} %all-to-all-done.refs_0_, bf16[64,192]{1,0:T(8,128)(2,1)S(1)} %get-tuple-element.25.refs_1_, bf16[64,192]{1,0:T(8,128)(2,1)S(1)} %get-tuple-element.26.refs_2_), custom_call_target="tpu_custom_call" | custom-call | tf_op jit(solution)/shard_map/attend/pallas_call | solution.py:50
  37.2 18.5 %all_to_all.20 = bf16[16,64,384]{2,1,0:T(8,128)(2,1)S(1)} all-to-all(bf16[16,64,384]{2,1,0:T(8,128)(2,1)S(1)} %get-tuple-element.27), channel_id=1, replica_groups=mesh['y'=4,'z'=4,'x'=4,'half'=2,'core'=2] {'y','x'}, dimensions={0} | all-to-all | bytes 1572864 | tf_op jit(solution)/shard_map/all_to_all | solution.py:29
  56.0 1.1 %collective-permute-start.6 = (bf16[16,384]{1,0:T(8,128)(2,1)S(1)}, bf16[16,384]{1,0:T(8,128)(2,1)S(1)}, u32[]{:S(2)}, u32[]{:S(2)}) collective-permute-start(bf16[16,384]{1,0:T(8,128)(2,1)S(1)} %get-tuple-element.50), channel_id=1, source_target_pairs={{0,32},{16,48},{32,0},{48,16},{1,33},{17,49},{33,1},{49,17},{2,34}... | collective-permute-start | bytes 36872 | tf_op jit(solution)/shard_map/ppermute | solution.py:21
  57.1 2.8 %collective-permute-start.5 = (bf16[16,384]{1,0:T(8,128)(2,1)S(1)}, bf16[16,384]{1,0:T(8,128)(2,1)S(1)}, u32[]{:S(2)}, u32[]{:S(2)}) collective-permute-start(bf16[16,384]{1,0:T(8,128)(2,1)S(1)} %get-tuple-element.51), channel_id=1, source_target_pairs={{0,48},{16,0},{32,16},{48,32},{1,49},{17,1},{33,17},{49,33},{2,50}... | collective-permute-start | bytes 36872 | tf_op jit(solution)/shard_map/ppermute | solution.py:21
  60.4 1.1 collective-permute-done.7
  62.7 1.4 %weights.1 = (bf16[16,192,128]{2,1,0:T(8,128)(2,1)}, bf16[256,384]{1,0:T(8,128)(2,1)S(1)}) custom-call(bf16[4,16,384]{2,1,0:T(8,128)(2,1)S(1)} %pad_maximum_fusion.3.refs_0_, bf16[256,384]{1,0:T(8,128)(2,1)S(1)} %get-tuple-element.23.refs_0_.refs_2_.refs_1_, bf16[256,192]{1,0:T(8,128)(2,1)S(1)} %get-tuple-element.31.refs_2_, bf16[16,192]{1,0:T(8,128)(2,1)S(1)} %copy-done.7, ...), custom_call_target="tpu_custom_call" | custom-call | tf_op jit(solution)/shard_map/weights/pallas_call | solution.py:50
  64.1 4.9 %all-to-all-start.2 = ((bf16[16,192,128]{2,1,0:T(8,128)(2,1)}), bf16[16,192,128]{2,1,0:T(8,128)(2,1)S(1)}, u32[]{:S(2)}, u32[]{:S(2)}) async-start(bf16[16,192,128]{2,1,0:T(8,128)(2,1)} %get-tuple-element.37), calls=%async_computation.2 | async-start | bytes 1572864 | tf_op jit(solution)/shard_map/all_to_all | solution.py:29
  70.5 1.3 %collective-permute-done.8 = bf16[224,384]{1,0:T(8,128)(2,1)S(1)} collective-permute-done((bf16[224,384]{1,0:T(8,128)(2,1)S(1)}, bf16[224,384]{1,0:T(8,128)(2,1)S(1)}, u32[]{:S(2)}, u32[]{:S(2)}) %collective-permute-start.8) | collective-permute-done | bytes 172064 | tf_op jit(solution)/shard_map/ppermute | solution.py:25
  72.0 7.3 %all-to-all-done.2 = bf16[16,192,128]{2,1,0:T(8,128)(2,1)S(1)} async-done(((bf16[16,192,128]{2,1,0:T(8,128)(2,1)}), bf16[16,192,128]{2,1,0:T(8,128)(2,1)S(1)}, u32[]{:S(2)}, u32[]{:S(2)}) %all-to-all-start.2) | async-done | bytes 786464 | tf_op jit(solution)/shard_map/all_to_all | solution.py:29
  79.4 3.5 %collective-permute-start.13 = (bf16[192,128]{1,0:T(8,128)(2,1)S(1)}, bf16[192,128]{1,0:T(8,128)(2,1)S(1)}, u32[]{:S(2)}, u32[]{:S(2)}) collective-permute-start(bf16[192,128]{1,0:T(8,128)(2,1)S(1)} %reduce_sum.25), channel_id=1, source_target_pairs={{0,48},{16,0},{32,16},{48,32},{1,49},{17,1},{33,17},{49,33},{2,50}... | collective-permute-start | bytes 147464 | tf_op jit(solution)/shard_map/ppermute | solution.py:21
  84.6 4.1 %collective-permute-done.12 = bf16[192,128]{1,0:T(8,128)(2,1)S(1)} collective-permute-done((bf16[192,128]{1,0:T(8,128)(2,1)S(1)}, bf16[192,128]{1,0:T(8,128)(2,1)S(1)}, u32[]{:S(2)}, u32[]{:S(2)}) %collective-permute-start.12) | collective-permute-done | bytes 49184 | tf_op jit(solution)/shard_map/ppermute | solution.py:21
  88.8 1.0 broadcast_in_dim.5
  89.8 4.8 %all-to-all-start.3 = ((bf16[16,192,128]{2,1,0:T(8,128)(2,1)}), bf16[16,192,128]{2,1,0:T(8,128)(2,1)S(1)}, u32[]{:S(2)}, u32[]{:S(2)}) async-start(bf16[16,192,128]{2,1,0:T(8,128)(2,1)} %broadcast_in_dim.5), calls=%async_computation.3 | async-start | bytes 1572864 | tf_op jit(solution)/shard_map/all_to_all | solution.py:29
  94.7 6.4 %collective-permute-start.9 = (bf16[192,384]{1,0:T(8,128)(2,1)S(1)}, bf16[192,384]{1,0:T(8,128)(2,1)S(1)}, u32[]{:S(2)}, u32[]{:S(2)}) collective-permute-start(bf16[192,384]{1,0:T(8,128)(2,1)S(1)} %pad_maximum_fusion.1), channel_id=1, source_target_pairs={{0,2},{2,0},{1,3},{3,1},{4,6},{6,4},{5,7},{7,5},{8,10},{10,8},{9,1... | collective-permute-start | bytes 442376 | tf_op jit(solution)/shard_map/ppermute | solution.py:25
  101.1 3.1 %collective-permute-done.9 = bf16[192,384]{1,0:T(8,128)(2,1)S(1)} collective-permute-done((bf16[192,384]{1,0:T(8,128)(2,1)S(1)}, bf16[192,384]{1,0:T(8,128)(2,1)S(1)}, u32[]{:S(2)}, u32[]{:S(2)}) %collective-permute-start.9) | collective-permute-done | bytes 147488 | tf_op jit(solution)/shard_map/ppermute | solution.py:25
  106.9 1.2 %finish.1 = (f32[3,192,384]{2,1,0:T(8,128)}, f32[192,768]{1,0:T(8,128)}) custom-call(bf16[16,192,128]{2,1,0:T(8,128)(2,1)S(1)} %all-to-all-done.3.refs_0_), custom_call_target="tpu_custom_call" | custom-call | tf_op jit(solution)/shard_map/finish/pallas_call | solution.py:50
  (72 shorter events, 16.5 us)
Async XLA Ops:
  1.3 1.0 copy-start
  2.3 0.9 copy-start.3
  5.4 6.0 %collective-permute-start.2 = (bf16[16,384]{1,0:T(8,128)(2,1)S(1)}, bf16[16,384]{1,0:T(8,128)(2,1)S(1)}, u32[]{:S(2)}, u32[]{:S(2)}) collective-permute-start(bf16[16,384]{1,0:T(8,128)(2,1)S(1)} %get-tuple-element.22), channel_id=1, source_target_pairs={{0,48},{16,0},{32,16},{48,32},{1,49},{17,1},{33,17},{49,33},{2,50}... | collective-permute-start | bytes 36872 | tf_op jit(solution)/shard_map/ppermute | solution.py:21
  10.0 4.6 %collective-permute-start.1 = (bf16[16,384]{1,0:T(8,128)(2,1)S(1)}, bf16[16,384]{1,0:T(8,128)(2,1)S(1)}, u32[]{:S(2)}, u32[]{:S(2)}) collective-permute-start(bf16[16,384]{1,0:T(8,128)(2,1)S(1)} %get-tuple-element.22), channel_id=1, source_target_pairs={{0,32},{16,48},{32,0},{48,16},{1,33},{17,49},{33,1},{49,17},{2,34}... | collective-permute-start | bytes 36872 | tf_op jit(solution)/shard_map/ppermute | solution.py:21
  10.0 5.5 %collective-permute-start = (bf16[16,384]{1,0:T(8,128)(2,1)S(1)}, bf16[16,384]{1,0:T(8,128)(2,1)S(1)}, u32[]{:S(2)}, u32[]{:S(2)}) collective-permute-start(bf16[16,384]{1,0:T(8,128)(2,1)S(1)} %get-tuple-element.22), channel_id=1, source_target_pairs={{0,16},{16,32},{32,48},{48,0},{1,17},{17,33},{33,49},{49,1},{2,18}... | collective-permute-start | bytes 36872 | tf_op jit(solution)/shard_map/ppermute | solution.py:21
  16.5 7.6 %copy-start.5 = (bf16[64,192]{1,0:T(8,128)(2,1)S(1)}, bf16[64,192]{1,0:T(8,128)(2,1)}, u32[]{:S(2)}) copy-start(bf16[64,192]{1,0:T(8,128)(2,1)} %refs_5_.3) | copy-start | bytes 73732
  16.5 17.1 %copy-start.1 = (bf16[3,192,384]{2,1,0:T(8,128)(2,1)S(1)}, bf16[3,192,384]{2,1,0:T(8,128)(2,1)}, u32[]{:S(2)}) copy-start(bf16[3,192,384]{2,1,0:T(8,128)(2,1)} %refs_5_.5) | copy-start | bytes 1327108
  16.5 17.2 %copy-start.4 = (bf16[192,384]{1,0:T(8,128)(2,1)S(1)}, bf16[192,384]{1,0:T(8,128)(2,1)}, u32[]{:S(2)}) copy-start(bf16[192,384]{1,0:T(8,128)(2,1)} %refs_7_.1) | copy-start | bytes 442372
  16.5 19.3 %all-to-all-start = ((bf16[16,64,384]{2,1,0:T(8,128)(2,1)}), bf16[16,64,384]{2,1,0:T(8,128)(2,1)S(1)}, u32[]{:S(2)}, u32[]{:S(2)}) async-start(bf16[16,64,384]{2,1,0:T(8,128)(2,1)} %broadcast_in_dim.4), calls=%async_computation | async-start | bytes 1572864 | tf_op jit(solution)/shard_map/all_to_all | solution.py:29
  24.1 9.5 %copy-start.2 = (bf16[192,768]{1,0:T(8,128)(2,1)S(1)}, bf16[192,768]{1,0:T(8,128)(2,1)}, u32[]{:S(2)}) copy-start(bf16[192,768]{1,0:T(8,128)(2,1)} %refs_5_.4) | copy-start | bytes 884740
  24.1 1.3 %collective-permute-start.3 = (bf16[64,192]{1,0:T(8,128)(2,1)S(1)}, bf16[64,192]{1,0:T(8,128)(2,1)S(1)}, u32[]{:S(2)}, u32[]{:S(2)}) collective-permute-start(bf16[64,192]{1,0:T(8,128)(2,1)S(1)} %copy-done.5), channel_id=1, source_target_pairs={{0,1},{1,0},{2,3},{3,2},{4,5},{5,4},{6,7},{7,6},{8,9},{9,8},{10,11... | collective-permute-start | bytes 73736 | tf_op jit(solution)/shard_map/ppermute | solution.py:25
  25.5 8.1 %collective-permute-start.4 = (bf16[64,384]{1,0:T(8,128)(2,1)S(1)}, bf16[64,384]{1,0:T(8,128)(2,1)S(1)}, u32[]{:S(2)}, u32[]{:S(2)}) collective-permute-start(bf16[64,384]{1,0:T(8,128)(2,1)S(1)} %maximum_select_fusion.2), channel_id=1, source_target_pairs={{0,2},{2,0},{1,3},{3,1},{4,6},{6,4},{5,7},{7,5},{8,10},{10,8},{9,1... | collective-permute-start | bytes 147464 | tf_op jit(solution)/shard_map/ppermute | solution.py:25
  55.9 5.6 %collective-permute-start.7 = (bf16[16,384]{1,0:T(8,128)(2,1)S(1)}, bf16[16,384]{1,0:T(8,128)(2,1)S(1)}, u32[]{:S(2)}, u32[]{:S(2)}) collective-permute-start(bf16[16,384]{1,0:T(8,128)(2,1)S(1)} %get-tuple-element.49), channel_id=1, source_target_pairs={{0,16},{16,32},{32,48},{48,0},{1,17},{17,33},{33,49},{49,1},{2,18}... | collective-permute-start | bytes 36872 | tf_op jit(solution)/shard_map/ppermute | solution.py:21
  56.0 5.5 %collective-permute-start.6 = (bf16[16,384]{1,0:T(8,128)(2,1)S(1)}, bf16[16,384]{1,0:T(8,128)(2,1)S(1)}, u32[]{:S(2)}, u32[]{:S(2)}) collective-permute-start(bf16[16,384]{1,0:T(8,128)(2,1)S(1)} %get-tuple-element.50), channel_id=1, source_target_pairs={{0,32},{16,48},{32,0},{48,16},{1,33},{17,49},{33,1},{49,17},{2,34}... | collective-permute-start | bytes 36872 | tf_op jit(solution)/shard_map/ppermute | solution.py:21
  57.1 4.9 %collective-permute-start.5 = (bf16[16,384]{1,0:T(8,128)(2,1)S(1)}, bf16[16,384]{1,0:T(8,128)(2,1)S(1)}, u32[]{:S(2)}, u32[]{:S(2)}) collective-permute-start(bf16[16,384]{1,0:T(8,128)(2,1)S(1)} %get-tuple-element.51), channel_id=1, source_target_pairs={{0,48},{16,0},{32,16},{48,32},{1,49},{17,1},{33,17},{49,33},{2,50}... | collective-permute-start | bytes 36872 | tf_op jit(solution)/shard_map/ppermute | solution.py:21
  62.0 0.7 copy-start.9
  64.1 15.1 %all-to-all-start.2 = ((bf16[16,192,128]{2,1,0:T(8,128)(2,1)}), bf16[16,192,128]{2,1,0:T(8,128)(2,1)S(1)}, u32[]{:S(2)}, u32[]{:S(2)}) async-start(bf16[16,192,128]{2,1,0:T(8,128)(2,1)} %get-tuple-element.37), calls=%async_computation.2 | async-start | bytes 1572864 | tf_op jit(solution)/shard_map/all_to_all | solution.py:29
  70.3 1.5 %collective-permute-start.8 = (bf16[224,384]{1,0:T(8,128)(2,1)S(1)}, bf16[224,384]{1,0:T(8,128)(2,1)S(1)}, u32[]{:S(2)}, u32[]{:S(2)}) collective-permute-start(bf16[224,384]{1,0:T(8,128)(2,1)S(1)} %pad_maximum_fusion), channel_id=1, source_target_pairs={{0,1},{1,0},{2,3},{3,2},{4,5},{5,4},{6,7},{7,6},{8,9},{9,8},{10,11... | collective-permute-start | bytes 516104 | tf_op jit(solution)/shard_map/ppermute | solution.py:25
  79.4 5.3 %collective-permute-start.13 = (bf16[192,128]{1,0:T(8,128)(2,1)S(1)}, bf16[192,128]{1,0:T(8,128)(2,1)S(1)}, u32[]{:S(2)}, u32[]{:S(2)}) collective-permute-start(bf16[192,128]{1,0:T(8,128)(2,1)S(1)} %reduce_sum.25), channel_id=1, source_target_pairs={{0,48},{16,0},{32,16},{48,32},{1,49},{17,1},{33,17},{49,33},{2,50}... | collective-permute-start | bytes 147464 | tf_op jit(solution)/shard_map/ppermute | solution.py:21
  82.9 5.9 %collective-permute-start.12 = (bf16[192,128]{1,0:T(8,128)(2,1)S(1)}, bf16[192,128]{1,0:T(8,128)(2,1)S(1)}, u32[]{:S(2)}, u32[]{:S(2)}) collective-permute-start(bf16[192,128]{1,0:T(8,128)(2,1)S(1)} %reduce_sum.25), channel_id=1, source_target_pairs={{0,16},{16,32},{32,48},{48,0},{1,17},{17,33},{33,49},{49,1},{2,18}... | collective-permute-start | bytes 147464 | tf_op jit(solution)/shard_map/ppermute | solution.py:21
  82.9 5.9 %collective-permute-start.11 = (bf16[192,128]{1,0:T(8,128)(2,1)S(1)}, bf16[192,128]{1,0:T(8,128)(2,1)S(1)}, u32[]{:S(2)}, u32[]{:S(2)}) collective-permute-start(bf16[192,128]{1,0:T(8,128)(2,1)S(1)} %reduce_sum.25), channel_id=1, source_target_pairs={{0,32},{16,48},{32,0},{48,16},{1,33},{17,49},{33,1},{49,17},{2,34}... | collective-permute-start | bytes 147464 | tf_op jit(solution)/shard_map/ppermute | solution.py:21
  89.8 17.1 %all-to-all-start.3 = ((bf16[16,192,128]{2,1,0:T(8,128)(2,1)}), bf16[16,192,128]{2,1,0:T(8,128)(2,1)S(1)}, u32[]{:S(2)}, u32[]{:S(2)}) async-start(bf16[16,192,128]{2,1,0:T(8,128)(2,1)} %broadcast_in_dim.5), calls=%async_computation.3 | async-start | bytes 1572864 | tf_op jit(solution)/shard_map/all_to_all | solution.py:29
  94.7 9.5 %collective-permute-start.9 = (bf16[192,384]{1,0:T(8,128)(2,1)S(1)}, bf16[192,384]{1,0:T(8,128)(2,1)S(1)}, u32[]{:S(2)}, u32[]{:S(2)}) collective-permute-start(bf16[192,384]{1,0:T(8,128)(2,1)S(1)} %pad_maximum_fusion.1), channel_id=1, source_target_pairs={{0,2},{2,0},{1,3},{3,1},{4,6},{6,4},{5,7},{7,5},{8,10},{10,8},{9,1... | collective-permute-start | bytes 442376 | tf_op jit(solution)/shard_map/ppermute | solution.py:25
  104.6 1.4 %collective-permute-start.10 = (bf16[128,384]{1,0:T(8,128)(2,1)S(1)}, bf16[128,384]{1,0:T(8,128)(2,1)S(1)}, u32[]{:S(2)}, u32[]{:S(2)}) collective-permute-start(bf16[128,384]{1,0:T(8,128)(2,1)S(1)} %back.1), channel_id=1, source_target_pairs={{0,1},{1,0},{2,3},{3,2},{4,5},{5,4},{6,7},{7,6},{8,9},{9,8},{10,11... | collective-permute-start | bytes 294920 | tf_op jit(solution)/shard_map/ppermute | solution.py:25
  (4 other events, 2.8 us)

commit v2 on v1

v2 whole, which is shorter than its diff:
```python
import numpy as np

import jax
import jax.numpy as jnp
from jax import lax
from jax.experimental import pallas as pl
from jax.experimental.pallas import tpu as pltpu
from jax.sharding import Mesh
from jax.sharding import PartitionSpec as P

HEAD_DIM = 96
EPSILON = 1e-06
F32 = jnp.float32
BF16 = jnp.bfloat16
TILE = ("y", "z", "x")
HEAD = ("half", "core")
PLANE = ("y", "x")


def shift(block, axis, step):
    return lax.ppermute(block, axis, [(i, (i + step) % 4) for i in range(4)])


def swap(block, axis):
    return lax.ppermute(block, axis, [(0, 1), (1, 0)])


def swap_pair(block):
    return lax.ppermute(block, "z", [(i, i ^ 1) for i in range(4)])


def exchange(blocks, axes):
    return lax.all_to_all(blocks, axes, 0, 0, tiled=True)


def sum_four(parts):
    wide = [p.astype(F32) for p in parts]
    return (wide[0] + wide[2]) + (wide[1] + wide[3])


def fuse(function, outs, name, direct=False, flops=None):
    def call(*operands):
        count, stored = len(operands), len(outs)

        def kernel(*refs):
            sources, targets = refs[:count], refs[count : count + stored]
            if direct:
                held = refs[count + stored : -1]
                fetches = [
                    pltpu.make_async_copy(source, target, refs[-1].at[i])
                    for i, (source, target) in enumerate(zip(sources, held))
                ]
                for fetch in fetches:
                    fetch.start()
                for fetch in fetches:
                    fetch.wait()
                sources = held
            results = function(*[ref[...] for ref in sources])
            for ref, result in zip(targets, results):
                ref[...] = result

        scratch = []
        if direct:
            scratch = [pltpu.VMEM(x.shape, x.dtype) for x in operands]
            scratch.append(pltpu.SemaphoreType.DMA((count,)))
        return pl.pallas_call(
            kernel,
            out_shape=[jax.ShapeDtypeStruct(shape, dtype) for shape, dtype in outs],
            in_specs=[pl.BlockSpec(memory_space=pl.ANY if direct else pltpu.VMEM)] * count,
            out_specs=[pl.BlockSpec(memory_space=pltpu.VMEM)] * stored,
            scratch_shapes=scratch,
            compiler_params=pltpu.CompilerParams(vmem_limit_bytes=(60 if direct else 32) * 1024 * 1024),
            cost_estimate=flops
            and pl.CostEstimate(flops=flops, bytes_accessed=0, transcendentals=0),
            name=name,
        )(*operands)

    return call


def either(which, first, second):
    return jnp.where(which == 0, first, second)


def dot(a, b, contract):
    return lax.dot_general(a, b, (contract, ((), ())), preferred_element_type=F32)


def dot_nn(a, b):
    return dot(a, b, ((1,), (0,)))


def dot_nt(a, b):
    return dot(a, b, ((1,), (1,)))


def dot_tn(a, b):
    return dot(a, b, ((0,), (0,)))


def token_of(place):
    a, b, r, c = place >> 6, (place >> 4) & 3, (place >> 3) & 1, place & 7
    return (4 * r + a) * 32 + 4 * c + b


def query_of(place):
    a, b, r, c = place >> 5, (place >> 4) & 1, (place >> 3) & 1, place & 7
    return (2 * r + a) * 16 + 2 * c + b


def selector(count, source, transposed):
    rows = lax.broadcasted_iota(jnp.int32, (count, count), 0)
    columns = lax.broadcasted_iota(jnp.int32, (count, count), 1)
    hit = source(columns) == rows if transposed else source(rows) == columns
    return jnp.where(hit, 1.0, 0.0).astype(BF16)


def normalize(values_in):
    center = values_in - jnp.mean(values_in, axis=-1, keepdims=True)
    inv_std = lax.rsqrt(jnp.mean(center * center, axis=-1, keepdims=True) + EPSILON)
    return center * inv_std, inv_std


def pool_keys(feature, weight):
    wide = weight.astype(F32)
    total = wide[0:1] * feature[0:16]
    for k in range(1, 16):
        total = total + wide[k : k + 1] * feature[16 * k : 16 * k + 16]
    return total


def spread_keys(upstream, weight):
    wide = weight.astype(F32)
    return jnp.concatenate([wide[k : k + 1] * upstream for k in range(16)], axis=0)


def query_blocks():
    out = []
    for a2 in range(2):
        for b2 in range(2):
            out.append(
                [
                    (2 * a1 + b1, (2 * a2 + a1) * 4 + 2 * b2 + b1)
                    for a1 in range(2)
                    for b1 in range(2)
                ]
            )
    return out


def pool_queries(feature, weight):
    wide = weight.astype(F32)
    rows = []
    for members in query_blocks():
        total = None
        for tap, block in members:
            term = feature[16 * block : 16 * block + 16]
            if weight is not None:
                term = wide[tap : tap + 1] * term
            total = term if total is None else total + term
        rows.append(total)
    return jnp.concatenate(rows, axis=0)


def spread_queries(upstream, weight):
    wide = weight.astype(F32)
    blocks = [None] * 16
    for place, members in enumerate(query_blocks()):
        for tap, block in members:
            blocks[block] = wide[tap : tap + 1] * upstream[16 * place : 16 * place + 16]
    return jnp.concatenate(blocks, axis=0)


def front(tokens, ln_gain, weight_kv, key_pool, value_pool):
    held = dot_nn(selector(256, token_of, False), tokens)
    unit, _ = normalize(held)
    normed = (unit * ln_gain[None, :]).astype(BF16)
    key_pooled = pool_keys(dot_nt(normed, weight_kv[1]), key_pool)
    value_pooled = pool_keys(dot_nt(normed, weight_kv[2]), value_pool)
    odd = lax.rem(lax.axis_index("z"), 2)
    blank = jnp.zeros((16, 64), F32)
    rows = [
        jnp.concatenate([key_pooled[:, part], value_pooled[:, part], blank], axis=1)
        for part in (slice(0, HEAD_DIM), slice(HEAD_DIM, 2 * HEAD_DIM))
    ]
    same = either(odd, rows[0], rows[1]).astype(BF16)
    other = either(odd, rows[1], rows[0]).astype(BF16)
    return same, other, normed, held.astype(BF16)


def fold_rows(rows_in):
    count = rows_in.shape[0] // 2
    return jnp.concatenate([rows_in[:count, :192], rows_in[count:, :192]], axis=1)


def unfold_rows(rows_in):
    return jnp.concatenate([rows_in[:, :192], rows_in[:, 192:]], axis=0)


def copy_line(part_0, part_1, part_2, part_3):
    line = jnp.concatenate([part_0, part_1, part_2, part_3], axis=0)
    line = fold_rows(line.astype(F32)).astype(BF16)
    return (jnp.broadcast_to(line[None], (16, 32, 384)),)


def middle(
    normed, held, weight_q, query_pool, cot_0, cot_1, cot_2, cot_3, proj_weight, skip_weight
):
    core, half = lax.axis_index("core"), lax.axis_index("half")
    pairs = [
        jnp.concatenate([either(core, p, q), either(core, q, p)], axis=1)
        for p, q in ((cot_0.astype(F32), cot_1.astype(F32)), (cot_2.astype(F32), cot_3.astype(F32)))
    ]
    full_cotangent = jnp.concatenate(
        [either(half, pairs[0], pairs[1]), either(half, pairs[1], pairs[0])], axis=1
    ).astype(BF16)
    query_pooled = pool_queries(dot_nt(normed, weight_q[0]), query_pool).astype(BF16)
    to_held = selector(64, query_of, False)
    held_cotangent = dot_nn(to_held, full_cotangent).astype(BF16)
    d_attended = dot_nt(held_cotangent, proj_weight).astype(BF16)
    ones = jnp.ones((4, held.shape[1]), F32)
    pooled_input = (pool_queries(held.astype(F32), ones) * 0.25).astype(BF16)
    natural = dot_nn(selector(64, query_of, True), pooled_input).astype(BF16)
    skipped = dot_nt(natural, skip_weight)
    own_cotangent = dot_nn(to_held, cot_0).astype(BF16)
    d_pooled = dot_nn(own_cotangent, skip_weight).astype(BF16)
    blank = jnp.zeros((64, 64), F32)
    queries, grads = query_pooled.astype(F32), d_attended.astype(F32)
    rows = [
        jnp.concatenate([queries[:, part], grads[:, part], blank], axis=1)
        for part in (slice(0, HEAD_DIM), slice(HEAD_DIM, 2 * HEAD_DIM))
    ]
    odd = lax.rem(lax.axis_index("z"), 2)
    mine = either(odd, rows[0], rows[1]).astype(BF16)
    theirs = either(odd, rows[1], rows[0]).astype(BF16)
    return mine, theirs, held_cotangent, skipped, d_pooled


def attend(rows_kv, mine, received):
    rows_kv = unfold_rows(rows_kv.reshape(512, 384))
    scale = HEAD_DIM ** (-0.5)
    wide = jnp.concatenate([mine, received], axis=0).astype(F32)[:, :192]
    lanes = lax.broadcasted_iota(jnp.int32, (128, 192), 1)
    on_keys = lanes < HEAD_DIM
    packed = jnp.concatenate(
        [jnp.where(on_keys, wide, 0.0), jnp.where(on_keys, 0.0, wide)], axis=0
    ).astype(BF16)
    products = dot_nt(packed, rows_kv)
    exp_scores = jnp.exp(products[:128] * scale)
    row_total = jnp.sum(exp_scores, axis=-1, keepdims=True)
    attn_probs = (exp_scores / row_total).astype(BF16)
    dprobs = products[128:]
    probs_wide = attn_probs.astype(F32)
    row_delta = jnp.sum(probs_wide * dprobs, axis=-1, keepdims=True)
    d_scores = (scale * probs_wide * (dprobs - row_delta)).astype(BF16)
    both = jnp.concatenate([d_scores, attn_probs], axis=0)
    rows_grad = fold_rows(dot_tn(both, packed)).astype(BF16).reshape(16, 32, 384)
    mixed = dot_nn(both, rows_kv)
    mixed = jnp.where(on_keys, mixed[:128], mixed[128:])
    mixed = mixed + jnp.concatenate([wide[:, HEAD_DIM:], wide[:, :HEAD_DIM]], axis=1)
    mixed = jnp.concatenate([mixed, jnp.zeros((128, 64), F32)], axis=1)
    return rows_grad, mixed[:64], mixed[64:].astype(BF16)


def cut(rows_in):
    return [rows_in[:, i : i + 128] for i in range(0, rows_in.shape[1], 128)]


def after(mixed, returned, normed, query_pool, held_cotangent, proj_weight):
    odd = lax.rem(lax.axis_index("z"), 2)
    returned = returned.astype(F32)
    first, second = either(odd, mixed, returned), either(odd, returned, mixed)
    query_grad = jnp.concatenate([first[:, :HEAD_DIM], second[:, :HEAD_DIM]], axis=1)
    attended = jnp.concatenate(
        [first[:, HEAD_DIM : 2 * HEAD_DIM], second[:, HEAD_DIM : 2 * HEAD_DIM]], axis=1
    ).astype(BF16)
    d_queries = spread_queries(query_grad, query_pool).astype(BF16)
    pieces = cut(dot_tn(d_queries, normed)) + cut(dot_tn(attended, held_cotangent))
    natural = dot_nn(selector(64, query_of, True), attended).astype(BF16)
    head_part = dot_nn(natural, proj_weight).astype(BF16)
    return jnp.stack(pieces).astype(BF16), d_queries, head_part


def weights(
    part_0,
    part_1,
    part_2,
    part_3,
    normed,
    d_queries,
    key_pool,
    value_pool,
    qkv_weight,
    pieces,
    d_pooled,
    head_part,
):
    core, odd = lax.axis_index("core"), lax.rem(lax.axis_index("z"), 2)
    same = part_0.astype(F32) + part_2.astype(F32)
    other = part_1.astype(F32) + part_3.astype(F32)
    per_head = [either(odd, same, other), either(odd, other, same)]
    key_grad = jnp.concatenate([t[:, :HEAD_DIM] for t in per_head], axis=1)
    value_grad = jnp.concatenate([t[:, HEAD_DIM : 2 * HEAD_DIM] for t in per_head], axis=1)
    d_keys = spread_keys(key_grad, key_pool).astype(BF16)
    d_values = spread_keys(value_grad, value_pool).astype(BF16)
    more = jnp.stack(cut(dot_tn(d_keys, normed)) + cut(dot_tn(d_values, normed))).astype(BF16)
    blank = jnp.zeros((1, 192, 128), BF16)
    d_normed = dot_nn(d_queries, qkv_weight[0])
    d_normed = d_normed + dot_nn(d_keys, qkv_weight[1])
    d_normed = d_normed + dot_nn(d_values, qkv_weight[2])
    pooled, rows = d_pooled.astype(F32), head_part.astype(F32)
    loads = []
    for c in range(2):
        channels = [rows[:, 192 * (2 * p + c) : 192 * (2 * p + c) + 192] for p in range(2)]
        loads.append(
            jnp.concatenate(
                [
                    d_normed[128 * c : 128 * c + 128],
                    pooled[32 * c : 32 * c + 32],
                    jnp.concatenate(channels, axis=1),
                ],
                axis=0,
            )
        )
    kept = either(core, loads[0], loads[1]).astype(BF16)
    sent = either(core, loads[1], loads[0]).astype(BF16)
    return jnp.concatenate([pieces, more, blank], axis=0), kept, sent


def settle(part_0, part_1, part_2, part_3):
    total = sum_four([part_0, part_1, part_2, part_3]).astype(BF16)
    return (jnp.broadcast_to(total[None], (16, *total.shape)),)


def line_sum(arrived):
    total = arrived[0].astype(F32)
    for source in range(1, 16):
        total = total + arrived[source].astype(F32)
    line = unfold_rows(total)
    line = jnp.concatenate([line, jnp.zeros((64, 64), F32)], axis=1).astype(BF16)
    return tuple(line[16 * k : 16 * k + 16] for k in range(4))


def finish(pieces):
    wide = pieces.astype(F32)

    def join(start, count):
        return jnp.concatenate([wide[start + i] for i in range(count)], axis=1)

    qkv_grad = jnp.stack([join(0, 3), join(9, 3), join(12, 3)])
    return qkv_grad, join(3, 6)


def mix(kept, received):
    half = lax.axis_index("half")
    both = kept.astype(F32) + received.astype(F32)
    rows = [both[160:, :192], both[160:, 192:]]
    leaving = either(half, rows[1], rows[0])
    staying = either(half, rows[0], rows[1])
    folded = jnp.concatenate([leaving[:32], leaving[32:]], axis=1)
    return both[:160].astype(BF16), jnp.concatenate([both[:160], folded], axis=0).astype(BF16), staying


def back(both, taken, staying, skipped, held, ln_gain):
    core = lax.axis_index("core")
    total = both.astype(F32) + taken[:160].astype(F32)
    held = held.astype(F32)
    unit, inv_std = normalize(either(core, held[:128], held[128:]))
    scaled = total[:128] * ln_gain[None, :]
    grad = inv_std * (
        scaled
        - jnp.mean(scaled, axis=-1, keepdims=True)
        - unit * jnp.mean(scaled * unit, axis=-1, keepdims=True)
    )
    pooled = total[128:160] * 0.25
    grown = []
    for block in range(8):
        half = (block % 4) // 2
        grown.append(pooled[16 * half : 16 * half + 16])
    folded = taken[160:].astype(F32)
    arrived = jnp.concatenate([folded[:, :192], folded[:, 192:]], axis=0)
    block_out = (staying + arrived + skipped).astype(BF16)
    return (grad + jnp.concatenate(grown, axis=0)).astype(BF16), block_out


def unpermute(own_rows, other_rows):
    core = lax.axis_index("core")
    own_rows, other_rows = own_rows.astype(F32), other_rows.astype(F32)
    ordered = jnp.concatenate(
        [either(core, own_rows, other_rows), either(core, other_rows, own_rows)], axis=0
    ).astype(BF16)
    return (dot_nn(selector(256, token_of, True), ordered).astype(BF16),)


def local(
    tokens,
    ln_gain,
    qkv_weight,
    query_pool,
    key_pool,
    value_pool,
    proj_weight,
    skip_weight,
    cotangent,
):
    cot_far = swap(cotangent, "half")
    cot_near = swap(cotangent, "core")

    same_kv, other_kv, normed, held = fuse(
        front,
        [((16, 256), BF16)] * 2 + [((256, 384), BF16)] * 2,
        "front",
        direct=True,
    )(tokens, ln_gain, qkv_weight, key_pool, value_pool)
    line_kv = [same_kv, shift(other_kv, "z", 1), shift(same_kv, "z", 2), shift(other_kv, "z", 3)]
    line_kv, cot_far = lax.optimization_barrier((line_kv, cot_far))
    cot_both = swap(cot_far, "core")
    (copies_kv,) = fuse(copy_line, [((16, 32, 384), BF16)], "copy_line")(*line_kv)
    rows_kv = exchange(copies_kv, PLANE)

    mine, theirs, held_cotangent, skipped, d_pooled = fuse(
        middle,
        [
            ((64, 256), BF16),
            ((64, 256), BF16),
            ((64, 768), BF16),
            ((64, 192), F32),
            ((64, 384), BF16),
        ],
        "middle",
    )(
        normed,
        held,
        qkv_weight,
        query_pool,
        cotangent,
        cot_near,
        cot_far,
        cot_both,
        proj_weight,
        skip_weight,
    )
    rows_grad, mixed, returned = fuse(
        attend, [((16, 32, 384), BF16), ((64, 256), F32), ((64, 256), BF16)], "attend"
    )(rows_kv, mine, swap_pair(theirs))

    arrived = exchange(rows_grad, PLANE)
    line = fuse(line_sum, [((16, 256), BF16)] * 4, "line_sum")(arrived)
    parts = [line[0]] + [shift(line[k], "z", -k) for k in (1, 2, 3)]
    pieces, d_queries, head_part = fuse(
        after, [((9, 192, 128), BF16), ((256, 192), BF16), ((64, 768), BF16)], "after"
    )(mixed, swap_pair(returned), normed, query_pool, held_cotangent, proj_weight)

    pieces, kept, sent = fuse(
        weights,
        [((16, 192, 128), BF16), ((224, 384), BF16), ((224, 384), BF16)],
        "weights",
    )(
        *parts,
        normed,
        d_queries,
        key_pool,
        value_pool,
        qkv_weight,
        pieces,
        d_pooled,
        head_part,
    )

    both, sent, staying = fuse(
        mix, [((160, 384), BF16), ((192, 384), BF16), ((64, 192), F32)], "mix"
    )(kept, swap(sent, "core"))
    taken = swap(sent, "half")

    reduced = jnp.sum(exchange(pieces, PLANE).astype(F32), axis=0).astype(BF16)
    reduced, both = lax.optimization_barrier((reduced, both))
    (copies,) = fuse(settle, [((16, 192, 128), BF16)], "settle")(
        reduced, *[shift(reduced, "z", k) for k in (1, 2, 3)]
    )
    qkv_grad, proj_grad = fuse(finish, [((3, 192, 384), F32), ((192, 768), F32)], "finish")(
        exchange(copies, PLANE)
    )

    own_rows, block_out = fuse(back, [((128, 384), BF16), ((64, 192), BF16)], "back", flops=8 * 10**9)(
        both, taken, staying, skipped, held, ln_gain
    )
    (input_grad,) = fuse(unpermute, [((256, 384), BF16)], "unpermute")(
        own_rows, swap(own_rows, "core")
    )
    return (block_out, input_grad, qkv_grad, proj_grad)


def solution(mesh):
    grid = Mesh(
        np.asarray(mesh.devices).reshape(4, 4, 4, 2, 2), ("y", "z", "x", "half", "core")
    )
    placed = (
        P(TILE, None),
        P(),
        P(None, HEAD, None),
        P(None, HEAD),
        P(None, HEAD),
        P(None, HEAD),
        P(HEAD, None),
        P(HEAD, None),
        P(TILE, HEAD),
    )
    return jax.shard_map(
        local,
        mesh=grid,
        in_specs=placed,
        out_specs=(P(TILE, HEAD), P(TILE, None), P(None, HEAD, None), P(HEAD, None)),
        check_vma=False,
    )
```

time: 110 us -> 103 us (0.936)
  waiting for transfers between devices: 28.4 us -> 48.1 us
  blocking collectives: 18.5 us -> 0 us
  local copies, waits for them, and re-layouts: 9.34 us -> 1.4 us
  Pallas kernels: 7.02 us -> 12.2 us
  starting transfers between devices: 42.8 us -> 38.8 us
    all_to_all x1 -> x0, blocking collectives: 18.5 us -> none  [exchange_plane(): return lax.all_to_all(blocks, PLANE, 0, 0, tiled=True)]
    all_to_all x3 -> x4, waiting for transfers between devices: 8.12 us -> 25.3 us  [exchange(): return lax.all_to_all(blocks, axes, 0, 0, tiled=True)]
    ppermute x9, starting transfers between devices: 13.7 us -> 7.96 us  [shift(): return lax.ppermute(block, axis, [(i, (i + step) % 4) for i in range(4)])]
    ppermute x5 -> x6, waiting for transfers between devices: 9.2 us -> 3.56 us  [swap(): return lax.ppermute(block, axis, [(0, 1), (1, 0)])]
    all_to_all x3 -> x4, starting transfers between devices: 17.3 us -> 22.7 us  [exchange(): return lax.all_to_all(blocks, axes, 0, 0, tiled=True)]
    pallas_call x8 -> x12, Pallas kernels: 7.02 us -> 12.2 us  [call(): pl.pallas_call(kernel, out_shape=[jax.ShapeDtypeStruct(shape, dtype) for...]
    ppermute x9, waiting for transfers between devices: 11.1 us -> 15.3 us  [shift(): return lax.ppermute(block, axis, [(i, (i + step) % 4) for i in range(4)])]
    ppermute x0 -> x2, waiting for transfers between devices: none -> 3.9 us  [swap_pair(): return lax.ppermute(block, 'z', [(i, i ^ 1) for i in range(4)])]
  transfers between devices with their start and end apart: 17 -> 21, of which waited for: 14 -> 18; matrix products, arithmetic and copies ran while one was open for 3% -> 0% of each run, Pallas kernels for 2% -> 7%
where the time goes in v2:
time: 103 us; the launch traced here: 101 us
  waiting for transfers between devices  48.1 us (47%)
  starting transfers between devices  38.8 us (38%)
  Pallas kernels  12.2 us (12%)
  local copies, waits for them, and re-layouts  1.4 us (1%)
    all_to_all x4, waiting for transfers between devices, exchange(): return lax.all_to_all(blocks, axes, 0, 0, tiled=True)  25.3 us
    all_to_all x4, starting transfers between devices, exchange(): return lax.all_to_all(blocks, axes, 0, 0, tiled=True)  22.7 us
    ppermute x9, waiting for transfers between devices, shift(): return lax.ppermute(block, axis, [(i, (i + step) % 4) for i in range(4)])  15.3 us
    pallas_call x12, Pallas kernels, call(): pl.pallas_call(kernel, out_shape=[jax.ShapeDtypeStruct(shape, dtype) for...  12.2 us
    ppermute x6, starting transfers between devices, swap(): return lax.ppermute(block, axis, [(0, 1), (1, 0)])  7.99 us
    ppermute x9, starting transfers between devices, shift(): return lax.ppermute(block, axis, [(i, (i + step) % 4) for i in range(4)])  7.96 us
    ppermute x2, waiting for transfers between devices, swap_pair(): return lax.ppermute(block, 'z', [(i, i ^ 1) for i in range(4)])  3.9 us
    ppermute x6, waiting for transfers between devices, swap(): return lax.ppermute(block, axis, [(0, 1), (1, 0)])  3.56 us
  transfers between devices with their start and end apart: 21, of which 18 were waited for; matrix products, arithmetic and copies ran while one was open for 0% of the time, Pallas kernels for 7%

profile of v2, /device:TPU:2, one launch (start us, length us, event | category | flops | bytes accessed | tf_op | source)
XLA Modules:
  0.0 101.3 jit_solution(16304791665572425978)
XLA Ops:
  0.6 7.3 %collective-permute-start.3 = (bf16[64,192]{1,0:T(8,128)(2,1)}, bf16[64,192]{1,0:T(8,128)(2,1)S(1)}, u32[]{:S(2)}, u32[]{:S(2)}) collective-permute-start(bf16[64,192]{1,0:T(8,128)(2,1)} %refs_4_.3), channel_id=1, source_target_pairs={{0,2},{2,0},{1,3},{3,1},{4,6},{6,4},{5,7},{7,5},{8,10},{10,8},{9,1... | collective-permute-start | bytes 73736 | tf_op jit(solution)/shard_map/ppermute | solution.py:25
  7.9 2.6 %front.1 = (bf16[16,256]{1,0:T(8,128)(2,1)}, bf16[16,256]{1,0:T(8,128)(2,1)}, bf16[256,384]{1,0:T(8,128)(2,1)}, bf16[256,384]{1,0:T(8,128)(2,1)}) custom-call(bf16[256,384]{1,0:T(8,128)(2,1)} %refs_0_.1, f32[384]{0:T(512)} %refs_5_.3, bf16[3,192,384]{2,1,0:T(8,128)(2,1)} %refs_8_.3, bf16[16,192]{1,0:T(8,128)(2,1)} %refs_6_.1, bf16[16,192]{1,0:T(8,128)(2,1)} %refs_7_.1), custom_call_target="tpu_custom_call" | custom-call | tf_op jit(solution)/shard_map/front/pallas_call | solution.py:66
  10.5 1.6 %collective-permute-start.1 = (bf16[16,256]{1,0:T(8,128)(2,1)}, bf16[16,256]{1,0:T(8,128)(2,1)S(1)}, u32[]{:S(2)}, u32[]{:S(2)}) collective-permute-start(bf16[16,256]{1,0:T(8,128)(2,1)} %get-tuple-element.42.refs_0_), channel_id=1, source_target_pairs={{0,32},{16,48},{32,0},{48,16},{1,33},{17,49},{33,1},{49,17},{2,34}... | collective-permute-start | bytes 24584 | tf_op jit(solution)/shard_map/ppermute | solution.py:21
  12.1 1.9 %collective-permute-start.2 = (bf16[16,256]{1,0:T(8,128)(2,1)}, bf16[16,256]{1,0:T(8,128)(2,1)S(1)}, u32[]{:S(2)}, u32[]{:S(2)}) collective-permute-start(bf16[16,256]{1,0:T(8,128)(2,1)} %get-tuple-element.41), channel_id=1, source_target_pairs={{0,48},{16,0},{32,16},{48,32},{1,49},{17,1},{33,17},{49,33},{2,50}... | collective-permute-start | bytes 24584 | tf_op jit(solution)/shard_map/ppermute | solution.py:21
  16.0 3.7 %collective-permute-done.refs_1_ = bf16[16,256]{1,0:T(8,128)(2,1)S(1)} collective-permute-done((bf16[16,256]{1,0:T(8,128)(2,1)}, bf16[16,256]{1,0:T(8,128)(2,1)S(1)}, u32[]{:S(2)}, u32[]{:S(2)}) %collective-permute-start) | collective-permute-done | bytes 8224 | tf_op jit(solution)/shard_map/ppermute | solution.py:21
  21.2 7.6 %all-to-all-start = ((bf16[16,32,384]{2,1,0:T(8,128)(2,1)}), bf16[16,32,384]{2,1,0:T(8,128)(2,1)S(1)}, u32[]{:S(2)}, u32[]{:S(2)}) async-start(bf16[16,32,384]{2,1,0:T(8,128)(2,1)} %copy_line.1), calls=%async_computation | async-start | bytes 786432 | tf_op jit(solution)/shard_map/all_to_all | solution.py:33
  31.1 3.9 %collective-permute-done.6.refs_2_ = bf16[64,256]{1,0:T(8,128)(2,1)S(1)} collective-permute-done((bf16[64,256]{1,0:T(8,128)(2,1)S(1)}, bf16[64,256]{1,0:T(8,128)(2,1)S(1)}, u32[]{:S(2)}, u32[]{:S(2)}) %collective-permute-start.6) | collective-permute-done | bytes 32800 | tf_op jit(solution)/shard_map/ppermute | solution.py:29
  35.0 1.9 %all-to-all-done.refs_0_ = bf16[16,32,384]{2,1,0:T(8,128)(2,1)S(1)} async-done(((bf16[16,32,384]{2,1,0:T(8,128)(2,1)}), bf16[16,32,384]{2,1,0:T(8,128)(2,1)S(1)}, u32[]{:S(2)}, u32[]{:S(2)}) %all-to-all-start) | async-done | bytes 393248 | tf_op jit(solution)/shard_map/all_to_all | solution.py:33
  36.9 1.8 %attend.1 = (bf16[16,32,384]{2,1,0:T(8,128)(2,1)}, f32[64,256]{1,0:T(8,128)S(1)}, bf16[64,256]{1,0:T(8,128)(2,1)S(1)}) custom-call(bf16[16,32,384]{2,1,0:T(8,128)(2,1)S(1)} %all-to-all-done.refs_0_, bf16[64,256]{1,0:T(8,128)(2,1)S(1)} %get-tuple-element.49.refs_1_, bf16[64,256]{1,0:T(8,128)(2,1)S(1)} %collective-permute-done.6.refs_2_), custom_call_target="tpu_custom_call" | custom-call | tf_op jit(solution)/shard_map/attend/pallas_call | solution.py:66
  38.7 5.4 %all-to-all-start.1 = ((bf16[16,32,384]{2,1,0:T(8,128)(2,1)}), bf16[16,32,384]{2,1,0:T(8,128)(2,1)S(1)}, u32[]{:S(2)}, u32[]{:S(2)}) async-start(bf16[16,32,384]{2,1,0:T(8,128)(2,1)} %get-tuple-element.51), calls=%async_computation.1 | async-start | bytes 786432 | tf_op jit(solution)/shard_map/all_to_all | solution.py:33
  44.1 8.1 %all-to-all-done.1.refs_0_ = bf16[16,32,384]{2,1,0:T(8,128)(2,1)S(1)} async-done(((bf16[16,32,384]{2,1,0:T(8,128)(2,1)}), bf16[16,32,384]{2,1,0:T(8,128)(2,1)S(1)}, u32[]{:S(2)}, u32[]{:S(2)}) %all-to-all-start.1) | async-done | bytes 393248 | tf_op jit(solution)/shard_map/all_to_all | solution.py:33
  52.4 2.0 %collective-permute-start.8 = (bf16[16,256]{1,0:T(8,128)(2,1)S(1)}, bf16[16,256]{1,0:T(8,128)(2,1)S(1)}, u32[]{:S(2)}, u32[]{:S(2)}) collective-permute-start(bf16[16,256]{1,0:T(8,128)(2,1)S(1)} %get-tuple-element.54), channel_id=1, source_target_pairs={{0,32},{16,48},{32,0},{48,16},{1,33},{17,49},{33,1},{49,17},{2,34}... | collective-permute-start | bytes 24584 | tf_op jit(solution)/shard_map/ppermute | solution.py:21
  57.0 2.8 %collective-permute-done.9.refs_3_ = bf16[16,256]{1,0:T(8,128)(2,1)S(1)} collective-permute-done((bf16[16,256]{1,0:T(8,128)(2,1)S(1)}, bf16[16,256]{1,0:T(8,128)(2,1)S(1)}, u32[]{:S(2)}, u32[]{:S(2)}) %collective-permute-start.9) | collective-permute-done | bytes 8224 | tf_op jit(solution)/shard_map/ppermute | solution.py:21
  59.8 1.5 %weights.1 = (bf16[16,192,128]{2,1,0:T(8,128)(2,1)}, bf16[224,384]{1,0:T(8,128)(2,1)S(1)}, bf16[224,384]{1,0:T(8,128)(2,1)S(1)}) custom-call(bf16[16,256]{1,0:T(8,128)(2,1)S(1)} %get-tuple-element.52.refs_0_, bf16[16,256]{1,0:T(8,128)(2,1)S(1)} %collective-permute-done.7.refs_1_, bf16[16,256]{1,0:T(8,128)(2,1)S(1)} %collective-permute-done.8.refs_2_, ...), custom_call_target="tpu_custom_call" | custom-call | tf_op jit(solution)/shard_map/weights/pallas_call | solution.py:66
  61.3 4.9 %all-to-all-start.2 = ((bf16[16,192,128]{2,1,0:T(8,128)(2,1)}), bf16[16,192,128]{2,1,0:T(8,128)(2,1)S(1)}, u32[]{:S(2)}, u32[]{:S(2)}) async-start(bf16[16,192,128]{2,1,0:T(8,128)(2,1)} %get-tuple-element.63), calls=%async_computation.2 | async-start | bytes 1572864 | tf_op jit(solution)/shard_map/all_to_all | solution.py:33
  66.2 1.4 %collective-permute-done.11.refs_1_ = bf16[224,384]{1,0:T(8,128)(2,1)S(1)} collective-permute-done((bf16[224,384]{1,0:T(8,128)(2,1)S(1)}, bf16[224,384]{1,0:T(8,128)(2,1)S(1)}, u32[]{:S(2)}, u32[]{:S(2)}) %collective-permute-start.11) | collective-permute-done | bytes 172064 | tf_op jit(solution)/shard_map/ppermute | solution.py:25
  67.9 8.8 %all-to-all-done.2 = bf16[16,192,128]{2,1,0:T(8,128)(2,1)S(1)} async-done(((bf16[16,192,128]{2,1,0:T(8,128)(2,1)}), bf16[16,192,128]{2,1,0:T(8,128)(2,1)S(1)}, u32[]{:S(2)}, u32[]{:S(2)}) %all-to-all-start.2) | async-done | bytes 786464 | tf_op jit(solution)/shard_map/all_to_all | solution.py:33
  77.6 1.5 %collective-permute-start.14 = (bf16[192,128]{1,0:T(8,128)(2,1)S(1)}, bf16[192,128]{1,0:T(8,128)(2,1)S(1)}, u32[]{:S(2)}, u32[]{:S(2)}) collective-permute-start(bf16[192,128]{1,0:T(8,128)(2,1)S(1)} %reduce_sum.12.refs_0_), channel_id=1, source_target_pairs={{0,16},{16,32},{32,48},{48,0},{1,17},{17,33},{33,49},{49,1},{2,18}... | collective-permute-start | bytes 147464 | tf_op jit(solution)/shard_map/ppermute | solution.py:21
  79.1 2.1 %collective-permute-done.16.refs_3_ = bf16[192,128]{1,0:T(8,128)(2,1)S(1)} collective-permute-done((bf16[192,128]{1,0:T(8,128)(2,1)S(1)}, bf16[192,128]{1,0:T(8,128)(2,1)S(1)}, u32[]{:S(2)}, u32[]{:S(2)}) %collective-permute-start.16) | collective-permute-done | bytes 49184 | tf_op jit(solution)/shard_map/ppermute | solution.py:21
  81.1 1.4 %collective-permute-done.15.refs_2_ = bf16[192,128]{1,0:T(8,128)(2,1)S(1)} collective-permute-done((bf16[192,128]{1,0:T(8,128)(2,1)S(1)}, bf16[192,128]{1,0:T(8,128)(2,1)S(1)}, u32[]{:S(2)}, u32[]{:S(2)}) %collective-permute-start.15) | collective-permute-done | bytes 49184 | tf_op jit(solution)/shard_map/ppermute | solution.py:21
  82.6 1.5 %collective-permute-done.14.refs_1_ = bf16[192,128]{1,0:T(8,128)(2,1)S(1)} collective-permute-done((bf16[192,128]{1,0:T(8,128)(2,1)S(1)}, bf16[192,128]{1,0:T(8,128)(2,1)S(1)}, u32[]{:S(2)}, u32[]{:S(2)}) %collective-permute-start.14) | collective-permute-done | bytes 49184 | tf_op jit(solution)/shard_map/ppermute | solution.py:21
  85.0 4.9 %all-to-all-start.3 = ((bf16[16,192,128]{2,1,0:T(8,128)(2,1)}), bf16[16,192,128]{2,1,0:T(8,128)(2,1)S(1)}, u32[]{:S(2)}, u32[]{:S(2)}) async-start(bf16[16,192,128]{2,1,0:T(8,128)(2,1)} %settle.1), calls=%async_computation.3 | async-start | bytes 1572864 | tf_op jit(solution)/shard_map/all_to_all | solution.py:33
  91.5 1.3 %collective-permute-done.13.refs_1_ = bf16[128,384]{1,0:T(8,128)(2,1)S(1)} collective-permute-done((bf16[128,384]{1,0:T(8,128)(2,1)S(1)}, bf16[128,384]{1,0:T(8,128)(2,1)S(1)}, u32[]{:S(2)}, u32[]{:S(2)}) %collective-permute-start.13) | collective-permute-done | bytes 98336 | tf_op jit(solution)/shard_map/ppermute | solution.py:25
  93.7 6.5 %all-to-all-done.3.refs_0_ = bf16[16,192,128]{2,1,0:T(8,128)(2,1)S(1)} async-done(((bf16[16,192,128]{2,1,0:T(8,128)(2,1)}), bf16[16,192,128]{2,1,0:T(8,128)(2,1)S(1)}, u32[]{:S(2)}, u32[]{:S(2)}) %all-to-all-start.3) | async-done | bytes 786464 | tf_op jit(solution)/shard_map/all_to_all | solution.py:33
  (53 shorter events, 14.4 us)
Async XLA Ops:
  0.6 19.0 %collective-permute-start.3 = (bf16[64,192]{1,0:T(8,128)(2,1)}, bf16[64,192]{1,0:T(8,128)(2,1)S(1)}, u32[]{:S(2)}, u32[]{:S(2)}) collective-permute-start(bf16[64,192]{1,0:T(8,128)(2,1)} %refs_4_.3), channel_id=1, source_target_pairs={{0,2},{2,0},{1,3},{3,1},{4,6},{6,4},{5,7},{7,5},{8,10},{10,8},{9,1... | collective-permute-start | bytes 73736 | tf_op jit(solution)/shard_map/ppermute | solution.py:25
  7.9 22.4 %copy-start.4 = (bf16[192,384]{1,0:T(8,128)(2,1)S(1)}, bf16[192,384]{1,0:T(8,128)(2,1)}, u32[]{:S(2)}) copy-start(bf16[192,384]{1,0:T(8,128)(2,1)} %refs_9_.1) | copy-start | bytes 442372
  10.5 4.8 %collective-permute-start.1 = (bf16[16,256]{1,0:T(8,128)(2,1)}, bf16[16,256]{1,0:T(8,128)(2,1)S(1)}, u32[]{:S(2)}, u32[]{:S(2)}) collective-permute-start(bf16[16,256]{1,0:T(8,128)(2,1)} %get-tuple-element.42.refs_0_), channel_id=1, source_target_pairs={{0,32},{16,48},{32,0},{48,16},{1,33},{17,49},{33,1},{49,17},{2,34}... | collective-permute-start | bytes 24584 | tf_op jit(solution)/shard_map/ppermute | solution.py:21
  12.1 3.9 %collective-permute-start.2 = (bf16[16,256]{1,0:T(8,128)(2,1)}, bf16[16,256]{1,0:T(8,128)(2,1)S(1)}, u32[]{:S(2)}, u32[]{:S(2)}) collective-permute-start(bf16[16,256]{1,0:T(8,128)(2,1)} %get-tuple-element.41), channel_id=1, source_target_pairs={{0,48},{16,0},{32,16},{48,32},{1,49},{17,1},{33,17},{49,33},{2,50}... | collective-permute-start | bytes 24584 | tf_op jit(solution)/shard_map/ppermute | solution.py:21
  14.0 5.7 %collective-permute-start = (bf16[16,256]{1,0:T(8,128)(2,1)}, bf16[16,256]{1,0:T(8,128)(2,1)S(1)}, u32[]{:S(2)}, u32[]{:S(2)}) collective-permute-start(bf16[16,256]{1,0:T(8,128)(2,1)} %get-tuple-element.41), channel_id=1, source_target_pairs={{0,16},{16,32},{32,48},{48,0},{1,17},{17,33},{33,49},{49,1},{2,18}... | collective-permute-start | bytes 24584 | tf_op jit(solution)/shard_map/ppermute | solution.py:21
  20.4 10.0 %copy-start.2 = (bf16[192,768]{1,0:T(8,128)(2,1)S(1)}, bf16[192,768]{1,0:T(8,128)(2,1)}, u32[]{:S(2)}) copy-start(bf16[192,768]{1,0:T(8,128)(2,1)} %refs_5_.2) | copy-start | bytes 884740
  20.4 10.0 %copy-start.3 = (bf16[256,384]{1,0:T(8,128)(2,1)S(1)}, bf16[256,384]{1,0:T(8,128)(2,1)}, u32[]{:S(2)}) copy-start(bf16[256,384]{1,0:T(8,128)(2,1)} %get-tuple-element.47.refs_1_.refs_4_) | copy-start | bytes 589828
  21.2 15.6 %all-to-all-start = ((bf16[16,32,384]{2,1,0:T(8,128)(2,1)}), bf16[16,32,384]{2,1,0:T(8,128)(2,1)S(1)}, u32[]{:S(2)}, u32[]{:S(2)}) async-start(bf16[16,32,384]{2,1,0:T(8,128)(2,1)} %copy_line.1), calls=%async_computation | async-start | bytes 786432 | tf_op jit(solution)/shard_map/all_to_all | solution.py:33
  28.9 1.3 %collective-permute-start.4 = (bf16[64,192]{1,0:T(8,128)(2,1)S(1)}, bf16[64,192]{1,0:T(8,128)(2,1)S(1)}, u32[]{:S(2)}, u32[]{:S(2)}) collective-permute-start(bf16[64,192]{1,0:T(8,128)(2,1)S(1)} %copy-done.7), channel_id=1, source_target_pairs={{0,1},{1,0},{2,3},{3,2},{4,5},{5,4},{6,7},{7,6},{8,9},{9,8},{10,11... | collective-permute-start | bytes 73736 | tf_op jit(solution)/shard_map/ppermute | solution.py:25
  29.0 1.4 %collective-permute-start.5 = (bf16[64,192]{1,0:T(8,128)(2,1)S(1)}, bf16[64,192]{1,0:T(8,128)(2,1)S(1)}, u32[]{:S(2)}, u32[]{:S(2)}) collective-permute-start(bf16[64,192]{1,0:T(8,128)(2,1)S(1)} %collective-permute-done.3.refs_6_), channel_id=1, source_target_pairs={{0,1},{1,0},{2,3},{3,2},{4,5},{5,4},{6,7},{7,6},{8,9},{9,8},{10,11... | collective-permute-start | bytes 73736 | tf_op jit(solution)/shard_map/ppermute | solution.py:25
  31.0 4.0 %collective-permute-start.6 = (bf16[64,256]{1,0:T(8,128)(2,1)S(1)}, bf16[64,256]{1,0:T(8,128)(2,1)S(1)}, u32[]{:S(2)}, u32[]{:S(2)}) collective-permute-start(bf16[64,256]{1,0:T(8,128)(2,1)S(1)} %get-tuple-element.50), channel_id=1, source_target_pairs={{0,16},{16,0},{32,48},{48,32},{1,17},{17,1},{33,49},{49,33},{2,18}... | collective-permute-start | bytes 98312 | tf_op jit(solution)/shard_map/ppermute | solution.py:29
  38.7 13.5 %all-to-all-start.1 = ((bf16[16,32,384]{2,1,0:T(8,128)(2,1)}), bf16[16,32,384]{2,1,0:T(8,128)(2,1)S(1)}, u32[]{:S(2)}, u32[]{:S(2)}) async-start(bf16[16,32,384]{2,1,0:T(8,128)(2,1)} %get-tuple-element.51), calls=%async_computation.1 | async-start | bytes 786432 | tf_op jit(solution)/shard_map/all_to_all | solution.py:33
  44.0 10.3 %collective-permute-start.10 = (bf16[64,256]{1,0:T(8,128)(2,1)S(1)}, bf16[64,256]{1,0:T(8,128)(2,1)S(1)}, u32[]{:S(2)}, u32[]{:S(2)}) collective-permute-start(bf16[64,256]{1,0:T(8,128)(2,1)S(1)} %get-tuple-element.57), channel_id=1, source_target_pairs={{0,16},{16,0},{32,48},{48,32},{1,17},{17,1},{33,49},{49,33},{2,18}... | collective-permute-start | bytes 98312 | tf_op jit(solution)/shard_map/ppermute | solution.py:29
  52.3 3.7 %collective-permute-start.7 = (bf16[16,256]{1,0:T(8,128)(2,1)S(1)}, bf16[16,256]{1,0:T(8,128)(2,1)S(1)}, u32[]{:S(2)}, u32[]{:S(2)}) collective-permute-start(bf16[16,256]{1,0:T(8,128)(2,1)S(1)} %get-tuple-element.53), channel_id=1, source_target_pairs={{0,48},{16,0},{32,16},{48,32},{1,49},{17,1},{33,17},{49,33},{2,50}... | collective-permute-start | bytes 24584 | tf_op jit(solution)/shard_map/ppermute | solution.py:21
  52.4 4.7 %collective-permute-start.8 = (bf16[16,256]{1,0:T(8,128)(2,1)S(1)}, bf16[16,256]{1,0:T(8,128)(2,1)S(1)}, u32[]{:S(2)}, u32[]{:S(2)}) collective-permute-start(bf16[16,256]{1,0:T(8,128)(2,1)S(1)} %get-tuple-element.54), channel_id=1, source_target_pairs={{0,32},{16,48},{32,0},{48,16},{1,33},{17,49},{33,1},{49,17},{2,34}... | collective-permute-start | bytes 24584 | tf_op jit(solution)/shard_map/ppermute | solution.py:21
  54.4 5.4 %collective-permute-start.9 = (bf16[16,256]{1,0:T(8,128)(2,1)S(1)}, bf16[16,256]{1,0:T(8,128)(2,1)S(1)}, u32[]{:S(2)}, u32[]{:S(2)}) collective-permute-start(bf16[16,256]{1,0:T(8,128)(2,1)S(1)} %get-tuple-element.55), channel_id=1, source_target_pairs={{0,16},{16,32},{32,48},{48,0},{1,17},{17,33},{33,49},{49,1},{2,18}... | collective-permute-start | bytes 24584 | tf_op jit(solution)/shard_map/ppermute | solution.py:21
  61.3 15.4 %all-to-all-start.2 = ((bf16[16,192,128]{2,1,0:T(8,128)(2,1)}), bf16[16,192,128]{2,1,0:T(8,128)(2,1)S(1)}, u32[]{:S(2)}, u32[]{:S(2)}) async-start(bf16[16,192,128]{2,1,0:T(8,128)(2,1)} %get-tuple-element.63), calls=%async_computation.2 | async-start | bytes 1572864 | tf_op jit(solution)/shard_map/all_to_all | solution.py:33
  66.2 1.4 %collective-permute-start.11 = (bf16[224,384]{1,0:T(8,128)(2,1)S(1)}, bf16[224,384]{1,0:T(8,128)(2,1)S(1)}, u32[]{:S(2)}, u32[]{:S(2)}) collective-permute-start(bf16[224,384]{1,0:T(8,128)(2,1)S(1)} %get-tuple-element.65), channel_id=1, source_target_pairs={{0,1},{1,0},{2,3},{3,2},{4,5},{5,4},{6,7},{7,6},{8,9},{9,8},{10,11... | collective-permute-start | bytes 516104 | tf_op jit(solution)/shard_map/ppermute | solution.py:25
  67.7 22.1 %collective-permute-start.12 = (bf16[192,384]{1,0:T(8,128)(2,1)S(1)}, bf16[192,384]{1,0:T(8,128)(2,1)S(1)}, u32[]{:S(2)}, u32[]{:S(2)}) collective-permute-start(bf16[192,384]{1,0:T(8,128)(2,1)S(1)} %get-tuple-element.68), channel_id=1, source_target_pairs={{0,2},{2,0},{1,3},{3,1},{4,6},{6,4},{5,7},{7,5},{8,10},{10,8},{9,1... | collective-permute-start | bytes 442376 | tf_op jit(solution)/shard_map/ppermute | solution.py:25
  76.8 4.3 %collective-permute-start.16 = (bf16[192,128]{1,0:T(8,128)(2,1)S(1)}, bf16[192,128]{1,0:T(8,128)(2,1)S(1)}, u32[]{:S(2)}, u32[]{:S(2)}) collective-permute-start(bf16[192,128]{1,0:T(8,128)(2,1)S(1)} %reduce_sum.12.refs_0_), channel_id=1, source_target_pairs={{0,48},{16,0},{32,16},{48,32},{1,49},{17,1},{33,17},{49,33},{2,50}... | collective-permute-start | bytes 147464 | tf_op jit(solution)/shard_map/ppermute | solution.py:21
  77.6 5.0 %collective-permute-start.15 = (bf16[192,128]{1,0:T(8,128)(2,1)S(1)}, bf16[192,128]{1,0:T(8,128)(2,1)S(1)}, u32[]{:S(2)}, u32[]{:S(2)}) collective-permute-start(bf16[192,128]{1,0:T(8,128)(2,1)S(1)} %reduce_sum.12.refs_0_), channel_id=1, source_target_pairs={{0,32},{16,48},{32,0},{48,16},{1,33},{17,49},{33,1},{49,17},{2,34}... | collective-permute-start | bytes 147464 | tf_op jit(solution)/shard_map/ppermute | solution.py:21
  77.6 6.4 %collective-permute-start.14 = (bf16[192,128]{1,0:T(8,128)(2,1)S(1)}, bf16[192,128]{1,0:T(8,128)(2,1)S(1)}, u32[]{:S(2)}, u32[]{:S(2)}) collective-permute-start(bf16[192,128]{1,0:T(8,128)(2,1)S(1)} %reduce_sum.12.refs_0_), channel_id=1, source_target_pairs={{0,16},{16,32},{32,48},{48,0},{1,17},{17,33},{33,49},{49,1},{2,18}... | collective-permute-start | bytes 147464 | tf_op jit(solution)/shard_map/ppermute | solution.py:21
  85.0 15.2 %all-to-all-start.3 = ((bf16[16,192,128]{2,1,0:T(8,128)(2,1)}), bf16[16,192,128]{2,1,0:T(8,128)(2,1)S(1)}, u32[]{:S(2)}, u32[]{:S(2)}) async-start(bf16[16,192,128]{2,1,0:T(8,128)(2,1)} %settle.1), calls=%async_computation.3 | async-start | bytes 1572864 | tf_op jit(solution)/shard_map/all_to_all | solution.py:33
  91.5 1.3 %collective-permute-start.13 = (bf16[128,384]{1,0:T(8,128)(2,1)S(1)}, bf16[128,384]{1,0:T(8,128)(2,1)S(1)}, u32[]{:S(2)}, u32[]{:S(2)}) collective-permute-start(bf16[128,384]{1,0:T(8,128)(2,1)S(1)} %get-tuple-element.72.refs_0_), channel_id=1, source_target_pairs={{0,1},{1,0},{2,3},{3,2},{4,5},{5,4},{6,7},{7,6},{8,9},{9,8},{10,11... | collective-permute-start | bytes 294920 | tf_op jit(solution)/shard_map/ppermute | solution.py:25
  (8 other events, 39.0 us)

commit v3 on v2

--- a/solution.py
+++ b/solution.py
@@ -25,8 +25,16 @@
     return lax.ppermute(block, axis, [(0, 1), (1, 0)])
 
 
-def swap_pair(block):
-    return lax.ppermute(block, "z", [(i, i ^ 1) for i in range(4)])
+def swap_z(block, bit):
+    return lax.ppermute(block, "z", [(i, i ^ bit) for i in range(4)])
+
+
+def exchange_pairs(blocks):
+    groups = [
+        [16 * y + 4 * z + x for y in range(4) for z in (first, first + 1) for x in range(4)]
+        for first in (0, 2)
+    ]
+    return lax.all_to_all(blocks, TILE, 0, 0, tiled=True, axis_index_groups=groups)
 
 
 def exchange(blocks, axes):
@@ -177,15 +185,13 @@
     normed = (unit * ln_gain[None, :]).astype(BF16)
     key_pooled = pool_keys(dot_nt(normed, weight_kv[1]), key_pool)
     value_pooled = pool_keys(dot_nt(normed, weight_kv[2]), value_pool)
-    odd = lax.rem(lax.axis_index("z"), 2)
     blank = jnp.zeros((16, 64), F32)
     rows = [
         jnp.concatenate([key_pooled[:, part], value_pooled[:, part], blank], axis=1)
         for part in (slice(0, HEAD_DIM), slice(HEAD_DIM, 2 * HEAD_DIM))
     ]
-    same = either(odd, rows[0], rows[1]).astype(BF16)
-    other = either(odd, rows[1], rows[0]).astype(BF16)
-    return same, other, normed, held.astype(BF16)
+    rows = jnp.concatenate(rows, axis=0).astype(BF16)
+    return rows, rows, normed, held.astype(BF16)
 
 
 def fold_rows(rows_in):
@@ -197,10 +203,14 @@
     return jnp.concatenate([rows_in[:, :192], rows_in[:, 192:]], axis=0)
 
 
-def copy_line(part_0, part_1, part_2, part_3):
-    line = jnp.concatenate([part_0, part_1, part_2, part_3], axis=0)
-    line = fold_rows(line.astype(F32)).astype(BF16)
-    return (jnp.broadcast_to(line[None], (16, 32, 384)),)
+def copy_pair(own, other):
+    wide, other = own.astype(F32), other.astype(F32)
+    heads = [
+        fold_rows(jnp.concatenate([wide[start : start + 16], other[start : start + 16]], axis=0))
+        for start in (0, 16)
+    ]
+    heads = jnp.concatenate([jnp.broadcast_to(h[None, None], (1, 4, 16, 384)) for h in heads])
+    return (jnp.broadcast_to(heads[None], (4, 2, 4, 16, 384)).astype(BF16).reshape(32, 16, 384),)
 
 
 def middle(
@@ -254,7 +264,7 @@
     row_delta = jnp.sum(probs_wide * dprobs, axis=-1, keepdims=True)
     d_scores = (scale * probs_wide * (dprobs - row_delta)).astype(BF16)
     both = jnp.concatenate([d_scores, attn_probs], axis=0)
-    rows_grad = fold_rows(dot_tn(both, packed)).astype(BF16).reshape(16, 32, 384)
+    rows_grad = fold_rows(dot_tn(both, packed)).astype(BF16).reshape(32, 16, 384)
     mixed = dot_nn(both, rows_kv)
     mixed = jnp.where(on_keys, mixed[:128], mixed[128:])
     mixed = mixed + jnp.concatenate([wide[:, HEAD_DIM:], wide[:, :HEAD_DIM]], axis=1)
@@ -281,30 +291,26 @@
     return jnp.stack(pieces).astype(BF16), d_queries, head_part
 
 
-def weights(
-    part_0,
-    part_1,
-    part_2,
-    part_3,
-    normed,
-    d_queries,
-    key_pool,
-    value_pool,
-    qkv_weight,
-    pieces,
-    d_pooled,
-    head_part,
-):
-    core, odd = lax.axis_index("core"), lax.rem(lax.axis_index("z"), 2)
-    same = part_0.astype(F32) + part_2.astype(F32)
-    other = part_1.astype(F32) + part_3.astype(F32)
-    per_head = [either(odd, same, other), either(odd, other, same)]
+def tile_grads(own, other, key_pool, value_pool):
+    total = own.astype(F32) + other.astype(F32)
+    per_head = [total[:16], total[16:]]
     key_grad = jnp.concatenate([t[:, :HEAD_DIM] for t in per_head], axis=1)
     value_grad = jnp.concatenate([t[:, HEAD_DIM : 2 * HEAD_DIM] for t in per_head], axis=1)
     d_keys = spread_keys(key_grad, key_pool).astype(BF16)
     d_values = spread_keys(value_grad, value_pool).astype(BF16)
+    return d_keys, d_values
+
+
+def weights(own, other, normed, key_pool, value_pool, pieces):
+    d_keys, d_values = tile_grads(own, other, key_pool, value_pool)
     more = jnp.stack(cut(dot_tn(d_keys, normed)) + cut(dot_tn(d_values, normed))).astype(BF16)
     blank = jnp.zeros((1, 192, 128), BF16)
+    pieces = jnp.concatenate([pieces, more, blank], axis=0).reshape(32, 96, 128)
+    return pieces, d_keys, d_values
+
+
+def spread(d_keys, d_values, d_queries, qkv_weight, d_pooled, head_part):
+    core = lax.axis_index("core")
     d_normed = dot_nn(d_queries, qkv_weight[0])
     d_normed = d_normed + dot_nn(d_keys, qkv_weight[1])
     d_normed = d_normed + dot_nn(d_values, qkv_weight[2])
@@ -324,31 +330,59 @@
         )
     kept = either(core, loads[0], loads[1]).astype(BF16)
     sent = either(core, loads[1], loads[0]).astype(BF16)
-    return jnp.concatenate([pieces, more, blank], axis=0), kept, sent
-
-
-def settle(part_0, part_1, part_2, part_3):
-    total = sum_four([part_0, part_1, part_2, part_3]).astype(BF16)
-    return (jnp.broadcast_to(total[None], (16, *total.shape)),)
-
-
-def line_sum(arrived):
-    total = arrived[0].astype(F32)
-    for source in range(1, 16):
-        total = total + arrived[source].astype(F32)
-    line = unfold_rows(total)
-    line = jnp.concatenate([line, jnp.zeros((64, 64), F32)], axis=1).astype(BF16)
-    return tuple(line[16 * k : 16 * k + 16] for k in range(4))
+    return kept, sent
+
+
+def settle(part_0, part_1):
+    total = (part_0.astype(F32) + part_1.astype(F32)).astype(BF16)
+    return (jnp.broadcast_to(total[None], (32, *total.shape)),)
+
+
+def pair_sum(arrived):
+    arrived = arrived.reshape(4, 2, 4, 16, 384)
+    own, other = [], []
+    blank = jnp.zeros((16, 64), F32)
+    for h in range(2):
+        total = None
+        for y in range(4):
+            for x in range(4):
+                block = arrived[y, h, x].astype(F32)
+                total = block if total is None else total + block
+        own.append(jnp.concatenate([total[:, :192], blank], axis=1))
+        other.append(jnp.concatenate([total[:, 192:], blank], axis=1))
+    return jnp.concatenate(own, axis=0).astype(BF16), jnp.concatenate(other, axis=0).astype(BF16)
 
 
 def finish(pieces):
-    wide = pieces.astype(F32)
-
-    def join(start, count):
-        return jnp.concatenate([wide[start + i] for i in range(count)], axis=1)
-
-    qkv_grad = jnp.stack([join(0, 3), join(9, 3), join(12, 3)])
-    return qkv_grad, join(3, 6)
+    parts = [(0, 0), (1, 3), (1, 6), (0, 9), (0, 12)]
+
+    def kernel(source, qkv_grad, proj_grad, room, semaphores):
+        copies = []
+        for i, (output, start) in enumerate(parts):
+            for lane in range(3):
+                piece = source[2 * (start + lane) : 2 * (start + lane) + 2].reshape(192, 128)
+                room[i, :, 128 * lane : 128 * lane + 128] = piece.astype(F32)
+            if output == 0:
+                target = qkv_grad.at[(0, None, None, 1, 2)[i]]
+            else:
+                target = proj_grad.at[:, pl.ds(384 * (i - 1), 384)]
+            copies.append(pltpu.make_async_copy(room.at[i], target, semaphores.at[i]))
+            copies[-1].start()
+        for copy in copies:
+            copy.wait()
+
+    return pl.pallas_call(
+        kernel,
+        out_shape=[
+            jax.ShapeDtypeStruct((3, 192, 384), F32),
+            jax.ShapeDtypeStruct((192, 768), F32),
+        ],
+        in_specs=[pl.BlockSpec(memory_space=pltpu.VMEM)],
+        out_specs=[pl.BlockSpec(memory_space=pl.ANY)] * 2,
+        scratch_shapes=[pltpu.VMEM((5, 192, 384), F32), pltpu.SemaphoreType.DMA((5,))],
+        compiler_params=pltpu.CompilerParams(vmem_limit_bytes=32 * 1024 * 1024),
+        name="finish",
+    )(pieces)
 
 
 def mix(kept, received):
@@ -406,17 +440,17 @@
     cot_far = swap(cotangent, "half")
     cot_near = swap(cotangent, "core")
 
-    same_kv, other_kv, normed, held = fuse(
+    own_kv, sent_kv, normed, held = fuse(
         front,
-        [((16, 256), BF16)] * 2 + [((256, 384), BF16)] * 2,
+        [((32, 256), BF16)] * 2 + [((256, 384), BF16)] * 2,
         "front",
         direct=True,
     )(tokens, ln_gain, qkv_weight, key_pool, value_pool)
-    line_kv = [same_kv, shift(other_kv, "z", 1), shift(same_kv, "z", 2), shift(other_kv, "z", 3)]
-    line_kv, cot_far = lax.optimization_barrier((line_kv, cot_far))
+    other_kv = swap_z(sent_kv, 2)
+    other_kv, cot_far, cot_near = lax.optimization_barrier((other_kv, cot_far, cot_near))
     cot_both = swap(cot_far, "core")
-    (copies_kv,) = fuse(copy_line, [((16, 32, 384), BF16)], "copy_line")(*line_kv)
-    rows_kv = exchange(copies_kv, PLANE)
+    (copies_kv,) = fuse(copy_pair, [((32, 16, 384), BF16)], "copy_pair")(own_kv, other_kv)
+    rows_kv = exchange_pairs(copies_kv)
 
     mine, theirs, held_cotangent, skipped, d_pooled = fuse(
         middle,
@@ -441,30 +475,22 @@
         skip_weight,
     )
     rows_grad, mixed, returned = fuse(
-        attend, [((16, 32, 384), BF16), ((64, 256), F32), ((64, 256), BF16)], "attend"
-    )(rows_kv, mine, swap_pair(theirs))
-
-    arrived = exchange(rows_grad, PLANE)
-    line = fuse(line_sum, [((16, 256), BF16)] * 4, "line_sum")(arrived)
-    parts = [line[0]] + [shift(line[k], "z", -k) for k in (1, 2, 3)]
+        attend, [((32, 16, 384), BF16), ((64, 256), F32), ((64, 256), BF16)], "attend"
+    )(rows_kv, mine, swap_z(theirs, 1))
+
+    arrived = exchange_pairs(rows_grad)
+    own_grad, other_grad = fuse(pair_sum, [((32, 256), BF16)] * 2, "pair_sum")(arrived)
+    other_grad = swap_z(other_grad, 2)
     pieces, d_queries, head_part = fuse(
         after, [((9, 192, 128), BF16), ((256, 192), BF16), ((64, 768), BF16)], "after"
-    )(mixed, swap_pair(returned), normed, query_pool, held_cotangent, proj_weight)
-
-    pieces, kept, sent = fuse(
-        weights,
-        [((16, 192, 128), BF16), ((224, 384), BF16), ((224, 384), BF16)],
-        "weights",
-    )(
-        *parts,
-        normed,
-        d_queries,
-        key_pool,
-        value_pool,
-        qkv_weight,
-        pieces,
-        d_pooled,
-        head_part,
+    )(mixed, swap_z(returned, 1), normed, query_pool, held_cotangent, proj_weight)
+
+    pieces, d_keys, d_values = fuse(
+        weights, [((32, 96, 128), BF16)] + [((256, 192), BF16)] * 2, "weights"
+    )(own_grad, other_grad, normed, key_pool, value_pool, pieces)
+    arrived = exchange_pairs(pieces)
+    kept, sent = fuse(spread, [((224, 384), BF16)] * 2, "spread")(
+        d_keys, d_values, d_queries, qkv_weight, d_pooled, head_part
     )
 
     both, sent, staying = fuse(
@@ -472,16 +498,12 @@
     )(kept, swap(sent, "core"))
     taken = swap(sent, "half")
 
-    reduced = jnp.sum(exchange(pieces, PLANE).astype(F32), axis=0).astype(BF16)
+    reduced = jnp.sum(arrived.astype(F32), axis=0).astype(BF16)
     reduced, both = lax.optimization_barrier((reduced, both))
-    (copies,) = fuse(settle, [((16, 192, 128), BF16)], "settle")(
-        reduced, *[shift(reduced, "z", k) for k in (1, 2, 3)]
-    )
-    qkv_grad, proj_grad = fuse(finish, [((3, 192, 384), F32), ((192, 768), F32)], "finish")(
-        exchange(copies, PLANE)
-    )
-
-    own_rows, block_out = fuse(back, [((128, 384), BF16), ((64, 192), BF16)], "back", flops=8 * 10**9)(
+    (copies,) = fuse(settle, [((32, 96, 128), BF16)], "settle")(reduced, swap_z(reduced, 2))
+    qkv_grad, proj_grad = finish(exchange_pairs(copies))
+
+    own_rows, block_out = fuse(back, [((128, 384), BF16), ((64, 192), BF16)], "back", flops=20 * 10**9)(
         both, taken, staying, skipped, held, ln_gain
     )
     (input_grad,) = fuse(unpermute, [((256, 384), BF16)], "unpermute")(

time: 103 us -> 98.8 us (0.959); the launches traced: 101 us -> 98.2 us
  waiting for transfers between devices: 48.1 us -> 46.1 us
  starting transfers between devices: 38.8 us -> 37.4 us
    ppermute x11 -> x5, waiting for transfers between devices: 19.2 us -> 13.4 us  [swap_z(): return lax.ppermute(block, 'z', [(i, i ^ bit) for i in range(4)])]
    all_to_all x4, waiting for transfers between devices: 25.3 us -> 28.8 us  [exchange_pairs(): lax.all_to_all(blocks, TILE, 0, 0, tiled=True, axis_index_groups=groups)]
    ppermute x11 -> x5, starting transfers between devices: 8.06 us -> 6.28 us  [swap_z(): return lax.ppermute(block, 'z', [(i, i ^ bit) for i in range(4)])]
    pallas_call x0 -> x1, Pallas kernels: none -> 1.16 us  [finish(): pl.pallas_call(kernel, out_shape=[jax.ShapeDtypeStruct((3, 192, 384), F32...]
  transfers between devices with their start and end apart: 21 -> 15, of which waited for: 18 -> 11; matrix products, arithmetic and copies ran while one was open for 0% -> 0% of each run, Pallas kernels for 7% -> 7%
where the time goes in v3:
time: 98.8 us; the launch traced here: 98.2 us
  waiting for transfers between devices  46.1 us (47%)
  starting transfers between devices  37.4 us (38%)
  Pallas kernels  12.4 us (13%)
  local copies, waits for them, and re-layouts  1.42 us (1%)
    all_to_all x4, waiting for transfers between devices, exchange_pairs(): lax.all_to_all(blocks, TILE, 0, 0, tiled=True, axis_index_groups=groups)  28.8 us
    all_to_all x4, starting transfers between devices, exchange_pairs(): lax.all_to_all(blocks, TILE, 0, 0, tiled=True, axis_index_groups=groups)  22.9 us
    ppermute x5, waiting for transfers between devices, swap_z(): return lax.ppermute(block, 'z', [(i, i ^ bit) for i in range(4)])  13.4 us
    pallas_call x12, Pallas kernels, call(): pl.pallas_call(kernel, out_shape=[jax.ShapeDtypeStruct(shape, dtype) for...  11.2 us
    ppermute x6, starting transfers between devices, swap(): return lax.ppermute(block, axis, [(0, 1), (1, 0)])  8.25 us
    ppermute x5, starting transfers between devices, swap_z(): return lax.ppermute(block, 'z', [(i, i ^ bit) for i in range(4)])  6.28 us
    ppermute x6, waiting for transfers between devices, swap(): return lax.ppermute(block, axis, [(0, 1), (1, 0)])  3.89 us
  transfers between devices with their start and end apart: 15, of which 11 were waited for; matrix products, arithmetic and copies ran while one was open for 0% of the time, Pallas kernels for 7%

profile of v3, /device:TPU:2, one launch (start us, length us, event | category | flops | bytes accessed | tf_op | source)
XLA Modules:
  0.0 98.2 jit_solution(10046167413671099698)
XLA Ops:
  0.6 7.3 %collective-permute-start.1 = (bf16[64,192]{1,0:T(8,128)(2,1)}, bf16[64,192]{1,0:T(8,128)(2,1)S(1)}, u32[]{:S(2)}, u32[]{:S(2)}) collective-permute-start(bf16[64,192]{1,0:T(8,128)(2,1)} %refs_4_.4), channel_id=1, source_target_pairs={{0,2},{2,0},{1,3},{3,1},{4,6},{6,4},{5,7},{7,5},{8,10},{10,8},{9,1... | collective-permute-start | bytes 73736 | tf_op jit(solution)/shard_map/ppermute | solution.py:25
  7.9 2.6 %front.1 = (bf16[32,256]{1,0:T(8,128)(2,1)}, bf16[32,256]{1,0:T(8,128)(2,1)}, bf16[256,384]{1,0:T(8,128)(2,1)}, bf16[256,384]{1,0:T(8,128)(2,1)}) custom-call(bf16[256,384]{1,0:T(8,128)(2,1)} %refs_0_.1, f32[384]{0:T(512)} %refs_5_.3, bf16[3,192,384]{2,1,0:T(8,128)(2,1)} %refs_3_.9, bf16[16,192]{1,0:T(8,128)(2,1)} %refs_3_.8, bf16[16,192]{1,0:T(8,128)(2,1)} %refs_4_.5), custom_call_target="tpu_custom_call" | custom-call | tf_op jit(solution)/shard_map/front/pallas_call | solution.py:74
  10.5 1.6 %collective-permute-start = (bf16[32,256]{1,0:T(8,128)(2,1)}, bf16[32,256]{1,0:T(8,128)(2,1)S(1)}, u32[]{:S(2)}, u32[]{:S(2)}) collective-permute-start(bf16[32,256]{1,0:T(8,128)(2,1)} %get-tuple-element.39), channel_id=1, source_target_pairs={{0,32},{16,48},{32,0},{48,16},{1,33},{17,49},{33,1},{49,17},{2,34}... | collective-permute-start | bytes 49160 | tf_op jit(solution)/shard_map/ppermute | solution.py:29
  12.1 3.5 %collective-permute-done.refs_1_ = bf16[32,256]{1,0:T(8,128)(2,1)S(1)} collective-permute-done((bf16[32,256]{1,0:T(8,128)(2,1)}, bf16[32,256]{1,0:T(8,128)(2,1)S(1)}, u32[]{:S(2)}, u32[]{:S(2)}) %collective-permute-start) | collective-permute-done | bytes 16416 | tf_op jit(solution)/shard_map/ppermute | solution.py:29
  17.2 8.0 %all-to-all-start = ((bf16[32,16,384]{2,1,0:T(8,128)(2,1)}), bf16[32,16,384]{2,1,0:T(8,128)(2,1)S(1)}, u32[]{:S(2)}, u32[]{:S(2)}) async-start(bf16[32,16,384]{2,1,0:T(8,128)(2,1)} %copy_pair.1), calls=%async_computation | async-start | bytes 786432 | tf_op jit(solution)/shard_map/all_to_all | solution.py:37
  25.4 1.2 %collective-permute-done.3.refs_7_ = bf16[64,192]{1,0:T(8,128)(2,1)S(1)} collective-permute-done((bf16[64,192]{1,0:T(8,128)(2,1)S(1)}, bf16[64,192]{1,0:T(8,128)(2,1)S(1)}, u32[]{:S(2)}, u32[]{:S(2)}) %collective-permute-start.3) | collective-permute-done | bytes 24608 | tf_op jit(solution)/shard_map/ppermute | solution.py:25
  27.3 1.6 %collective-permute-start.4 = (bf16[64,256]{1,0:T(8,128)(2,1)S(1)}, bf16[64,256]{1,0:T(8,128)(2,1)S(1)}, u32[]{:S(2)}, u32[]{:S(2)}) collective-permute-start(bf16[64,256]{1,0:T(8,128)(2,1)S(1)} %get-tuple-element.46), channel_id=1, source_target_pairs={{0,16},{16,0},{32,48},{48,32},{1,17},{17,1},{33,49},{49,33},{2,18}... | collective-permute-start | bytes 98312 | tf_op jit(solution)/shard_map/ppermute | solution.py:29
  28.9 2.6 %collective-permute-done.4.refs_2_ = bf16[64,256]{1,0:T(8,128)(2,1)S(1)} collective-permute-done((bf16[64,256]{1,0:T(8,128)(2,1)S(1)}, bf16[64,256]{1,0:T(8,128)(2,1)S(1)}, u32[]{:S(2)}, u32[]{:S(2)}) %collective-permute-start.4) | collective-permute-done | bytes 32800 | tf_op jit(solution)/shard_map/ppermute | solution.py:29
  31.4 3.1 %all-to-all-done.refs_0_ = bf16[32,16,384]{2,1,0:T(8,128)(2,1)S(1)} async-done(((bf16[32,16,384]{2,1,0:T(8,128)(2,1)}), bf16[32,16,384]{2,1,0:T(8,128)(2,1)S(1)}, u32[]{:S(2)}, u32[]{:S(2)}) %all-to-all-start) | async-done | bytes 393248 | tf_op jit(solution)/shard_map/all_to_all | solution.py:37
  34.5 1.8 %attend.1 = (bf16[32,16,384]{2,1,0:T(8,128)(2,1)}, f32[64,256]{1,0:T(8,128)S(1)}, bf16[64,256]{1,0:T(8,128)(2,1)S(1)}) custom-call(bf16[32,16,384]{2,1,0:T(8,128)(2,1)S(1)} %all-to-all-done.refs_0_, bf16[64,256]{1,0:T(8,128)(2,1)S(1)} %get-tuple-element.45.refs_1_, bf16[64,256]{1,0:T(8,128)(2,1)S(1)} %collective-permute-done.4.refs_2_), custom_call_target="tpu_custom_call" | custom-call | tf_op jit(solution)/shard_map/attend/pallas_call | solution.py:74
  36.3 5.1 %all-to-all-start.1 = ((bf16[32,16,384]{2,1,0:T(8,128)(2,1)}), bf16[32,16,384]{2,1,0:T(8,128)(2,1)S(1)}, u32[]{:S(2)}, u32[]{:S(2)}) async-start(bf16[32,16,384]{2,1,0:T(8,128)(2,1)} %get-tuple-element.47), calls=%async_computation.1 | async-start | bytes 786432 | tf_op jit(solution)/shard_map/all_to_all | solution.py:37
  41.4 1.6 %collective-permute-start.6 = (bf16[64,256]{1,0:T(8,128)(2,1)S(1)}, bf16[64,256]{1,0:T(8,128)(2,1)S(1)}, u32[]{:S(2)}, u32[]{:S(2)}) collective-permute-start(bf16[64,256]{1,0:T(8,128)(2,1)S(1)} %get-tuple-element.51), channel_id=1, source_target_pairs={{0,16},{16,0},{32,48},{48,32},{1,17},{17,1},{33,49},{49,33},{2,18}... | collective-permute-start | bytes 98312 | tf_op jit(solution)/shard_map/ppermute | solution.py:29
  42.9 7.6 %all-to-all-done.1.refs_0_ = bf16[32,16,384]{2,1,0:T(8,128)(2,1)S(1)} async-done(((bf16[32,16,384]{2,1,0:T(8,128)(2,1)}), bf16[32,16,384]{2,1,0:T(8,128)(2,1)S(1)}, u32[]{:S(2)}, u32[]{:S(2)}) %all-to-all-start.1) | async-done | bytes 393248 | tf_op jit(solution)/shard_map/all_to_all | solution.py:37
  50.7 1.5 %collective-permute-start.5 = (bf16[32,256]{1,0:T(8,128)(2,1)S(1)}, bf16[32,256]{1,0:T(8,128)(2,1)S(1)}, u32[]{:S(2)}, u32[]{:S(2)}) collective-permute-start(bf16[32,256]{1,0:T(8,128)(2,1)S(1)} %get-tuple-element.49), channel_id=1, source_target_pairs={{0,32},{16,48},{32,0},{48,16},{1,33},{17,49},{33,1},{49,17},{2,34}... | collective-permute-start | bytes 49160 | tf_op jit(solution)/shard_map/ppermute | solution.py:29
  52.8 2.6 %collective-permute-done.5.refs_1_ = bf16[32,256]{1,0:T(8,128)(2,1)S(1)} collective-permute-done((bf16[32,256]{1,0:T(8,128)(2,1)S(1)}, bf16[32,256]{1,0:T(8,128)(2,1)S(1)}, u32[]{:S(2)}, u32[]{:S(2)}) %collective-permute-start.5) | collective-permute-done | bytes 16416 | tf_op jit(solution)/shard_map/ppermute | solution.py:29
  55.4 1.3 %weights.1 = (bf16[32,96,128]{2,1,0:T(8,128)(2,1)}, bf16[256,192]{1,0:T(8,128)(2,1)S(1)}, bf16[256,192]{1,0:T(8,128)(2,1)S(1)}) custom-call(bf16[32,256]{1,0:T(8,128)(2,1)S(1)} %get-tuple-element.48.refs_0_, bf16[32,256]{1,0:T(8,128)(2,1)S(1)} %collective-permute-done.5.refs_1_, bf16[256,384]{1,0:T(8,128)(2,1)S(1)} %copy-done.1, ...), custom_call_target="tpu_custom_call" | custom-call | tf_op jit(solution)/shard_map/weights/pallas_call | solution.py:74
  56.7 4.6 %all-to-all-start.2 = ((bf16[32,96,128]{2,1,0:T(8,128)(2,1)}), bf16[32,96,128]{2,1,0:T(8,128)(2,1)S(1)}, u32[]{:S(2)}, u32[]{:S(2)}) async-start(bf16[32,96,128]{2,1,0:T(8,128)(2,1)} %get-tuple-element.54), calls=%async_computation.2 | async-start | bytes 1572864 | tf_op jit(solution)/shard_map/all_to_all | solution.py:37
  61.8 1.4 %collective-permute-done.7.refs_1_ = bf16[224,384]{1,0:T(8,128)(2,1)S(1)} collective-permute-done((bf16[224,384]{1,0:T(8,128)(2,1)S(1)}, bf16[224,384]{1,0:T(8,128)(2,1)S(1)}, u32[]{:S(2)}, u32[]{:S(2)}) %collective-permute-start.7) | collective-permute-done | bytes 172064 | tf_op jit(solution)/shard_map/ppermute | solution.py:25
  64.2 11.2 %all-to-all-done.2 = bf16[32,96,128]{2,1,0:T(8,128)(2,1)S(1)} async-done(((bf16[32,96,128]{2,1,0:T(8,128)(2,1)}), bf16[32,96,128]{2,1,0:T(8,128)(2,1)S(1)}, u32[]{:S(2)}, u32[]{:S(2)}) %all-to-all-start.2) | async-done | bytes 786464 | tf_op jit(solution)/shard_map/all_to_all | solution.py:37
  75.6 4.7 %collective-permute-done.10.refs_1_ = bf16[96,128]{1,0:T(8,128)(2,1)S(1)} collective-permute-done((bf16[96,128]{1,0:T(8,128)(2,1)S(1)}, bf16[96,128]{1,0:T(8,128)(2,1)S(1)}, u32[]{:S(2)}, u32[]{:S(2)}) %collective-permute-start.10) | collective-permute-done | bytes 24608 | tf_op jit(solution)/shard_map/ppermute | solution.py:29
  81.3 5.1 %all-to-all-start.3 = ((bf16[32,96,128]{2,1,0:T(8,128)(2,1)}), bf16[32,96,128]{2,1,0:T(8,128)(2,1)S(1)}, u32[]{:S(2)}, u32[]{:S(2)}) async-start(bf16[32,96,128]{2,1,0:T(8,128)(2,1)} %settle.1), calls=%async_computation.3 | async-start | bytes 1572864 | tf_op jit(solution)/shard_map/all_to_all | solution.py:37
  88.0 1.3 %collective-permute-done.9.refs_1_ = bf16[128,384]{1,0:T(8,128)(2,1)S(1)} collective-permute-done((bf16[128,384]{1,0:T(8,128)(2,1)S(1)}, bf16[128,384]{1,0:T(8,128)(2,1)S(1)}, u32[]{:S(2)}, u32[]{:S(2)}) %collective-permute-start.9) | collective-permute-done | bytes 98336 | tf_op jit(solution)/shard_map/ppermute | solution.py:25
  90.2 6.9 %all-to-all-done.3.source = bf16[32,96,128]{2,1,0:T(8,128)(2,1)S(1)} async-done(((bf16[32,96,128]{2,1,0:T(8,128)(2,1)}), bf16[32,96,128]{2,1,0:T(8,128)(2,1)S(1)}, u32[]{:S(2)}, u32[]{:S(2)}) %all-to-all-start.3) | async-done | bytes 786464 | tf_op jit(solution)/shard_map/all_to_all | solution.py:37
  97.0 1.2 %finish.1 = (f32[3,192,384]{2,1,0:T(8,128)}, f32[192,768]{1,0:T(8,128)}) custom-call(bf16[32,96,128]{2,1,0:T(8,128)(2,1)S(1)} %all-to-all-done.3.source), custom_call_target="tpu_custom_call" | custom-call | tf_op jit(solution)/shard_map/finish/pallas_call | solution.py:374
  (42 shorter events, 8.1 us)
Async XLA Ops:
  0.6 15.0 %collective-permute-start.1 = (bf16[64,192]{1,0:T(8,128)(2,1)}, bf16[64,192]{1,0:T(8,128)(2,1)S(1)}, u32[]{:S(2)}, u32[]{:S(2)}) collective-permute-start(bf16[64,192]{1,0:T(8,128)(2,1)} %refs_4_.4), channel_id=1, source_target_pairs={{0,2},{2,0},{1,3},{3,1},{4,6},{6,4},{5,7},{7,5},{8,10},{10,8},{9,1... | collective-permute-start | bytes 73736 | tf_op jit(solution)/shard_map/ppermute | solution.py:25
  7.9 7.7 %collective-permute-start.2 = (bf16[64,192]{1,0:T(8,128)(2,1)}, bf16[64,192]{1,0:T(8,128)(2,1)S(1)}, u32[]{:S(2)}, u32[]{:S(2)}) collective-permute-start(bf16[64,192]{1,0:T(8,128)(2,1)} %refs_4_.4), channel_id=1, source_target_pairs={{0,1},{1,0},{2,3},{3,2},{4,5},{5,4},{6,7},{7,6},{8,9},{9,8},{10,11... | collective-permute-start | bytes 73736 | tf_op jit(solution)/shard_map/ppermute | solution.py:25
  7.9 18.7 %copy-start.4 = (bf16[192,384]{1,0:T(8,128)(2,1)S(1)}, bf16[192,384]{1,0:T(8,128)(2,1)}, u32[]{:S(2)}) copy-start(bf16[192,384]{1,0:T(8,128)(2,1)} %refs_9_.1) | copy-start | bytes 442372
  10.5 5.1 %collective-permute-start = (bf16[32,256]{1,0:T(8,128)(2,1)}, bf16[32,256]{1,0:T(8,128)(2,1)S(1)}, u32[]{:S(2)}, u32[]{:S(2)}) collective-permute-start(bf16[32,256]{1,0:T(8,128)(2,1)} %get-tuple-element.39), channel_id=1, source_target_pairs={{0,32},{16,48},{32,0},{48,16},{1,33},{17,49},{33,1},{49,17},{2,34}... | collective-permute-start | bytes 49160 | tf_op jit(solution)/shard_map/ppermute | solution.py:29
  16.4 10.2 %copy-start.2 = (bf16[192,768]{1,0:T(8,128)(2,1)S(1)}, bf16[192,768]{1,0:T(8,128)(2,1)}, u32[]{:S(2)}) copy-start(bf16[192,768]{1,0:T(8,128)(2,1)} %refs_5_.2) | copy-start | bytes 884740
  16.4 10.2 %copy-start.3 = (bf16[256,384]{1,0:T(8,128)(2,1)S(1)}, bf16[256,384]{1,0:T(8,128)(2,1)}, u32[]{:S(2)}) copy-start(bf16[256,384]{1,0:T(8,128)(2,1)} %get-tuple-element.42.refs_1_.refs_4_) | copy-start | bytes 589828
  17.2 9.4 %copy-start = (bf16[3,192,384]{2,1,0:T(8,128)(2,1)S(1)}, bf16[3,192,384]{2,1,0:T(8,128)(2,1)}, u32[]{:S(2)}) copy-start(bf16[3,192,384]{2,1,0:T(8,128)(2,1)} %refs_3_.9) | copy-start | bytes 1327108
  17.2 9.4 %copy-start.1 = (bf16[256,384]{1,0:T(8,128)(2,1)S(1)}, bf16[256,384]{1,0:T(8,128)(2,1)}, u32[]{:S(2)}) copy-start(bf16[256,384]{1,0:T(8,128)(2,1)} %get-tuple-element.41.refs_0_.refs_2_) | copy-start | bytes 589828
  17.2 9.4 %copy-start.7 = (bf16[64,192]{1,0:T(8,128)(2,1)S(1)}, bf16[64,192]{1,0:T(8,128)(2,1)}, u32[]{:S(2)}) copy-start(bf16[64,192]{1,0:T(8,128)(2,1)} %refs_4_.4) | copy-start | bytes 73732
  17.2 17.2 %all-to-all-start = ((bf16[32,16,384]{2,1,0:T(8,128)(2,1)}), bf16[32,16,384]{2,1,0:T(8,128)(2,1)S(1)}, u32[]{:S(2)}, u32[]{:S(2)}) async-start(bf16[32,16,384]{2,1,0:T(8,128)(2,1)} %copy_pair.1), calls=%async_computation | async-start | bytes 786432 | tf_op jit(solution)/shard_map/all_to_all | solution.py:37
  25.3 1.4 %copy-start.9 = (bf16[4,192]{1,0:T(4,128)(2,1)S(1)}, bf16[4,192]{1,0:T(4,128)(2,1)}, u32[]{:S(2)}) copy-start(bf16[4,192]{1,0:T(4,128)(2,1)} %refs_3_.7) | copy-start | bytes 4612
  25.3 1.3 %collective-permute-start.3 = (bf16[64,192]{1,0:T(8,128)(2,1)S(1)}, bf16[64,192]{1,0:T(8,128)(2,1)S(1)}, u32[]{:S(2)}, u32[]{:S(2)}) collective-permute-start(bf16[64,192]{1,0:T(8,128)(2,1)S(1)} %collective-permute-done.1.refs_6_), channel_id=1, source_target_pairs={{0,1},{1,0},{2,3},{3,2},{4,5},{5,4},{6,7},{7,6},{8,9},{9,8},{10,11... | collective-permute-start | bytes 73736 | tf_op jit(solution)/shard_map/ppermute | solution.py:25
  27.3 4.1 %collective-permute-start.4 = (bf16[64,256]{1,0:T(8,128)(2,1)S(1)}, bf16[64,256]{1,0:T(8,128)(2,1)S(1)}, u32[]{:S(2)}, u32[]{:S(2)}) collective-permute-start(bf16[64,256]{1,0:T(8,128)(2,1)S(1)} %get-tuple-element.46), channel_id=1, source_target_pairs={{0,16},{16,0},{32,48},{48,32},{1,17},{17,1},{33,49},{49,33},{2,18}... | collective-permute-start | bytes 98312 | tf_op jit(solution)/shard_map/ppermute | solution.py:29
  36.3 14.3 %all-to-all-start.1 = ((bf16[32,16,384]{2,1,0:T(8,128)(2,1)}), bf16[32,16,384]{2,1,0:T(8,128)(2,1)S(1)}, u32[]{:S(2)}, u32[]{:S(2)}) async-start(bf16[32,16,384]{2,1,0:T(8,128)(2,1)} %get-tuple-element.47), calls=%async_computation.1 | async-start | bytes 786432 | tf_op jit(solution)/shard_map/all_to_all | solution.py:37
  41.4 10.8 %collective-permute-start.6 = (bf16[64,256]{1,0:T(8,128)(2,1)S(1)}, bf16[64,256]{1,0:T(8,128)(2,1)S(1)}, u32[]{:S(2)}, u32[]{:S(2)}) collective-permute-start(bf16[64,256]{1,0:T(8,128)(2,1)S(1)} %get-tuple-element.51), channel_id=1, source_target_pairs={{0,16},{16,0},{32,48},{48,32},{1,17},{17,1},{33,49},{49,33},{2,18}... | collective-permute-start | bytes 98312 | tf_op jit(solution)/shard_map/ppermute | solution.py:29
  50.7 4.7 %collective-permute-start.5 = (bf16[32,256]{1,0:T(8,128)(2,1)S(1)}, bf16[32,256]{1,0:T(8,128)(2,1)S(1)}, u32[]{:S(2)}, u32[]{:S(2)}) collective-permute-start(bf16[32,256]{1,0:T(8,128)(2,1)S(1)} %get-tuple-element.49), channel_id=1, source_target_pairs={{0,32},{16,48},{32,0},{48,16},{1,33},{17,49},{33,1},{49,17},{2,34}... | collective-permute-start | bytes 49160 | tf_op jit(solution)/shard_map/ppermute | solution.py:29
  52.2 3.2 %copy-start.5 = (bf16[16,192]{1,0:T(8,128)(2,1)S(1)}, bf16[16,192]{1,0:T(8,128)(2,1)}, u32[]{:S(2)}) copy-start(bf16[16,192]{1,0:T(8,128)(2,1)} %refs_3_.8) | copy-start | bytes 18436
  52.2 3.2 %copy-start.6 = (bf16[16,192]{1,0:T(8,128)(2,1)S(1)}, bf16[16,192]{1,0:T(8,128)(2,1)}, u32[]{:S(2)}) copy-start(bf16[16,192]{1,0:T(8,128)(2,1)} %refs_4_.5) | copy-start | bytes 18436
  56.7 18.7 %all-to-all-start.2 = ((bf16[32,96,128]{2,1,0:T(8,128)(2,1)}), bf16[32,96,128]{2,1,0:T(8,128)(2,1)S(1)}, u32[]{:S(2)}, u32[]{:S(2)}) async-start(bf16[32,96,128]{2,1,0:T(8,128)(2,1)} %get-tuple-element.54), calls=%async_computation.2 | async-start | bytes 1572864 | tf_op jit(solution)/shard_map/all_to_all | solution.py:37
  61.7 1.5 %collective-permute-start.7 = (bf16[224,384]{1,0:T(8,128)(2,1)S(1)}, bf16[224,384]{1,0:T(8,128)(2,1)S(1)}, u32[]{:S(2)}, u32[]{:S(2)}) collective-permute-start(bf16[224,384]{1,0:T(8,128)(2,1)S(1)} %get-tuple-element.61), channel_id=1, source_target_pairs={{0,1},{1,0},{2,3},{3,2},{4,5},{5,4},{6,7},{7,6},{8,9},{9,8},{10,11... | collective-permute-start | bytes 516104 | tf_op jit(solution)/shard_map/ppermute | solution.py:25
  63.4 23.0 %collective-permute-start.8 = (bf16[192,384]{1,0:T(8,128)(2,1)S(1)}, bf16[192,384]{1,0:T(8,128)(2,1)S(1)}, u32[]{:S(2)}, u32[]{:S(2)}) collective-permute-start(bf16[192,384]{1,0:T(8,128)(2,1)S(1)} %get-tuple-element.64), channel_id=1, source_target_pairs={{0,2},{2,0},{1,3},{3,1},{4,6},{6,4},{5,7},{7,5},{8,10},{10,8},{9,1... | collective-permute-start | bytes 442376 | tf_op jit(solution)/shard_map/ppermute | solution.py:25
  75.5 4.8 %collective-permute-start.10 = (bf16[96,128]{1,0:T(8,128)(2,1)S(1)}, bf16[96,128]{1,0:T(8,128)(2,1)S(1)}, u32[]{:S(2)}, u32[]{:S(2)}) collective-permute-start(bf16[96,128]{1,0:T(8,128)(2,1)S(1)} %reduce_sum.12.refs_0_), channel_id=1, source_target_pairs={{0,32},{16,48},{32,0},{48,16},{1,33},{17,49},{33,1},{49,17},{2,34}... | collective-permute-start | bytes 73736 | tf_op jit(solution)/shard_map/ppermute | solution.py:29
  81.3 15.8 %all-to-all-start.3 = ((bf16[32,96,128]{2,1,0:T(8,128)(2,1)}), bf16[32,96,128]{2,1,0:T(8,128)(2,1)S(1)}, u32[]{:S(2)}, u32[]{:S(2)}) async-start(bf16[32,96,128]{2,1,0:T(8,128)(2,1)} %settle.1), calls=%async_computation.3 | async-start | bytes 1572864 | tf_op jit(solution)/shard_map/all_to_all | solution.py:37
  88.0 1.3 %collective-permute-start.9 = (bf16[128,384]{1,0:T(8,128)(2,1)S(1)}, bf16[128,384]{1,0:T(8,128)(2,1)S(1)}, u32[]{:S(2)}, u32[]{:S(2)}) collective-permute-start(bf16[128,384]{1,0:T(8,128)(2,1)S(1)} %get-tuple-element.68.refs_0_), channel_id=1, source_target_pairs={{0,1},{1,0},{2,3},{3,2},{4,5},{5,4},{6,7},{7,6},{8,9},{9,8},{10,11... | collective-permute-start | bytes 294920 | tf_op jit(solution)/shard_map/ppermute | solution.py:25
  (2 other events, 1.4 us)

commit v4 on v3

--- a/solution.py
+++ b/solution.py
@@ -309,20 +309,32 @@
     return pieces, d_keys, d_values
 
 
-def spread(d_keys, d_values, d_queries, qkv_weight, d_pooled, head_part):
+def spread(d_keys, d_values, d_queries, qkv_weight, d_pooled, head_part, held, ln_gain):
     core = lax.axis_index("core")
     d_normed = dot_nn(d_queries, qkv_weight[0])
     d_normed = d_normed + dot_nn(d_keys, qkv_weight[1])
     d_normed = d_normed + dot_nn(d_values, qkv_weight[2])
-    pooled, rows = d_pooled.astype(F32), head_part.astype(F32)
+    unit, inv_std = normalize(held.astype(F32))
+    scaled = d_normed * ln_gain[None, :]
+    grad = inv_std * (
+        scaled
+        - jnp.mean(scaled, axis=-1, keepdims=True)
+        - unit * jnp.mean(scaled * unit, axis=-1, keepdims=True)
+    )
+    pooled, rows = d_pooled.astype(F32) * 0.25, head_part.astype(F32)
+    grown = []
+    for block in range(16):
+        place = 2 * (block // 8) + (block % 4) // 2
+        grown.append(pooled[16 * place : 16 * place + 16])
+    grad = (grad + jnp.concatenate(grown, axis=0)).astype(BF16)
+    grad = dot_nn(selector(256, token_of, True), grad)
     loads = []
     for c in range(2):
         channels = [rows[:, 192 * (2 * p + c) : 192 * (2 * p + c) + 192] for p in range(2)]
         loads.append(
             jnp.concatenate(
                 [
-                    d_normed[128 * c : 128 * c + 128],
-                    pooled[32 * c : 32 * c + 32],
+                    grad[128 * c : 128 * c + 128],
                     jnp.concatenate(channels, axis=1),
                 ],
                 axis=0,
@@ -388,42 +400,26 @@
 def mix(kept, received):
     half = lax.axis_index("half")
     both = kept.astype(F32) + received.astype(F32)
-    rows = [both[160:, :192], both[160:, 192:]]
+    rows = [both[128:, :192], both[128:, 192:]]
     leaving = either(half, rows[1], rows[0])
     staying = either(half, rows[0], rows[1])
     folded = jnp.concatenate([leaving[:32], leaving[32:]], axis=1)
-    return both[:160].astype(BF16), jnp.concatenate([both[:160], folded], axis=0).astype(BF16), staying
-
-
-def back(both, taken, staying, skipped, held, ln_gain):
-    core = lax.axis_index("core")
-    total = both.astype(F32) + taken[:160].astype(F32)
-    held = held.astype(F32)
-    unit, inv_std = normalize(either(core, held[:128], held[128:]))
-    scaled = total[:128] * ln_gain[None, :]
-    grad = inv_std * (
-        scaled
-        - jnp.mean(scaled, axis=-1, keepdims=True)
-        - unit * jnp.mean(scaled * unit, axis=-1, keepdims=True)
-    )
-    pooled = total[128:160] * 0.25
-    grown = []
-    for block in range(8):
-        half = (block % 4) // 2
-        grown.append(pooled[16 * half : 16 * half + 16])
-    folded = taken[160:].astype(F32)
+    sent = jnp.concatenate([both[:128], folded], axis=0).astype(BF16)
+    return both[:128].astype(BF16), sent, staying
+
+
+def back(both, taken, staying, skipped):
+    rows = both.astype(F32) + taken[:128].astype(F32)
+    folded = taken[128:].astype(F32)
     arrived = jnp.concatenate([folded[:, :192], folded[:, 192:]], axis=0)
-    block_out = (staying + arrived + skipped).astype(BF16)
-    return (grad + jnp.concatenate(grown, axis=0)).astype(BF16), block_out
-
-
-def unpermute(own_rows, other_rows):
+    return rows.astype(BF16), (staying + arrived + skipped).astype(BF16)
+
+
+def join(own_rows, other_rows):
     core = lax.axis_index("core")
     own_rows, other_rows = own_rows.astype(F32), other_rows.astype(F32)
-    ordered = jnp.concatenate(
-        [either(core, own_rows, other_rows), either(core, other_rows, own_rows)], axis=0
-    ).astype(BF16)
-    return (dot_nn(selector(256, token_of, True), ordered).astype(BF16),)
+    rows = [either(core, own_rows, other_rows), either(core, other_rows, own_rows)]
+    return (jnp.concatenate(rows, axis=0).astype(BF16),)
 
 
 def local(
@@ -437,7 +433,6 @@
     skip_weight,
     cotangent,
 ):
-    cot_far = swap(cotangent, "half")
     cot_near = swap(cotangent, "core")
 
     own_kv, sent_kv, normed, held = fuse(
@@ -447,9 +442,11 @@
         direct=True,
     )(tokens, ln_gain, qkv_weight, key_pool, value_pool)
     other_kv = swap_z(sent_kv, 2)
-    other_kv, cot_far, cot_near = lax.optimization_barrier((other_kv, cot_far, cot_near))
+    leaving, held = lax.optimization_barrier((cotangent, held))
+    cot_far = swap(leaving, "half")
+    (copies_kv,) = fuse(copy_pair, [((32, 16, 384), BF16)], "copy_pair")(own_kv, other_kv)
+    copies_kv, cot_far, cot_near = lax.optimization_barrier((copies_kv, cot_far, cot_near))
     cot_both = swap(cot_far, "core")
-    (copies_kv,) = fuse(copy_pair, [((32, 16, 384), BF16)], "copy_pair")(own_kv, other_kv)
     rows_kv = exchange_pairs(copies_kv)
 
     mine, theirs, held_cotangent, skipped, d_pooled = fuse(
@@ -489,12 +486,12 @@
         weights, [((32, 96, 128), BF16)] + [((256, 192), BF16)] * 2, "weights"
     )(own_grad, other_grad, normed, key_pool, value_pool, pieces)
     arrived = exchange_pairs(pieces)
-    kept, sent = fuse(spread, [((224, 384), BF16)] * 2, "spread")(
-        d_keys, d_values, d_queries, qkv_weight, d_pooled, head_part
+    kept, sent = fuse(spread, [((192, 384), BF16)] * 2, "spread")(
+        d_keys, d_values, d_queries, qkv_weight, d_pooled, head_part, held, ln_gain
     )
 
     both, sent, staying = fuse(
-        mix, [((160, 384), BF16), ((192, 384), BF16), ((64, 192), F32)], "mix"
+        mix, [((128, 384), BF16), ((160, 384), BF16), ((64, 192), F32)], "mix"
     )(kept, swap(sent, "core"))
     taken = swap(sent, "half")
 
@@ -504,9 +501,9 @@
     qkv_grad, proj_grad = finish(exchange_pairs(copies))
 
     own_rows, block_out = fuse(back, [((128, 384), BF16), ((64, 192), BF16)], "back", flops=20 * 10**9)(
-        both, taken, staying, skipped, held, ln_gain
-    )
-    (input_grad,) = fuse(unpermute, [((256, 384), BF16)], "unpermute")(
+        both, taken, staying, skipped
+    )
+    (input_grad,) = fuse(join, [((256, 384), BF16)], "join")(
         own_rows, swap(own_rows, "core")
     )
     return (block_out, input_grad, qkv_grad, proj_grad)

time: 98.8 us -> 97.1 us (0.983)
  waiting for transfers between devices: 46.1 us -> 42.1 us
  starting transfers between devices: 37.4 us -> 39.8 us
    all_to_all x4, waiting for transfers between devices: 28.8 us -> 26.1 us  [exchange_pairs(): lax.all_to_all(blocks, TILE, 0, 0, tiled=True, axis_index_groups=groups)]
    ppermute x5, starting transfers between devices: 6.28 us -> 7.63 us  [swap_z(): return lax.ppermute(block, 'z', [(i, i ^ bit) for i in range(4)])]
    ppermute x5, waiting for transfers between devices: 13.4 us -> 12.1 us  [swap_z(): return lax.ppermute(block, 'z', [(i, i ^ bit) for i in range(4)])]
  transfers between devices with their start and end apart: 15 -> 15, of which waited for: 11 -> 11; matrix products, arithmetic and copies ran while one was open for 0% -> 0% of each run, Pallas kernels for 7% -> 8%
where the time goes in v4:
time: 97.1 us; the launch traced here: 96.5 us
  waiting for transfers between devices  42.1 us (43%)
  starting transfers between devices  39.8 us (41%)
  Pallas kernels  12.3 us (13%)
  local copies, waits for them, and re-layouts  1.43 us (1%)
    all_to_all x4, waiting for transfers between devices, exchange_pairs(): lax.all_to_all(blocks, TILE, 0, 0, tiled=True, axis_index_groups=groups)  26.1 us
    all_to_all x4, starting transfers between devices, exchange_pairs(): lax.all_to_all(blocks, TILE, 0, 0, tiled=True, axis_index_groups=groups)  23.2 us
    ppermute x5, waiting for transfers between devices, swap_z(): return lax.ppermute(block, 'z', [(i, i ^ bit) for i in range(4)])  12.1 us
    pallas_call x12, Pallas kernels, call(): pl.pallas_call(kernel, out_shape=[jax.ShapeDtypeStruct(shape, dtype) for...  11.1 us
    ppermute x6, starting transfers between devices, swap(): return lax.ppermute(block, axis, [(0, 1), (1, 0)])  9.02 us
    ppermute x5, starting transfers between devices, swap_z(): return lax.ppermute(block, 'z', [(i, i ^ bit) for i in range(4)])  7.63 us
    ppermute x6, waiting for transfers between devices, swap(): return lax.ppermute(block, axis, [(0, 1), (1, 0)])  3.86 us
  transfers between devices with their start and end apart: 15, of which 11 were waited for; matrix products, arithmetic and copies ran while one was open for 0% of the time, Pallas kernels for 8%

profile of v4, /device:TPU:2, one launch (start us, length us, event | category | flops | bytes accessed | tf_op | source)
XLA Modules:
  0.0 96.5 jit_solution(10918651205881333230)
XLA Ops:
  0.8 2.6 %front.1 = (bf16[32,256]{1,0:T(8,128)(2,1)}, bf16[32,256]{1,0:T(8,128)(2,1)}, bf16[256,384]{1,0:T(8,128)(2,1)}, bf16[256,384]{1,0:T(8,128)(2,1)}) custom-call(bf16[256,384]{1,0:T(8,128)(2,1)} %refs_0_.1, f32[384]{0:T(512)} %refs_7_.1, bf16[3,192,384]{2,1,0:T(8,128)(2,1)} %refs_3_.9, bf16[16,192]{1,0:T(8,128)(2,1)} %refs_3_.8, bf16[16,192]{1,0:T(8,128)(2,1)} %refs_4_.5), custom_call_target="tpu_custom_call" | custom-call | tf_op jit(solution)/shard_map/front/pallas_call | solution.py:74
  3.4 7.3 %collective-permute-start.1 = (bf16[64,192]{1,0:T(8,128)(2,1)S(1)}, bf16[64,192]{1,0:T(8,128)(2,1)S(1)}, u32[]{:S(2)}, u32[]{:S(2)}) collective-permute-start(bf16[64,192]{1,0:T(8,128)(2,1)S(1)} %copy-done.7), channel_id=1, source_target_pairs={{0,2},{2,0},{1,3},{3,1},{4,6},{6,4},{5,7},{7,5},{8,10},{10,8},{9,1... | collective-permute-start | bytes 73736 | tf_op jit(solution)/shard_map/ppermute | solution.py:25
  10.7 1.5 %collective-permute-start = (bf16[32,256]{1,0:T(8,128)(2,1)}, bf16[32,256]{1,0:T(8,128)(2,1)S(1)}, u32[]{:S(2)}, u32[]{:S(2)}) collective-permute-start(bf16[32,256]{1,0:T(8,128)(2,1)} %get-tuple-element.41), channel_id=1, source_target_pairs={{0,32},{16,48},{32,0},{48,16},{1,33},{17,49},{33,1},{49,17},{2,34}... | collective-permute-start | bytes 49160 | tf_op jit(solution)/shard_map/ppermute | solution.py:29
  12.1 3.4 %collective-permute-done.refs_1_ = bf16[32,256]{1,0:T(8,128)(2,1)S(1)} collective-permute-done((bf16[32,256]{1,0:T(8,128)(2,1)}, bf16[32,256]{1,0:T(8,128)(2,1)S(1)}, u32[]{:S(2)}, u32[]{:S(2)}) %collective-permute-start) | collective-permute-done | bytes 16416 | tf_op jit(solution)/shard_map/ppermute | solution.py:29
  17.1 8.2 %all-to-all-start = ((bf16[32,16,384]{2,1,0:T(8,128)(2,1)}), bf16[32,16,384]{2,1,0:T(8,128)(2,1)S(1)}, u32[]{:S(2)}, u32[]{:S(2)}) async-start(bf16[32,16,384]{2,1,0:T(8,128)(2,1)} %copy_pair.1), calls=%async_computation | async-start | bytes 786432 | tf_op jit(solution)/shard_map/all_to_all | solution.py:37
  27.3 1.6 %collective-permute-start.4 = (bf16[64,256]{1,0:T(8,128)(2,1)S(1)}, bf16[64,256]{1,0:T(8,128)(2,1)S(1)}, u32[]{:S(2)}, u32[]{:S(2)}) collective-permute-start(bf16[64,256]{1,0:T(8,128)(2,1)S(1)} %get-tuple-element.50), channel_id=1, source_target_pairs={{0,16},{16,0},{32,48},{48,32},{1,17},{17,1},{33,49},{49,33},{2,18}... | collective-permute-start | bytes 98312 | tf_op jit(solution)/shard_map/ppermute | solution.py:29
  28.9 2.4 %collective-permute-done.4.refs_2_ = bf16[64,256]{1,0:T(8,128)(2,1)S(1)} collective-permute-done((bf16[64,256]{1,0:T(8,128)(2,1)S(1)}, bf16[64,256]{1,0:T(8,128)(2,1)S(1)}, u32[]{:S(2)}, u32[]{:S(2)}) %collective-permute-start.4) | collective-permute-done | bytes 32800 | tf_op jit(solution)/shard_map/ppermute | solution.py:29
  31.3 2.8 %all-to-all-done.refs_0_ = bf16[32,16,384]{2,1,0:T(8,128)(2,1)S(1)} async-done(((bf16[32,16,384]{2,1,0:T(8,128)(2,1)}), bf16[32,16,384]{2,1,0:T(8,128)(2,1)S(1)}, u32[]{:S(2)}, u32[]{:S(2)}) %all-to-all-start) | async-done | bytes 393248 | tf_op jit(solution)/shard_map/all_to_all | solution.py:37
  34.2 1.8 %attend.1 = (bf16[32,16,384]{2,1,0:T(8,128)(2,1)}, f32[64,256]{1,0:T(8,128)S(1)}, bf16[64,256]{1,0:T(8,128)(2,1)S(1)}) custom-call(bf16[32,16,384]{2,1,0:T(8,128)(2,1)S(1)} %all-to-all-done.refs_0_, bf16[64,256]{1,0:T(8,128)(2,1)S(1)} %get-tuple-element.49.refs_1_, bf16[64,256]{1,0:T(8,128)(2,1)S(1)} %collective-permute-done.4.refs_2_), custom_call_target="tpu_custom_call" | custom-call | tf_op jit(solution)/shard_map/attend/pallas_call | solution.py:74
  35.9 5.5 %all-to-all-start.1 = ((bf16[32,16,384]{2,1,0:T(8,128)(2,1)}), bf16[32,16,384]{2,1,0:T(8,128)(2,1)S(1)}, u32[]{:S(2)}, u32[]{:S(2)}) async-start(bf16[32,16,384]{2,1,0:T(8,128)(2,1)} %get-tuple-element.51), calls=%async_computation.1 | async-start | bytes 786432 | tf_op jit(solution)/shard_map/all_to_all | solution.py:37
  41.4 1.6 %collective-permute-start.6 = (bf16[64,256]{1,0:T(8,128)(2,1)S(1)}, bf16[64,256]{1,0:T(8,128)(2,1)S(1)}, u32[]{:S(2)}, u32[]{:S(2)}) collective-permute-start(bf16[64,256]{1,0:T(8,128)(2,1)S(1)} %get-tuple-element.55), channel_id=1, source_target_pairs={{0,16},{16,0},{32,48},{48,32},{1,17},{17,1},{33,49},{49,33},{2,18}... | collective-permute-start | bytes 98312 | tf_op jit(solution)/shard_map/ppermute | solution.py:29
  43.0 7.4 %all-to-all-done.1.refs_0_ = bf16[32,16,384]{2,1,0:T(8,128)(2,1)S(1)} async-done(((bf16[32,16,384]{2,1,0:T(8,128)(2,1)}), bf16[32,16,384]{2,1,0:T(8,128)(2,1)S(1)}, u32[]{:S(2)}, u32[]{:S(2)}) %all-to-all-start.1) | async-done | bytes 393248 | tf_op jit(solution)/shard_map/all_to_all | solution.py:37
  50.5 1.5 %collective-permute-start.5 = (bf16[32,256]{1,0:T(8,128)(2,1)S(1)}, bf16[32,256]{1,0:T(8,128)(2,1)S(1)}, u32[]{:S(2)}, u32[]{:S(2)}) collective-permute-start(bf16[32,256]{1,0:T(8,128)(2,1)S(1)} %get-tuple-element.53), channel_id=1, source_target_pairs={{0,32},{16,48},{32,0},{48,16},{1,33},{17,49},{33,1},{49,17},{2,34}... | collective-permute-start | bytes 49160 | tf_op jit(solution)/shard_map/ppermute | solution.py:29
  52.7 2.6 %collective-permute-done.5.refs_1_ = bf16[32,256]{1,0:T(8,128)(2,1)S(1)} collective-permute-done((bf16[32,256]{1,0:T(8,128)(2,1)S(1)}, bf16[32,256]{1,0:T(8,128)(2,1)S(1)}, u32[]{:S(2)}, u32[]{:S(2)}) %collective-permute-start.5) | collective-permute-done | bytes 16416 | tf_op jit(solution)/shard_map/ppermute | solution.py:29
  55.3 1.3 %weights.1 = (bf16[32,96,128]{2,1,0:T(8,128)(2,1)}, bf16[256,192]{1,0:T(8,128)(2,1)S(1)}, bf16[256,192]{1,0:T(8,128)(2,1)S(1)}) custom-call(bf16[32,256]{1,0:T(8,128)(2,1)S(1)} %get-tuple-element.52.refs_0_, bf16[32,256]{1,0:T(8,128)(2,1)S(1)} %collective-permute-done.5.refs_1_, bf16[256,384]{1,0:T(8,128)(2,1)S(1)} %copy-done.1, ...), custom_call_target="tpu_custom_call" | custom-call | tf_op jit(solution)/shard_map/weights/pallas_call | solution.py:74
  56.6 4.7 %all-to-all-start.2 = ((bf16[32,96,128]{2,1,0:T(8,128)(2,1)}), bf16[32,96,128]{2,1,0:T(8,128)(2,1)S(1)}, u32[]{:S(2)}, u32[]{:S(2)}) async-start(bf16[32,96,128]{2,1,0:T(8,128)(2,1)} %get-tuple-element.58), calls=%async_computation.2 | async-start | bytes 1572864 | tf_op jit(solution)/shard_map/all_to_all | solution.py:37
  62.8 1.4 %collective-permute-done.7.refs_1_ = bf16[192,384]{1,0:T(8,128)(2,1)S(1)} collective-permute-done((bf16[192,384]{1,0:T(8,128)(2,1)S(1)}, bf16[192,384]{1,0:T(8,128)(2,1)S(1)}, u32[]{:S(2)}, u32[]{:S(2)}) %collective-permute-start.7) | collective-permute-done | bytes 147488 | tf_op jit(solution)/shard_map/ppermute | solution.py:25
  64.3 1.5 %collective-permute-start.8 = (bf16[160,384]{1,0:T(8,128)(2,1)S(1)}, bf16[160,384]{1,0:T(8,128)(2,1)S(1)}, u32[]{:S(2)}, u32[]{:S(2)}) collective-permute-start(bf16[160,384]{1,0:T(8,128)(2,1)S(1)} %get-tuple-element.68), channel_id=1, source_target_pairs={{0,2},{2,0},{1,3},{3,1},{4,6},{6,4},{5,7},{7,5},{8,10},{10,8},{9,1... | collective-permute-start | bytes 368648 | tf_op jit(solution)/shard_map/ppermute | solution.py:25
  65.8 6.6 %all-to-all-done.2 = bf16[32,96,128]{2,1,0:T(8,128)(2,1)S(1)} async-done(((bf16[32,96,128]{2,1,0:T(8,128)(2,1)}), bf16[32,96,128]{2,1,0:T(8,128)(2,1)S(1)}, u32[]{:S(2)}, u32[]{:S(2)}) %all-to-all-start.2) | async-done | bytes 786464 | tf_op jit(solution)/shard_map/all_to_all | solution.py:37
  72.5 1.5 %collective-permute-start.10 = (bf16[96,128]{1,0:T(8,128)(2,1)S(1)}, bf16[96,128]{1,0:T(8,128)(2,1)S(1)}, u32[]{:S(2)}, u32[]{:S(2)}) collective-permute-start(bf16[96,128]{1,0:T(8,128)(2,1)S(1)} %reduce_sum.12.refs_0_), channel_id=1, source_target_pairs={{0,32},{16,48},{32,0},{48,16},{1,33},{17,49},{33,1},{49,17},{2,34}... | collective-permute-start | bytes 73736 | tf_op jit(solution)/shard_map/ppermute | solution.py:29
  74.0 3.7 %collective-permute-done.10.refs_1_ = bf16[96,128]{1,0:T(8,128)(2,1)S(1)} collective-permute-done((bf16[96,128]{1,0:T(8,128)(2,1)S(1)}, bf16[96,128]{1,0:T(8,128)(2,1)S(1)}, u32[]{:S(2)}, u32[]{:S(2)}) %collective-permute-start.10) | collective-permute-done | bytes 24608 | tf_op jit(solution)/shard_map/ppermute | solution.py:29
  78.6 4.7 %all-to-all-start.3 = ((bf16[32,96,128]{2,1,0:T(8,128)(2,1)}), bf16[32,96,128]{2,1,0:T(8,128)(2,1)S(1)}, u32[]{:S(2)}, u32[]{:S(2)}) async-start(bf16[32,96,128]{2,1,0:T(8,128)(2,1)} %settle.1), calls=%async_computation.3 | async-start | bytes 1572864 | tf_op jit(solution)/shard_map/all_to_all | solution.py:37
  84.1 1.3 %collective-permute-done.9.refs_1_ = bf16[128,384]{1,0:T(8,128)(2,1)S(1)} collective-permute-done((bf16[128,384]{1,0:T(8,128)(2,1)S(1)}, bf16[128,384]{1,0:T(8,128)(2,1)S(1)}, u32[]{:S(2)}, u32[]{:S(2)}) %collective-permute-start.9) | collective-permute-done | bytes 98336 | tf_op jit(solution)/shard_map/ppermute | solution.py:25
  86.1 9.3 %all-to-all-done.3.source = bf16[32,96,128]{2,1,0:T(8,128)(2,1)S(1)} async-done(((bf16[32,96,128]{2,1,0:T(8,128)(2,1)}), bf16[32,96,128]{2,1,0:T(8,128)(2,1)S(1)}, u32[]{:S(2)}, u32[]{:S(2)}) %all-to-all-start.3) | async-done | bytes 786464 | tf_op jit(solution)/shard_map/all_to_all | solution.py:37
  (42 shorter events, 9.6 us)
Async XLA Ops:
  0.6 2.8 %copy-start.7 = (bf16[64,192]{1,0:T(8,128)(2,1)S(1)}, bf16[64,192]{1,0:T(8,128)(2,1)}, u32[]{:S(2)}) copy-start(bf16[64,192]{1,0:T(8,128)(2,1)} %refs_4_.4) | copy-start | bytes 73732
  0.6 16.5 %collective-permute-start.2 = (bf16[64,192]{1,0:T(8,128)(2,1)}, bf16[64,192]{1,0:T(8,128)(2,1)S(1)}, u32[]{:S(2)}, u32[]{:S(2)}) collective-permute-start(bf16[64,192]{1,0:T(8,128)(2,1)} %refs_4_.4), channel_id=1, source_target_pairs={{0,1},{1,0},{2,3},{3,2},{4,5},{5,4},{6,7},{7,6},{8,9},{9,8},{10,11... | collective-permute-start | bytes 73736 | tf_op jit(solution)/shard_map/ppermute | solution.py:25
  0.7 25.9 %copy-start.4 = (bf16[192,384]{1,0:T(8,128)(2,1)S(1)}, bf16[192,384]{1,0:T(8,128)(2,1)}, u32[]{:S(2)}) copy-start(bf16[192,384]{1,0:T(8,128)(2,1)} %refs_9_.1) | copy-start | bytes 442372
  3.4 13.7 %collective-permute-start.1 = (bf16[64,192]{1,0:T(8,128)(2,1)S(1)}, bf16[64,192]{1,0:T(8,128)(2,1)S(1)}, u32[]{:S(2)}, u32[]{:S(2)}) collective-permute-start(bf16[64,192]{1,0:T(8,128)(2,1)S(1)} %copy-done.7), channel_id=1, source_target_pairs={{0,2},{2,0},{1,3},{3,1},{4,6},{6,4},{5,7},{7,5},{8,10},{10,8},{9,1... | collective-permute-start | bytes 73736 | tf_op jit(solution)/shard_map/ppermute | solution.py:25
  10.7 4.8 %collective-permute-start = (bf16[32,256]{1,0:T(8,128)(2,1)}, bf16[32,256]{1,0:T(8,128)(2,1)S(1)}, u32[]{:S(2)}, u32[]{:S(2)}) collective-permute-start(bf16[32,256]{1,0:T(8,128)(2,1)} %get-tuple-element.41), channel_id=1, source_target_pairs={{0,32},{16,48},{32,0},{48,16},{1,33},{17,49},{33,1},{49,17},{2,34}... | collective-permute-start | bytes 49160 | tf_op jit(solution)/shard_map/ppermute | solution.py:29
  16.2 10.4 %copy-start.2 = (bf16[192,768]{1,0:T(8,128)(2,1)S(1)}, bf16[192,768]{1,0:T(8,128)(2,1)}, u32[]{:S(2)}) copy-start(bf16[192,768]{1,0:T(8,128)(2,1)} %refs_5_.1) | copy-start | bytes 884740
  16.2 10.4 %copy-start.3 = (bf16[256,384]{1,0:T(8,128)(2,1)S(1)}, bf16[256,384]{1,0:T(8,128)(2,1)}, u32[]{:S(2)}) copy-start(bf16[256,384]{1,0:T(8,128)(2,1)} %get-tuple-element.46.refs_1_.refs_6_) | copy-start | bytes 589828
  17.1 9.6 %copy-start = (bf16[3,192,384]{2,1,0:T(8,128)(2,1)S(1)}, bf16[3,192,384]{2,1,0:T(8,128)(2,1)}, u32[]{:S(2)}) copy-start(bf16[3,192,384]{2,1,0:T(8,128)(2,1)} %refs_3_.9) | copy-start | bytes 1327108
  17.1 9.6 %copy-start.1 = (bf16[256,384]{1,0:T(8,128)(2,1)S(1)}, bf16[256,384]{1,0:T(8,128)(2,1)}, u32[]{:S(2)}) copy-start(bf16[256,384]{1,0:T(8,128)(2,1)} %get-tuple-element.45.refs_0_.refs_2_) | copy-start | bytes 589828
  17.1 9.6 %copy-start.9 = (bf16[4,192]{1,0:T(4,128)(2,1)S(1)}, bf16[4,192]{1,0:T(4,128)(2,1)}, u32[]{:S(2)}) copy-start(bf16[4,192]{1,0:T(4,128)(2,1)} %refs_3_.7) | copy-start | bytes 4612
  17.1 17.0 %all-to-all-start = ((bf16[32,16,384]{2,1,0:T(8,128)(2,1)}), bf16[32,16,384]{2,1,0:T(8,128)(2,1)S(1)}, u32[]{:S(2)}, u32[]{:S(2)}) async-start(bf16[32,16,384]{2,1,0:T(8,128)(2,1)} %copy_pair.1), calls=%async_computation | async-start | bytes 786432 | tf_op jit(solution)/shard_map/all_to_all | solution.py:37
  25.3 1.3 %collective-permute-start.3 = (bf16[64,192]{1,0:T(8,128)(2,1)S(1)}, bf16[64,192]{1,0:T(8,128)(2,1)S(1)}, u32[]{:S(2)}, u32[]{:S(2)}) collective-permute-start(bf16[64,192]{1,0:T(8,128)(2,1)S(1)} %collective-permute-done.1.refs_6_), channel_id=1, source_target_pairs={{0,1},{1,0},{2,3},{3,2},{4,5},{5,4},{6,7},{7,6},{8,9},{9,8},{10,11... | collective-permute-start | bytes 73736 | tf_op jit(solution)/shard_map/ppermute | solution.py:25
  27.3 4.0 %collective-permute-start.4 = (bf16[64,256]{1,0:T(8,128)(2,1)S(1)}, bf16[64,256]{1,0:T(8,128)(2,1)S(1)}, u32[]{:S(2)}, u32[]{:S(2)}) collective-permute-start(bf16[64,256]{1,0:T(8,128)(2,1)S(1)} %get-tuple-element.50), channel_id=1, source_target_pairs={{0,16},{16,0},{32,48},{48,32},{1,17},{17,1},{33,49},{49,33},{2,18}... | collective-permute-start | bytes 98312 | tf_op jit(solution)/shard_map/ppermute | solution.py:29
  35.9 14.5 %all-to-all-start.1 = ((bf16[32,16,384]{2,1,0:T(8,128)(2,1)}), bf16[32,16,384]{2,1,0:T(8,128)(2,1)S(1)}, u32[]{:S(2)}, u32[]{:S(2)}) async-start(bf16[32,16,384]{2,1,0:T(8,128)(2,1)} %get-tuple-element.51), calls=%async_computation.1 | async-start | bytes 786432 | tf_op jit(solution)/shard_map/all_to_all | solution.py:37
  41.4 10.6 %collective-permute-start.6 = (bf16[64,256]{1,0:T(8,128)(2,1)S(1)}, bf16[64,256]{1,0:T(8,128)(2,1)S(1)}, u32[]{:S(2)}, u32[]{:S(2)}) collective-permute-start(bf16[64,256]{1,0:T(8,128)(2,1)S(1)} %get-tuple-element.55), channel_id=1, source_target_pairs={{0,16},{16,0},{32,48},{48,32},{1,17},{17,1},{33,49},{49,33},{2,18}... | collective-permute-start | bytes 98312 | tf_op jit(solution)/shard_map/ppermute | solution.py:29
  50.5 4.7 %collective-permute-start.5 = (bf16[32,256]{1,0:T(8,128)(2,1)S(1)}, bf16[32,256]{1,0:T(8,128)(2,1)S(1)}, u32[]{:S(2)}, u32[]{:S(2)}) collective-permute-start(bf16[32,256]{1,0:T(8,128)(2,1)S(1)} %get-tuple-element.53), channel_id=1, source_target_pairs={{0,32},{16,48},{32,0},{48,16},{1,33},{17,49},{33,1},{49,17},{2,34}... | collective-permute-start | bytes 49160 | tf_op jit(solution)/shard_map/ppermute | solution.py:29
  52.1 3.2 %copy-start.5 = (bf16[16,192]{1,0:T(8,128)(2,1)S(1)}, bf16[16,192]{1,0:T(8,128)(2,1)}, u32[]{:S(2)}) copy-start(bf16[16,192]{1,0:T(8,128)(2,1)} %refs_3_.8) | copy-start | bytes 18436
  52.1 3.2 %copy-start.6 = (bf16[16,192]{1,0:T(8,128)(2,1)S(1)}, bf16[16,192]{1,0:T(8,128)(2,1)}, u32[]{:S(2)}) copy-start(bf16[16,192]{1,0:T(8,128)(2,1)} %refs_4_.5) | copy-start | bytes 18436
  56.6 15.8 %all-to-all-start.2 = ((bf16[32,96,128]{2,1,0:T(8,128)(2,1)}), bf16[32,96,128]{2,1,0:T(8,128)(2,1)S(1)}, u32[]{:S(2)}, u32[]{:S(2)}) async-start(bf16[32,96,128]{2,1,0:T(8,128)(2,1)} %get-tuple-element.58), calls=%async_computation.2 | async-start | bytes 1572864 | tf_op jit(solution)/shard_map/all_to_all | solution.py:37
  62.7 1.5 %collective-permute-start.7 = (bf16[192,384]{1,0:T(8,128)(2,1)S(1)}, bf16[192,384]{1,0:T(8,128)(2,1)S(1)}, u32[]{:S(2)}, u32[]{:S(2)}) collective-permute-start(bf16[192,384]{1,0:T(8,128)(2,1)S(1)} %get-tuple-element.65), channel_id=1, source_target_pairs={{0,1},{1,0},{2,3},{3,2},{4,5},{5,4},{6,7},{7,6},{8,9},{9,8},{10,11... | collective-permute-start | bytes 442376 | tf_op jit(solution)/shard_map/ppermute | solution.py:25
  64.3 19.0 %collective-permute-start.8 = (bf16[160,384]{1,0:T(8,128)(2,1)S(1)}, bf16[160,384]{1,0:T(8,128)(2,1)S(1)}, u32[]{:S(2)}, u32[]{:S(2)}) collective-permute-start(bf16[160,384]{1,0:T(8,128)(2,1)S(1)} %get-tuple-element.68), channel_id=1, source_target_pairs={{0,2},{2,0},{1,3},{3,1},{4,6},{6,4},{5,7},{7,5},{8,10},{10,8},{9,1... | collective-permute-start | bytes 368648 | tf_op jit(solution)/shard_map/ppermute | solution.py:25
  72.5 5.2 %collective-permute-start.10 = (bf16[96,128]{1,0:T(8,128)(2,1)S(1)}, bf16[96,128]{1,0:T(8,128)(2,1)S(1)}, u32[]{:S(2)}, u32[]{:S(2)}) collective-permute-start(bf16[96,128]{1,0:T(8,128)(2,1)S(1)} %reduce_sum.12.refs_0_), channel_id=1, source_target_pairs={{0,32},{16,48},{32,0},{48,16},{1,33},{17,49},{33,1},{49,17},{2,34}... | collective-permute-start | bytes 73736 | tf_op jit(solution)/shard_map/ppermute | solution.py:29
  78.6 16.7 %all-to-all-start.3 = ((bf16[32,96,128]{2,1,0:T(8,128)(2,1)}), bf16[32,96,128]{2,1,0:T(8,128)(2,1)S(1)}, u32[]{:S(2)}, u32[]{:S(2)}) async-start(bf16[32,96,128]{2,1,0:T(8,128)(2,1)} %settle.1), calls=%async_computation.3 | async-start | bytes 1572864 | tf_op jit(solution)/shard_map/all_to_all | solution.py:37
  84.0 1.3 %collective-permute-start.9 = (bf16[128,384]{1,0:T(8,128)(2,1)S(1)}, bf16[128,384]{1,0:T(8,128)(2,1)S(1)}, u32[]{:S(2)}, u32[]{:S(2)}) collective-permute-start(bf16[128,384]{1,0:T(8,128)(2,1)S(1)} %get-tuple-element.72.refs_0_), channel_id=1, source_target_pairs={{0,1},{1,0},{2,3},{3,2},{4,5},{5,4},{6,7},{7,6},{8,9},{9,8},{10,11... | collective-permute-start | bytes 294920 | tf_op jit(solution)/shard_map/ppermute | solution.py:25
  (2 other events, 1.4 us)

commit v5 on v4

--- a/solution.py
+++ b/solution.py
@@ -288,7 +288,7 @@
     pieces = cut(dot_tn(d_queries, normed)) + cut(dot_tn(attended, held_cotangent))
     natural = dot_nn(selector(64, query_of, True), attended).astype(BF16)
     head_part = dot_nn(natural, proj_weight).astype(BF16)
-    return jnp.stack(pieces).astype(BF16), d_queries, head_part
+    return jnp.stack(pieces).astype(BF16).reshape(18, 96, 128), d_queries, head_part
 
 
 def tile_grads(own, other, key_pool, value_pool):
@@ -301,12 +301,38 @@
     return d_keys, d_values
 
 
-def weights(own, other, normed, key_pool, value_pool, pieces):
-    d_keys, d_values = tile_grads(own, other, key_pool, value_pool)
-    more = jnp.stack(cut(dot_tn(d_keys, normed)) + cut(dot_tn(d_values, normed))).astype(BF16)
-    blank = jnp.zeros((1, 192, 128), BF16)
-    pieces = jnp.concatenate([pieces, more, blank], axis=0).reshape(32, 96, 128)
-    return pieces, d_keys, d_values
+def weights(own_grad, other_grad, normed, key_pool, value_pool, pieces):
+    def kernel(own, other, held, key_taps, value_taps, ready, out, d_keys, d_values, room, semaphores):
+        first = pltpu.make_async_copy(ready, out.at[pl.ds(0, 18)], semaphores.at[0])
+        first.start()
+        d_keys[...], d_values[...] = tile_grads(
+            own[...], other[...], key_taps[...], value_taps[...]
+        )
+        more = cut(dot_tn(d_keys[...], held[...])) + cut(dot_tn(d_values[...], held[...]))
+        for i, piece in enumerate(more):
+            room[2 * i] = piece[:96].astype(BF16)
+            room[2 * i + 1] = piece[96:].astype(BF16)
+        room[12] = jnp.zeros((96, 128), BF16)
+        room[13] = jnp.zeros((96, 128), BF16)
+        second = pltpu.make_async_copy(room, out.at[pl.ds(18, 14)], semaphores.at[1])
+        second.start()
+        first.wait()
+        second.wait()
+
+    vmem = pl.BlockSpec(memory_space=pltpu.VMEM)
+    return pl.pallas_call(
+        kernel,
+        out_shape=[
+            jax.ShapeDtypeStruct((32, 96, 128), BF16),
+            jax.ShapeDtypeStruct((256, 192), BF16),
+            jax.ShapeDtypeStruct((256, 192), BF16),
+        ],
+        in_specs=[vmem] * 6,
+        out_specs=[pl.BlockSpec(memory_space=pl.ANY), vmem, vmem],
+        scratch_shapes=[pltpu.VMEM((14, 96, 128), BF16), pltpu.SemaphoreType.DMA((2,))],
+        compiler_params=pltpu.CompilerParams(vmem_limit_bytes=32 * 1024 * 1024),
+        name="weights",
+    )(own_grad, other_grad, normed, key_pool, value_pool, pieces)
 
 
 def spread(d_keys, d_values, d_queries, qkv_weight, d_pooled, head_part, held, ln_gain):
@@ -479,12 +505,12 @@
     own_grad, other_grad = fuse(pair_sum, [((32, 256), BF16)] * 2, "pair_sum")(arrived)
     other_grad = swap_z(other_grad, 2)
     pieces, d_queries, head_part = fuse(
-        after, [((9, 192, 128), BF16), ((256, 192), BF16), ((64, 768), BF16)], "after"
+        after, [((18, 96, 128), BF16), ((256, 192), BF16), ((64, 768), BF16)], "after"
     )(mixed, swap_z(returned, 1), normed, query_pool, held_cotangent, proj_weight)
 
-    pieces, d_keys, d_values = fuse(
-        weights, [((32, 96, 128), BF16)] + [((256, 192), BF16)] * 2, "weights"
-    )(own_grad, other_grad, normed, key_pool, value_pool, pieces)
+    pieces, d_keys, d_values = weights(
+        own_grad, other_grad, normed, key_pool, value_pool, pieces
+    )
     arrived = exchange_pairs(pieces)
     kept, sent = fuse(spread, [((192, 384), BF16)] * 2, "spread")(
         d_keys, d_values, d_queries, qkv_weight, d_pooled, head_part, held, ln_gain
@@ -493,11 +519,12 @@
     both, sent, staying = fuse(
         mix, [((128, 384), BF16), ((160, 384), BF16), ((64, 192), F32)], "mix"
     )(kept, swap(sent, "core"))
+
+    reduced = jnp.sum(arrived.astype(F32), axis=0).astype(BF16)
+    other_sums = swap_z(reduced, 2)
+    other_sums, both, sent = lax.optimization_barrier((other_sums, both, sent))
     taken = swap(sent, "half")
-
-    reduced = jnp.sum(arrived.astype(F32), axis=0).astype(BF16)
-    reduced, both = lax.optimization_barrier((reduced, both))
-    (copies,) = fuse(settle, [((32, 96, 128), BF16)], "settle")(reduced, swap_z(reduced, 2))
+    (copies,) = fuse(settle, [((32, 96, 128), BF16)], "settle")(reduced, other_sums)
     qkv_grad, proj_grad = finish(exchange_pairs(copies))
 
     own_rows, block_out = fuse(back, [((128, 384), BF16), ((64, 192), BF16)], "back", flops=20 * 10**9)(

time: 97.1 us -> 96.9 us (level)
    all_to_all x4, waiting for transfers between devices: 26.1 us -> 24.1 us  [exchange_pairs(): lax.all_to_all(blocks, TILE, 0, 0, tiled=True, axis_index_groups=groups)]
    ppermute x6, waiting for transfers between devices: 3.86 us -> 5.85 us  [swap(): return lax.ppermute(block, axis, [(0, 1), (1, 0)])]
    pallas_call x12 -> x11, Pallas kernels: 11.1 us -> 9.8 us  [call(): pl.pallas_call(kernel, out_shape=[jax.ShapeDtypeStruct(shape, dtype) for...]
    pallas_call x0 -> x1, Pallas kernels: none -> 1.15 us  [weights(): pl.pallas_call(kernel, out_shape=[jax.ShapeDtypeStruct((32, 96, 128), BF1...]
where the time goes in v5:
time: 96.9 us; the launch traced here: 96.3 us
  waiting for transfers between devices  41.2 us (43%)
  starting transfers between devices  40.6 us (42%)
  Pallas kernels  12.1 us (12%)
  local copies, waits for them, and re-layouts  1.43 us (1%)
    all_to_all x4, waiting for transfers between devices, exchange_pairs(): lax.all_to_all(blocks, TILE, 0, 0, tiled=True, axis_index_groups=groups)  24.1 us
    all_to_all x4, starting transfers between devices, exchange_pairs(): lax.all_to_all(blocks, TILE, 0, 0, tiled=True, axis_index_groups=groups)  23.6 us
    ppermute x5, waiting for transfers between devices, swap_z(): return lax.ppermute(block, 'z', [(i, i ^ bit) for i in range(4)])  11.3 us
    pallas_call x11, Pallas kernels, call(): pl.pallas_call(kernel, out_shape=[jax.ShapeDtypeStruct(shape, dtype) for...  9.8 us
    ppermute x6, starting transfers between devices, swap(): return lax.ppermute(block, axis, [(0, 1), (1, 0)])  9.07 us
    ppermute x5, starting transfers between devices, swap_z(): return lax.ppermute(block, 'z', [(i, i ^ bit) for i in range(4)])  7.91 us
    ppermute x6, waiting for transfers between devices, swap(): return lax.ppermute(block, axis, [(0, 1), (1, 0)])  5.85 us
  transfers between devices with their start and end apart: 15, of which 11 were waited for; matrix products, arithmetic and copies ran while one was open for 0% of the time, Pallas kernels for 8%

profile of v5, /device:TPU:2, one launch (start us, length us, event | category | flops | bytes accessed | tf_op | source)
XLA Modules:
  0.0 96.3 jit_solution(9305893342391667337)
XLA Ops:
  0.8 2.6 %front.1 = (bf16[32,256]{1,0:T(8,128)(2,1)}, bf16[32,256]{1,0:T(8,128)(2,1)}, bf16[256,384]{1,0:T(8,128)(2,1)}, bf16[256,384]{1,0:T(8,128)(2,1)}) custom-call(bf16[256,384]{1,0:T(8,128)(2,1)} %refs_0_.1, f32[384]{0:T(512)} %refs_7_.1, bf16[3,192,384]{2,1,0:T(8,128)(2,1)} %refs_3_.7, bf16[16,192]{1,0:T(8,128)(2,1)} %key_taps.1, bf16[16,192]{1,0:T(8,128)(2,1)} %value_taps.1), custom_call_target="tpu_custom_call" | custom-call | tf_op jit(solution)/shard_map/front/pallas_call | solution.py:74
  3.4 7.3 %collective-permute-start.1 = (bf16[64,192]{1,0:T(8,128)(2,1)S(1)}, bf16[64,192]{1,0:T(8,128)(2,1)S(1)}, u32[]{:S(2)}, u32[]{:S(2)}) collective-permute-start(bf16[64,192]{1,0:T(8,128)(2,1)S(1)} %copy-done.7), channel_id=1, source_target_pairs={{0,2},{2,0},{1,3},{3,1},{4,6},{6,4},{5,7},{7,5},{8,10},{10,8},{9,1... | collective-permute-start | bytes 73736 | tf_op jit(solution)/shard_map/ppermute | solution.py:25
  10.7 1.5 %collective-permute-start = (bf16[32,256]{1,0:T(8,128)(2,1)}, bf16[32,256]{1,0:T(8,128)(2,1)S(1)}, u32[]{:S(2)}, u32[]{:S(2)}) collective-permute-start(bf16[32,256]{1,0:T(8,128)(2,1)} %get-tuple-element.42), channel_id=1, source_target_pairs={{0,32},{16,48},{32,0},{48,16},{1,33},{17,49},{33,1},{49,17},{2,34}... | collective-permute-start | bytes 49160 | tf_op jit(solution)/shard_map/ppermute | solution.py:29
  12.1 3.4 %collective-permute-done.refs_1_ = bf16[32,256]{1,0:T(8,128)(2,1)S(1)} collective-permute-done((bf16[32,256]{1,0:T(8,128)(2,1)}, bf16[32,256]{1,0:T(8,128)(2,1)S(1)}, u32[]{:S(2)}, u32[]{:S(2)}) %collective-permute-start) | collective-permute-done | bytes 16416 | tf_op jit(solution)/shard_map/ppermute | solution.py:29
  17.1 8.2 %all-to-all-start = ((bf16[32,16,384]{2,1,0:T(8,128)(2,1)}), bf16[32,16,384]{2,1,0:T(8,128)(2,1)S(1)}, u32[]{:S(2)}, u32[]{:S(2)}) async-start(bf16[32,16,384]{2,1,0:T(8,128)(2,1)} %copy_pair.1), calls=%async_computation | async-start | bytes 786432 | tf_op jit(solution)/shard_map/all_to_all | solution.py:37
  25.4 1.2 %collective-permute-done.3.refs_7_ = bf16[64,192]{1,0:T(8,128)(2,1)S(1)} collective-permute-done((bf16[64,192]{1,0:T(8,128)(2,1)S(1)}, bf16[64,192]{1,0:T(8,128)(2,1)S(1)}, u32[]{:S(2)}, u32[]{:S(2)}) %collective-permute-start.3) | collective-permute-done | bytes 24608 | tf_op jit(solution)/shard_map/ppermute | solution.py:25
  27.3 1.6 %collective-permute-start.4 = (bf16[64,256]{1,0:T(8,128)(2,1)S(1)}, bf16[64,256]{1,0:T(8,128)(2,1)S(1)}, u32[]{:S(2)}, u32[]{:S(2)}) collective-permute-start(bf16[64,256]{1,0:T(8,128)(2,1)S(1)} %get-tuple-element.51), channel_id=1, source_target_pairs={{0,16},{16,0},{32,48},{48,32},{1,17},{17,1},{33,49},{49,33},{2,18}... | collective-permute-start | bytes 98312 | tf_op jit(solution)/shard_map/ppermute | solution.py:29
  28.9 2.4 %collective-permute-done.4.refs_2_ = bf16[64,256]{1,0:T(8,128)(2,1)S(1)} collective-permute-done((bf16[64,256]{1,0:T(8,128)(2,1)S(1)}, bf16[64,256]{1,0:T(8,128)(2,1)S(1)}, u32[]{:S(2)}, u32[]{:S(2)}) %collective-permute-start.4) | collective-permute-done | bytes 32800 | tf_op jit(solution)/shard_map/ppermute | solution.py:29
  31.3 2.8 %all-to-all-done.refs_0_ = bf16[32,16,384]{2,1,0:T(8,128)(2,1)S(1)} async-done(((bf16[32,16,384]{2,1,0:T(8,128)(2,1)}), bf16[32,16,384]{2,1,0:T(8,128)(2,1)S(1)}, u32[]{:S(2)}, u32[]{:S(2)}) %all-to-all-start) | async-done | bytes 393248 | tf_op jit(solution)/shard_map/all_to_all | solution.py:37
  34.2 1.8 %attend.1 = (bf16[32,16,384]{2,1,0:T(8,128)(2,1)}, f32[64,256]{1,0:T(8,128)S(1)}, bf16[64,256]{1,0:T(8,128)(2,1)S(1)}) custom-call(bf16[32,16,384]{2,1,0:T(8,128)(2,1)S(1)} %all-to-all-done.refs_0_, bf16[64,256]{1,0:T(8,128)(2,1)S(1)} %get-tuple-element.50.refs_1_, bf16[64,256]{1,0:T(8,128)(2,1)S(1)} %collective-permute-done.4.refs_2_), custom_call_target="tpu_custom_call" | custom-call | tf_op jit(solution)/shard_map/attend/pallas_call | solution.py:74
  35.9 5.5 %all-to-all-start.1 = ((bf16[32,16,384]{2,1,0:T(8,128)(2,1)}), bf16[32,16,384]{2,1,0:T(8,128)(2,1)S(1)}, u32[]{:S(2)}, u32[]{:S(2)}) async-start(bf16[32,16,384]{2,1,0:T(8,128)(2,1)} %get-tuple-element.52), calls=%async_computation.1 | async-start | bytes 786432 | tf_op jit(solution)/shard_map/all_to_all | solution.py:37
  41.4 1.6 %collective-permute-start.6 = (bf16[64,256]{1,0:T(8,128)(2,1)S(1)}, bf16[64,256]{1,0:T(8,128)(2,1)S(1)}, u32[]{:S(2)}, u32[]{:S(2)}) collective-permute-start(bf16[64,256]{1,0:T(8,128)(2,1)S(1)} %get-tuple-element.56), channel_id=1, source_target_pairs={{0,16},{16,0},{32,48},{48,32},{1,17},{17,1},{33,49},{49,33},{2,18}... | collective-permute-start | bytes 98312 | tf_op jit(solution)/shard_map/ppermute | solution.py:29
  43.0 7.4 %all-to-all-done.1.refs_0_ = bf16[32,16,384]{2,1,0:T(8,128)(2,1)S(1)} async-done(((bf16[32,16,384]{2,1,0:T(8,128)(2,1)}), bf16[32,16,384]{2,1,0:T(8,128)(2,1)S(1)}, u32[]{:S(2)}, u32[]{:S(2)}) %all-to-all-start.1) | async-done | bytes 393248 | tf_op jit(solution)/shard_map/all_to_all | solution.py:37
  50.5 1.5 %collective-permute-start.5 = (bf16[32,256]{1,0:T(8,128)(2,1)S(1)}, bf16[32,256]{1,0:T(8,128)(2,1)S(1)}, u32[]{:S(2)}, u32[]{:S(2)}) collective-permute-start(bf16[32,256]{1,0:T(8,128)(2,1)S(1)} %get-tuple-element.54), channel_id=1, source_target_pairs={{0,32},{16,48},{32,0},{48,16},{1,33},{17,49},{33,1},{49,17},{2,34}... | collective-permute-start | bytes 49160 | tf_op jit(solution)/shard_map/ppermute | solution.py:29
  52.7 2.6 %collective-permute-done.5.other = bf16[32,256]{1,0:T(8,128)(2,1)S(1)} collective-permute-done((bf16[32,256]{1,0:T(8,128)(2,1)S(1)}, bf16[32,256]{1,0:T(8,128)(2,1)S(1)}, u32[]{:S(2)}, u32[]{:S(2)}) %collective-permute-start.5) | collective-permute-done | bytes 16416 | tf_op jit(solution)/shard_map/ppermute | solution.py:29
  56.4 4.8 %all-to-all-start.2 = ((bf16[32,96,128]{2,1,0:T(8,128)(2,1)}), bf16[32,96,128]{2,1,0:T(8,128)(2,1)S(1)}, u32[]{:S(2)}, u32[]{:S(2)}) async-start(bf16[32,96,128]{2,1,0:T(8,128)(2,1)} %get-tuple-element.59), calls=%async_computation.2 | async-start | bytes 1572864 | tf_op jit(solution)/shard_map/all_to_all | solution.py:37
  62.6 9.2 %all-to-all-done.2 = bf16[32,96,128]{2,1,0:T(8,128)(2,1)S(1)} async-done(((bf16[32,96,128]{2,1,0:T(8,128)(2,1)}), bf16[32,96,128]{2,1,0:T(8,128)(2,1)S(1)}, u32[]{:S(2)}, u32[]{:S(2)}) %all-to-all-start.2) | async-done | bytes 786464 | tf_op jit(solution)/shard_map/all_to_all | solution.py:37
  72.0 1.8 %collective-permute-start.7 = (bf16[96,128]{1,0:T(8,128)(2,1)S(1)}, bf16[96,128]{1,0:T(8,128)(2,1)S(1)}, u32[]{:S(2)}, u32[]{:S(2)}) collective-permute-start(bf16[96,128]{1,0:T(8,128)(2,1)S(1)} %reduce_sum.12.refs_0_), channel_id=1, source_target_pairs={{0,32},{16,48},{32,0},{48,16},{1,33},{17,49},{33,1},{49,17},{2,34}... | collective-permute-start | bytes 73736 | tf_op jit(solution)/shard_map/ppermute | solution.py:29
  73.9 2.9 %collective-permute-done.7.refs_1_ = bf16[96,128]{1,0:T(8,128)(2,1)S(1)} collective-permute-done((bf16[96,128]{1,0:T(8,128)(2,1)S(1)}, bf16[96,128]{1,0:T(8,128)(2,1)S(1)}, u32[]{:S(2)}, u32[]{:S(2)}) %collective-permute-start.7) | collective-permute-done | bytes 24608 | tf_op jit(solution)/shard_map/ppermute | solution.py:29
  76.8 1.5 %collective-permute-start.9 = (bf16[160,384]{1,0:T(8,128)(2,1)S(1)}, bf16[160,384]{1,0:T(8,128)(2,1)S(1)}, u32[]{:S(2)}, u32[]{:S(2)}) collective-permute-start(bf16[160,384]{1,0:T(8,128)(2,1)S(1)} %get-tuple-element.70), channel_id=1, source_target_pairs={{0,2},{2,0},{1,3},{3,1},{4,6},{6,4},{5,7},{7,5},{8,10},{10,8},{9,1... | collective-permute-start | bytes 368648 | tf_op jit(solution)/shard_map/ppermute | solution.py:25
  79.3 5.2 %all-to-all-start.3 = ((bf16[32,96,128]{2,1,0:T(8,128)(2,1)}), bf16[32,96,128]{2,1,0:T(8,128)(2,1)S(1)}, u32[]{:S(2)}, u32[]{:S(2)}) async-start(bf16[32,96,128]{2,1,0:T(8,128)(2,1)} %settle.1), calls=%async_computation.3 | async-start | bytes 1572864 | tf_op jit(solution)/shard_map/all_to_all | solution.py:37
  84.4 3.3 %collective-permute-done.9.refs_1_ = bf16[160,384]{1,0:T(8,128)(2,1)S(1)} collective-permute-done((bf16[160,384]{1,0:T(8,128)(2,1)S(1)}, bf16[160,384]{1,0:T(8,128)(2,1)S(1)}, u32[]{:S(2)}, u32[]{:S(2)}) %collective-permute-start.9) | collective-permute-done | bytes 122912 | tf_op jit(solution)/shard_map/ppermute | solution.py:25
  88.5 1.3 %collective-permute-done.10.refs_1_ = bf16[128,384]{1,0:T(8,128)(2,1)S(1)} collective-permute-done((bf16[128,384]{1,0:T(8,128)(2,1)S(1)}, bf16[128,384]{1,0:T(8,128)(2,1)S(1)}, u32[]{:S(2)}, u32[]{:S(2)}) %collective-permute-start.10) | collective-permute-done | bytes 98336 | tf_op jit(solution)/shard_map/ppermute | solution.py:25
  90.5 4.6 %all-to-all-done.3.source = bf16[32,96,128]{2,1,0:T(8,128)(2,1)S(1)} async-done(((bf16[32,96,128]{2,1,0:T(8,128)(2,1)}), bf16[32,96,128]{2,1,0:T(8,128)(2,1)S(1)}, u32[]{:S(2)}, u32[]{:S(2)}) %all-to-all-start.3) | async-done | bytes 786464 | tf_op jit(solution)/shard_map/all_to_all | solution.py:37
  (42 shorter events, 9.5 us)
Async XLA Ops:
  0.6 2.8 %copy-start.7 = (bf16[64,192]{1,0:T(8,128)(2,1)S(1)}, bf16[64,192]{1,0:T(8,128)(2,1)}, u32[]{:S(2)}) copy-start(bf16[64,192]{1,0:T(8,128)(2,1)} %refs_4_.3) | copy-start | bytes 73732
  0.6 16.5 %collective-permute-start.2 = (bf16[64,192]{1,0:T(8,128)(2,1)}, bf16[64,192]{1,0:T(8,128)(2,1)S(1)}, u32[]{:S(2)}, u32[]{:S(2)}) collective-permute-start(bf16[64,192]{1,0:T(8,128)(2,1)} %refs_4_.3), channel_id=1, source_target_pairs={{0,1},{1,0},{2,3},{3,2},{4,5},{5,4},{6,7},{7,6},{8,9},{9,8},{10,11... | collective-permute-start | bytes 73736 | tf_op jit(solution)/shard_map/ppermute | solution.py:25
  0.7 25.9 %copy-start.4 = (bf16[192,384]{1,0:T(8,128)(2,1)S(1)}, bf16[192,384]{1,0:T(8,128)(2,1)}, u32[]{:S(2)}) copy-start(bf16[192,384]{1,0:T(8,128)(2,1)} %refs_9_.1) | copy-start | bytes 442372
  3.4 13.7 %collective-permute-start.1 = (bf16[64,192]{1,0:T(8,128)(2,1)S(1)}, bf16[64,192]{1,0:T(8,128)(2,1)S(1)}, u32[]{:S(2)}, u32[]{:S(2)}) collective-permute-start(bf16[64,192]{1,0:T(8,128)(2,1)S(1)} %copy-done.7), channel_id=1, source_target_pairs={{0,2},{2,0},{1,3},{3,1},{4,6},{6,4},{5,7},{7,5},{8,10},{10,8},{9,1... | collective-permute-start | bytes 73736 | tf_op jit(solution)/shard_map/ppermute | solution.py:25
  10.7 4.8 %collective-permute-start = (bf16[32,256]{1,0:T(8,128)(2,1)}, bf16[32,256]{1,0:T(8,128)(2,1)S(1)}, u32[]{:S(2)}, u32[]{:S(2)}) collective-permute-start(bf16[32,256]{1,0:T(8,128)(2,1)} %get-tuple-element.42), channel_id=1, source_target_pairs={{0,32},{16,48},{32,0},{48,16},{1,33},{17,49},{33,1},{49,17},{2,34}... | collective-permute-start | bytes 49160 | tf_op jit(solution)/shard_map/ppermute | solution.py:29
  16.2 10.4 %copy-start.2 = (bf16[192,768]{1,0:T(8,128)(2,1)S(1)}, bf16[192,768]{1,0:T(8,128)(2,1)}, u32[]{:S(2)}) copy-start(bf16[192,768]{1,0:T(8,128)(2,1)} %refs_5_.1) | copy-start | bytes 884740
  16.2 10.4 %copy-start.3 = (bf16[256,384]{1,0:T(8,128)(2,1)S(1)}, bf16[256,384]{1,0:T(8,128)(2,1)}, u32[]{:S(2)}) copy-start(bf16[256,384]{1,0:T(8,128)(2,1)} %get-tuple-element.47.refs_1_.refs_6_) | copy-start | bytes 589828
  17.1 9.6 %copy-start = (bf16[3,192,384]{2,1,0:T(8,128)(2,1)S(1)}, bf16[3,192,384]{2,1,0:T(8,128)(2,1)}, u32[]{:S(2)}) copy-start(bf16[3,192,384]{2,1,0:T(8,128)(2,1)} %refs_3_.7) | copy-start | bytes 1327108
  17.1 9.6 %copy-start.1 = (bf16[256,384]{1,0:T(8,128)(2,1)S(1)}, bf16[256,384]{1,0:T(8,128)(2,1)}, u32[]{:S(2)}) copy-start(bf16[256,384]{1,0:T(8,128)(2,1)} %get-tuple-element.46.refs_0_.refs_2_.held) | copy-start | bytes 589828
  17.1 9.6 %copy-start.9 = (bf16[4,192]{1,0:T(4,128)(2,1)S(1)}, bf16[4,192]{1,0:T(4,128)(2,1)}, u32[]{:S(2)}) copy-start(bf16[4,192]{1,0:T(4,128)(2,1)} %refs_3_.6) | copy-start | bytes 4612
  17.1 17.0 %all-to-all-start = ((bf16[32,16,384]{2,1,0:T(8,128)(2,1)}), bf16[32,16,384]{2,1,0:T(8,128)(2,1)S(1)}, u32[]{:S(2)}, u32[]{:S(2)}) async-start(bf16[32,16,384]{2,1,0:T(8,128)(2,1)} %copy_pair.1), calls=%async_computation | async-start | bytes 786432 | tf_op jit(solution)/shard_map/all_to_all | solution.py:37
  25.3 1.3 %collective-permute-start.3 = (bf16[64,192]{1,0:T(8,128)(2,1)S(1)}, bf16[64,192]{1,0:T(8,128)(2,1)S(1)}, u32[]{:S(2)}, u32[]{:S(2)}) collective-permute-start(bf16[64,192]{1,0:T(8,128)(2,1)S(1)} %collective-permute-done.1.refs_6_), channel_id=1, source_target_pairs={{0,1},{1,0},{2,3},{3,2},{4,5},{5,4},{6,7},{7,6},{8,9},{9,8},{10,11... | collective-permute-start | bytes 73736 | tf_op jit(solution)/shard_map/ppermute | solution.py:25
  27.3 4.0 %collective-permute-start.4 = (bf16[64,256]{1,0:T(8,128)(2,1)S(1)}, bf16[64,256]{1,0:T(8,128)(2,1)S(1)}, u32[]{:S(2)}, u32[]{:S(2)}) collective-permute-start(bf16[64,256]{1,0:T(8,128)(2,1)S(1)} %get-tuple-element.51), channel_id=1, source_target_pairs={{0,16},{16,0},{32,48},{48,32},{1,17},{17,1},{33,49},{49,33},{2,18}... | collective-permute-start | bytes 98312 | tf_op jit(solution)/shard_map/ppermute | solution.py:29
  35.9 14.5 %all-to-all-start.1 = ((bf16[32,16,384]{2,1,0:T(8,128)(2,1)}), bf16[32,16,384]{2,1,0:T(8,128)(2,1)S(1)}, u32[]{:S(2)}, u32[]{:S(2)}) async-start(bf16[32,16,384]{2,1,0:T(8,128)(2,1)} %get-tuple-element.52), calls=%async_computation.1 | async-start | bytes 786432 | tf_op jit(solution)/shard_map/all_to_all | solution.py:37
  41.4 10.6 %collective-permute-start.6 = (bf16[64,256]{1,0:T(8,128)(2,1)S(1)}, bf16[64,256]{1,0:T(8,128)(2,1)S(1)}, u32[]{:S(2)}, u32[]{:S(2)}) collective-permute-start(bf16[64,256]{1,0:T(8,128)(2,1)S(1)} %get-tuple-element.56), channel_id=1, source_target_pairs={{0,16},{16,0},{32,48},{48,32},{1,17},{17,1},{33,49},{49,33},{2,18}... | collective-permute-start | bytes 98312 | tf_op jit(solution)/shard_map/ppermute | solution.py:29
  50.5 4.7 %collective-permute-start.5 = (bf16[32,256]{1,0:T(8,128)(2,1)S(1)}, bf16[32,256]{1,0:T(8,128)(2,1)S(1)}, u32[]{:S(2)}, u32[]{:S(2)}) collective-permute-start(bf16[32,256]{1,0:T(8,128)(2,1)S(1)} %get-tuple-element.54), channel_id=1, source_target_pairs={{0,32},{16,48},{32,0},{48,16},{1,33},{17,49},{33,1},{49,17},{2,34}... | collective-permute-start | bytes 49160 | tf_op jit(solution)/shard_map/ppermute | solution.py:29
  52.1 3.2 %copy-start.5 = (bf16[16,192]{1,0:T(8,128)(2,1)S(1)}, bf16[16,192]{1,0:T(8,128)(2,1)}, u32[]{:S(2)}) copy-start(bf16[16,192]{1,0:T(8,128)(2,1)} %key_taps.1) | copy-start | bytes 18436
  52.1 3.2 %copy-start.6 = (bf16[16,192]{1,0:T(8,128)(2,1)S(1)}, bf16[16,192]{1,0:T(8,128)(2,1)}, u32[]{:S(2)}) copy-start(bf16[16,192]{1,0:T(8,128)(2,1)} %value_taps.1) | copy-start | bytes 18436
  56.4 15.5 %all-to-all-start.2 = ((bf16[32,96,128]{2,1,0:T(8,128)(2,1)}), bf16[32,96,128]{2,1,0:T(8,128)(2,1)S(1)}, u32[]{:S(2)}, u32[]{:S(2)}) async-start(bf16[32,96,128]{2,1,0:T(8,128)(2,1)} %get-tuple-element.59), calls=%async_computation.2 | async-start | bytes 1572864 | tf_op jit(solution)/shard_map/all_to_all | solution.py:37
  62.5 11.2 %collective-permute-start.8 = (bf16[192,384]{1,0:T(8,128)(2,1)S(1)}, bf16[192,384]{1,0:T(8,128)(2,1)S(1)}, u32[]{:S(2)}, u32[]{:S(2)}) collective-permute-start(bf16[192,384]{1,0:T(8,128)(2,1)S(1)} %get-tuple-element.66), channel_id=1, source_target_pairs={{0,1},{1,0},{2,3},{3,2},{4,5},{5,4},{6,7},{7,6},{8,9},{9,8},{10,11... | collective-permute-start | bytes 442376 | tf_op jit(solution)/shard_map/ppermute | solution.py:25
  72.0 4.8 %collective-permute-start.7 = (bf16[96,128]{1,0:T(8,128)(2,1)S(1)}, bf16[96,128]{1,0:T(8,128)(2,1)S(1)}, u32[]{:S(2)}, u32[]{:S(2)}) collective-permute-start(bf16[96,128]{1,0:T(8,128)(2,1)S(1)} %reduce_sum.12.refs_0_), channel_id=1, source_target_pairs={{0,32},{16,48},{32,0},{48,16},{1,33},{17,49},{33,1},{49,17},{2,34}... | collective-permute-start | bytes 73736 | tf_op jit(solution)/shard_map/ppermute | solution.py:29
  76.8 11.0 %collective-permute-start.9 = (bf16[160,384]{1,0:T(8,128)(2,1)S(1)}, bf16[160,384]{1,0:T(8,128)(2,1)S(1)}, u32[]{:S(2)}, u32[]{:S(2)}) collective-permute-start(bf16[160,384]{1,0:T(8,128)(2,1)S(1)} %get-tuple-element.70), channel_id=1, source_target_pairs={{0,2},{2,0},{1,3},{3,1},{4,6},{6,4},{5,7},{7,5},{8,10},{10,8},{9,1... | collective-permute-start | bytes 368648 | tf_op jit(solution)/shard_map/ppermute | solution.py:25
  79.3 15.9 %all-to-all-start.3 = ((bf16[32,96,128]{2,1,0:T(8,128)(2,1)}), bf16[32,96,128]{2,1,0:T(8,128)(2,1)S(1)}, u32[]{:S(2)}, u32[]{:S(2)}) async-start(bf16[32,96,128]{2,1,0:T(8,128)(2,1)} %settle.1), calls=%async_computation.3 | async-start | bytes 1572864 | tf_op jit(solution)/shard_map/all_to_all | solution.py:37
  88.5 1.3 %collective-permute-start.10 = (bf16[128,384]{1,0:T(8,128)(2,1)S(1)}, bf16[128,384]{1,0:T(8,128)(2,1)S(1)}, u32[]{:S(2)}, u32[]{:S(2)}) collective-permute-start(bf16[128,384]{1,0:T(8,128)(2,1)S(1)} %get-tuple-element.74.refs_0_), channel_id=1, source_target_pairs={{0,1},{1,0},{2,3},{3,2},{4,5},{5,4},{6,7},{7,6},{8,9},{9,8},{10,11... | collective-permute-start | bytes 294920 | tf_op jit(solution)/shard_map/ppermute | solution.py:25
  (2 other events, 1.4 us)

commit v6 on v5

--- a/solution.py
+++ b/solution.py
@@ -519,12 +519,11 @@
     both, sent, staying = fuse(
         mix, [((128, 384), BF16), ((160, 384), BF16), ((64, 192), F32)], "mix"
     )(kept, swap(sent, "core"))
+    taken = swap(sent, "half")
 
     reduced = jnp.sum(arrived.astype(F32), axis=0).astype(BF16)
-    other_sums = swap_z(reduced, 2)
-    other_sums, both, sent = lax.optimization_barrier((other_sums, both, sent))
-    taken = swap(sent, "half")
-    (copies,) = fuse(settle, [((32, 96, 128), BF16)], "settle")(reduced, other_sums)
+    reduced, both = lax.optimization_barrier((reduced, both))
+    (copies,) = fuse(settle, [((32, 96, 128), BF16)], "settle")(reduced, swap_z(reduced, 2))
     qkv_grad, proj_grad = finish(exchange_pairs(copies))
 
     own_rows, block_out = fuse(back, [((128, 384), BF16), ((64, 192), BF16)], "back", flops=20 * 10**9)(

time: 96.9 us -> 96.9 us (level)
    all_to_all x4, waiting for transfers between devices: 24.1 us -> 26.1 us  [exchange_pairs(): lax.all_to_all(blocks, TILE, 0, 0, tiled=True, axis_index_groups=groups)]
    ppermute x6, waiting for transfers between devices: 5.85 us -> 3.86 us  [swap(): return lax.ppermute(block, axis, [(0, 1), (1, 0)])]
where the time goes in v6:
time: 96.9 us; the launch traced here: 96.4 us
  waiting for transfers between devices  42.1 us (43%)
  starting transfers between devices  39.8 us (41%)
  Pallas kernels  12.1 us (12%)
  local copies, waits for them, and re-layouts  1.43 us (1%)
    all_to_all x4, waiting for transfers between devices, exchange_pairs(): lax.all_to_all(blocks, TILE, 0, 0, tiled=True, axis_index_groups=groups)  26.1 us
    all_to_all x4, starting transfers between devices, exchange_pairs(): lax.all_to_all(blocks, TILE, 0, 0, tiled=True, axis_index_groups=groups)  23.2 us
    ppermute x5, waiting for transfers between devices, swap_z(): return lax.ppermute(block, 'z', [(i, i ^ bit) for i in range(4)])  12.1 us
    pallas_call x11, Pallas kernels, call(): pl.pallas_call(kernel, out_shape=[jax.ShapeDtypeStruct(shape, dtype) for...  9.8 us
    ppermute x6, starting transfers between devices, swap(): return lax.ppermute(block, axis, [(0, 1), (1, 0)])  9.02 us
    ppermute x5, starting transfers between devices, swap_z(): return lax.ppermute(block, 'z', [(i, i ^ bit) for i in range(4)])  7.62 us
    ppermute x6, waiting for transfers between devices, swap(): return lax.ppermute(block, axis, [(0, 1), (1, 0)])  3.86 us
  transfers between devices with their start and end apart: 15, of which 11 were waited for; matrix products, arithmetic and copies ran while one was open for 0% of the time, Pallas kernels for 8%

profile of v6, /device:TPU:2, one launch (start us, length us, event | category | flops | bytes accessed | tf_op | source)
XLA Modules:
  0.0 96.4 jit_solution(5960763914835686468)
XLA Ops:
  0.8 2.6 %front.1 = (bf16[32,256]{1,0:T(8,128)(2,1)}, bf16[32,256]{1,0:T(8,128)(2,1)}, bf16[256,384]{1,0:T(8,128)(2,1)}, bf16[256,384]{1,0:T(8,128)(2,1)}) custom-call(bf16[256,384]{1,0:T(8,128)(2,1)} %refs_0_.1, f32[384]{0:T(512)} %refs_7_.1, bf16[3,192,384]{2,1,0:T(8,128)(2,1)} %refs_3_.7, bf16[16,192]{1,0:T(8,128)(2,1)} %key_taps.1, bf16[16,192]{1,0:T(8,128)(2,1)} %value_taps.1), custom_call_target="tpu_custom_call" | custom-call | tf_op jit(solution)/shard_map/front/pallas_call | solution.py:74
  3.4 7.3 %collective-permute-start.1 = (bf16[64,192]{1,0:T(8,128)(2,1)S(1)}, bf16[64,192]{1,0:T(8,128)(2,1)S(1)}, u32[]{:S(2)}, u32[]{:S(2)}) collective-permute-start(bf16[64,192]{1,0:T(8,128)(2,1)S(1)} %copy-done.7), channel_id=1, source_target_pairs={{0,2},{2,0},{1,3},{3,1},{4,6},{6,4},{5,7},{7,5},{8,10},{10,8},{9,1... | collective-permute-start | bytes 73736 | tf_op jit(solution)/shard_map/ppermute | solution.py:25
  10.7 1.5 %collective-permute-start = (bf16[32,256]{1,0:T(8,128)(2,1)}, bf16[32,256]{1,0:T(8,128)(2,1)S(1)}, u32[]{:S(2)}, u32[]{:S(2)}) collective-permute-start(bf16[32,256]{1,0:T(8,128)(2,1)} %get-tuple-element.41), channel_id=1, source_target_pairs={{0,32},{16,48},{32,0},{48,16},{1,33},{17,49},{33,1},{49,17},{2,34}... | collective-permute-start | bytes 49160 | tf_op jit(solution)/shard_map/ppermute | solution.py:29
  12.1 3.4 %collective-permute-done.refs_1_ = bf16[32,256]{1,0:T(8,128)(2,1)S(1)} collective-permute-done((bf16[32,256]{1,0:T(8,128)(2,1)}, bf16[32,256]{1,0:T(8,128)(2,1)S(1)}, u32[]{:S(2)}, u32[]{:S(2)}) %collective-permute-start) | collective-permute-done | bytes 16416 | tf_op jit(solution)/shard_map/ppermute | solution.py:29
  17.1 8.2 %all-to-all-start = ((bf16[32,16,384]{2,1,0:T(8,128)(2,1)}), bf16[32,16,384]{2,1,0:T(8,128)(2,1)S(1)}, u32[]{:S(2)}, u32[]{:S(2)}) async-start(bf16[32,16,384]{2,1,0:T(8,128)(2,1)} %copy_pair.1), calls=%async_computation | async-start | bytes 786432 | tf_op jit(solution)/shard_map/all_to_all | solution.py:37
  25.4 1.2 %collective-permute-done.3.refs_7_ = bf16[64,192]{1,0:T(8,128)(2,1)S(1)} collective-permute-done((bf16[64,192]{1,0:T(8,128)(2,1)S(1)}, bf16[64,192]{1,0:T(8,128)(2,1)S(1)}, u32[]{:S(2)}, u32[]{:S(2)}) %collective-permute-start.3) | collective-permute-done | bytes 24608 | tf_op jit(solution)/shard_map/ppermute | solution.py:25
  27.3 1.6 %collective-permute-start.4 = (bf16[64,256]{1,0:T(8,128)(2,1)S(1)}, bf16[64,256]{1,0:T(8,128)(2,1)S(1)}, u32[]{:S(2)}, u32[]{:S(2)}) collective-permute-start(bf16[64,256]{1,0:T(8,128)(2,1)S(1)} %get-tuple-element.50), channel_id=1, source_target_pairs={{0,16},{16,0},{32,48},{48,32},{1,17},{17,1},{33,49},{49,33},{2,18}... | collective-permute-start | bytes 98312 | tf_op jit(solution)/shard_map/ppermute | solution.py:29
  28.9 2.4 %collective-permute-done.4.refs_2_ = bf16[64,256]{1,0:T(8,128)(2,1)S(1)} collective-permute-done((bf16[64,256]{1,0:T(8,128)(2,1)S(1)}, bf16[64,256]{1,0:T(8,128)(2,1)S(1)}, u32[]{:S(2)}, u32[]{:S(2)}) %collective-permute-start.4) | collective-permute-done | bytes 32800 | tf_op jit(solution)/shard_map/ppermute | solution.py:29
  31.3 2.8 %all-to-all-done.refs_0_ = bf16[32,16,384]{2,1,0:T(8,128)(2,1)S(1)} async-done(((bf16[32,16,384]{2,1,0:T(8,128)(2,1)}), bf16[32,16,384]{2,1,0:T(8,128)(2,1)S(1)}, u32[]{:S(2)}, u32[]{:S(2)}) %all-to-all-start) | async-done | bytes 393248 | tf_op jit(solution)/shard_map/all_to_all | solution.py:37
  34.2 1.8 %attend.1 = (bf16[32,16,384]{2,1,0:T(8,128)(2,1)}, f32[64,256]{1,0:T(8,128)S(1)}, bf16[64,256]{1,0:T(8,128)(2,1)S(1)}) custom-call(bf16[32,16,384]{2,1,0:T(8,128)(2,1)S(1)} %all-to-all-done.refs_0_, bf16[64,256]{1,0:T(8,128)(2,1)S(1)} %get-tuple-element.49.refs_1_, bf16[64,256]{1,0:T(8,128)(2,1)S(1)} %collective-permute-done.4.refs_2_), custom_call_target="tpu_custom_call" | custom-call | tf_op jit(solution)/shard_map/attend/pallas_call | solution.py:74
  35.9 5.5 %all-to-all-start.1 = ((bf16[32,16,384]{2,1,0:T(8,128)(2,1)}), bf16[32,16,384]{2,1,0:T(8,128)(2,1)S(1)}, u32[]{:S(2)}, u32[]{:S(2)}) async-start(bf16[32,16,384]{2,1,0:T(8,128)(2,1)} %get-tuple-element.51), calls=%async_computation.1 | async-start | bytes 786432 | tf_op jit(solution)/shard_map/all_to_all | solution.py:37
  41.4 1.6 %collective-permute-start.6 = (bf16[64,256]{1,0:T(8,128)(2,1)S(1)}, bf16[64,256]{1,0:T(8,128)(2,1)S(1)}, u32[]{:S(2)}, u32[]{:S(2)}) collective-permute-start(bf16[64,256]{1,0:T(8,128)(2,1)S(1)} %get-tuple-element.55), channel_id=1, source_target_pairs={{0,16},{16,0},{32,48},{48,32},{1,17},{17,1},{33,49},{49,33},{2,18}... | collective-permute-start | bytes 98312 | tf_op jit(solution)/shard_map/ppermute | solution.py:29
  43.0 7.4 %all-to-all-done.1.refs_0_ = bf16[32,16,384]{2,1,0:T(8,128)(2,1)S(1)} async-done(((bf16[32,16,384]{2,1,0:T(8,128)(2,1)}), bf16[32,16,384]{2,1,0:T(8,128)(2,1)S(1)}, u32[]{:S(2)}, u32[]{:S(2)}) %all-to-all-start.1) | async-done | bytes 393248 | tf_op jit(solution)/shard_map/all_to_all | solution.py:37
  50.5 1.5 %collective-permute-start.5 = (bf16[32,256]{1,0:T(8,128)(2,1)S(1)}, bf16[32,256]{1,0:T(8,128)(2,1)S(1)}, u32[]{:S(2)}, u32[]{:S(2)}) collective-permute-start(bf16[32,256]{1,0:T(8,128)(2,1)S(1)} %get-tuple-element.53), channel_id=1, source_target_pairs={{0,32},{16,48},{32,0},{48,16},{1,33},{17,49},{33,1},{49,17},{2,34}... | collective-permute-start | bytes 49160 | tf_op jit(solution)/shard_map/ppermute | solution.py:29
  52.7 2.6 %collective-permute-done.5.other = bf16[32,256]{1,0:T(8,128)(2,1)S(1)} collective-permute-done((bf16[32,256]{1,0:T(8,128)(2,1)S(1)}, bf16[32,256]{1,0:T(8,128)(2,1)S(1)}, u32[]{:S(2)}, u32[]{:S(2)}) %collective-permute-start.5) | collective-permute-done | bytes 16416 | tf_op jit(solution)/shard_map/ppermute | solution.py:29
  56.4 4.8 %all-to-all-start.2 = ((bf16[32,96,128]{2,1,0:T(8,128)(2,1)}), bf16[32,96,128]{2,1,0:T(8,128)(2,1)S(1)}, u32[]{:S(2)}, u32[]{:S(2)}) async-start(bf16[32,96,128]{2,1,0:T(8,128)(2,1)} %get-tuple-element.58), calls=%async_computation.2 | async-start | bytes 1572864 | tf_op jit(solution)/shard_map/all_to_all | solution.py:37
  62.6 1.4 %collective-permute-done.7.refs_1_ = bf16[192,384]{1,0:T(8,128)(2,1)S(1)} collective-permute-done((bf16[192,384]{1,0:T(8,128)(2,1)S(1)}, bf16[192,384]{1,0:T(8,128)(2,1)S(1)}, u32[]{:S(2)}, u32[]{:S(2)}) %collective-permute-start.7) | collective-permute-done | bytes 147488 | tf_op jit(solution)/shard_map/ppermute | solution.py:25
  64.2 1.5 %collective-permute-start.8 = (bf16[160,384]{1,0:T(8,128)(2,1)S(1)}, bf16[160,384]{1,0:T(8,128)(2,1)S(1)}, u32[]{:S(2)}, u32[]{:S(2)}) collective-permute-start(bf16[160,384]{1,0:T(8,128)(2,1)S(1)} %get-tuple-element.68), channel_id=1, source_target_pairs={{0,2},{2,0},{1,3},{3,1},{4,6},{6,4},{5,7},{7,5},{8,10},{10,8},{9,1... | collective-permute-start | bytes 368648 | tf_op jit(solution)/shard_map/ppermute | solution.py:25
  65.6 6.6 %all-to-all-done.2 = bf16[32,96,128]{2,1,0:T(8,128)(2,1)S(1)} async-done(((bf16[32,96,128]{2,1,0:T(8,128)(2,1)}), bf16[32,96,128]{2,1,0:T(8,128)(2,1)S(1)}, u32[]{:S(2)}, u32[]{:S(2)}) %all-to-all-start.2) | async-done | bytes 786464 | tf_op jit(solution)/shard_map/all_to_all | solution.py:37
  72.3 1.5 %collective-permute-start.10 = (bf16[96,128]{1,0:T(8,128)(2,1)S(1)}, bf16[96,128]{1,0:T(8,128)(2,1)S(1)}, u32[]{:S(2)}, u32[]{:S(2)}) collective-permute-start(bf16[96,128]{1,0:T(8,128)(2,1)S(1)} %reduce_sum.12.refs_0_), channel_id=1, source_target_pairs={{0,32},{16,48},{32,0},{48,16},{1,33},{17,49},{33,1},{49,17},{2,34}... | collective-permute-start | bytes 73736 | tf_op jit(solution)/shard_map/ppermute | solution.py:29
  73.8 3.7 %collective-permute-done.10.refs_1_ = bf16[96,128]{1,0:T(8,128)(2,1)S(1)} collective-permute-done((bf16[96,128]{1,0:T(8,128)(2,1)S(1)}, bf16[96,128]{1,0:T(8,128)(2,1)S(1)}, u32[]{:S(2)}, u32[]{:S(2)}) %collective-permute-start.10) | collective-permute-done | bytes 24608 | tf_op jit(solution)/shard_map/ppermute | solution.py:29
  78.5 4.7 %all-to-all-start.3 = ((bf16[32,96,128]{2,1,0:T(8,128)(2,1)}), bf16[32,96,128]{2,1,0:T(8,128)(2,1)S(1)}, u32[]{:S(2)}, u32[]{:S(2)}) async-start(bf16[32,96,128]{2,1,0:T(8,128)(2,1)} %settle.1), calls=%async_computation.3 | async-start | bytes 1572864 | tf_op jit(solution)/shard_map/all_to_all | solution.py:37
  83.9 1.3 %collective-permute-done.9.refs_1_ = bf16[128,384]{1,0:T(8,128)(2,1)S(1)} collective-permute-done((bf16[128,384]{1,0:T(8,128)(2,1)S(1)}, bf16[128,384]{1,0:T(8,128)(2,1)S(1)}, u32[]{:S(2)}, u32[]{:S(2)}) %collective-permute-start.9) | collective-permute-done | bytes 98336 | tf_op jit(solution)/shard_map/ppermute | solution.py:25
  85.9 9.3 %all-to-all-done.3.source = bf16[32,96,128]{2,1,0:T(8,128)(2,1)S(1)} async-done(((bf16[32,96,128]{2,1,0:T(8,128)(2,1)}), bf16[32,96,128]{2,1,0:T(8,128)(2,1)S(1)}, u32[]{:S(2)}, u32[]{:S(2)}) %all-to-all-start.3) | async-done | bytes 786464 | tf_op jit(solution)/shard_map/all_to_all | solution.py:37
  (42 shorter events, 9.5 us)
Async XLA Ops:
  0.6 2.8 %copy-start.7 = (bf16[64,192]{1,0:T(8,128)(2,1)S(1)}, bf16[64,192]{1,0:T(8,128)(2,1)}, u32[]{:S(2)}) copy-start(bf16[64,192]{1,0:T(8,128)(2,1)} %refs_4_.3) | copy-start | bytes 73732
  0.6 16.5 %collective-permute-start.2 = (bf16[64,192]{1,0:T(8,128)(2,1)}, bf16[64,192]{1,0:T(8,128)(2,1)S(1)}, u32[]{:S(2)}, u32[]{:S(2)}) collective-permute-start(bf16[64,192]{1,0:T(8,128)(2,1)} %refs_4_.3), channel_id=1, source_target_pairs={{0,1},{1,0},{2,3},{3,2},{4,5},{5,4},{6,7},{7,6},{8,9},{9,8},{10,11... | collective-permute-start | bytes 73736 | tf_op jit(solution)/shard_map/ppermute | solution.py:25
  0.7 25.9 %copy-start.4 = (bf16[192,384]{1,0:T(8,128)(2,1)S(1)}, bf16[192,384]{1,0:T(8,128)(2,1)}, u32[]{:S(2)}) copy-start(bf16[192,384]{1,0:T(8,128)(2,1)} %refs_9_.1) | copy-start | bytes 442372
  3.4 13.7 %collective-permute-start.1 = (bf16[64,192]{1,0:T(8,128)(2,1)S(1)}, bf16[64,192]{1,0:T(8,128)(2,1)S(1)}, u32[]{:S(2)}, u32[]{:S(2)}) collective-permute-start(bf16[64,192]{1,0:T(8,128)(2,1)S(1)} %copy-done.7), channel_id=1, source_target_pairs={{0,2},{2,0},{1,3},{3,1},{4,6},{6,4},{5,7},{7,5},{8,10},{10,8},{9,1... | collective-permute-start | bytes 73736 | tf_op jit(solution)/shard_map/ppermute | solution.py:25
  10.7 4.8 %collective-permute-start = (bf16[32,256]{1,0:T(8,128)(2,1)}, bf16[32,256]{1,0:T(8,128)(2,1)S(1)}, u32[]{:S(2)}, u32[]{:S(2)}) collective-permute-start(bf16[32,256]{1,0:T(8,128)(2,1)} %get-tuple-element.41), channel_id=1, source_target_pairs={{0,32},{16,48},{32,0},{48,16},{1,33},{17,49},{33,1},{49,17},{2,34}... | collective-permute-start | bytes 49160 | tf_op jit(solution)/shard_map/ppermute | solution.py:29
  16.2 10.4 %copy-start.2 = (bf16[192,768]{1,0:T(8,128)(2,1)S(1)}, bf16[192,768]{1,0:T(8,128)(2,1)}, u32[]{:S(2)}) copy-start(bf16[192,768]{1,0:T(8,128)(2,1)} %refs_5_.1) | copy-start | bytes 884740
  16.2 10.4 %copy-start.3 = (bf16[256,384]{1,0:T(8,128)(2,1)S(1)}, bf16[256,384]{1,0:T(8,128)(2,1)}, u32[]{:S(2)}) copy-start(bf16[256,384]{1,0:T(8,128)(2,1)} %get-tuple-element.46.refs_1_.refs_6_) | copy-start | bytes 589828
  17.1 9.6 %copy-start = (bf16[3,192,384]{2,1,0:T(8,128)(2,1)S(1)}, bf16[3,192,384]{2,1,0:T(8,128)(2,1)}, u32[]{:S(2)}) copy-start(bf16[3,192,384]{2,1,0:T(8,128)(2,1)} %refs_3_.7) | copy-start | bytes 1327108
  17.1 9.6 %copy-start.1 = (bf16[256,384]{1,0:T(8,128)(2,1)S(1)}, bf16[256,384]{1,0:T(8,128)(2,1)}, u32[]{:S(2)}) copy-start(bf16[256,384]{1,0:T(8,128)(2,1)} %get-tuple-element.45.refs_0_.refs_2_.held) | copy-start | bytes 589828
  17.1 9.6 %copy-start.9 = (bf16[4,192]{1,0:T(4,128)(2,1)S(1)}, bf16[4,192]{1,0:T(4,128)(2,1)}, u32[]{:S(2)}) copy-start(bf16[4,192]{1,0:T(4,128)(2,1)} %refs_3_.6) | copy-start | bytes 4612
  17.1 17.0 %all-to-all-start = ((bf16[32,16,384]{2,1,0:T(8,128)(2,1)}), bf16[32,16,384]{2,1,0:T(8,128)(2,1)S(1)}, u32[]{:S(2)}, u32[]{:S(2)}) async-start(bf16[32,16,384]{2,1,0:T(8,128)(2,1)} %copy_pair.1), calls=%async_computation | async-start | bytes 786432 | tf_op jit(solution)/shard_map/all_to_all | solution.py:37
  25.3 1.3 %collective-permute-start.3 = (bf16[64,192]{1,0:T(8,128)(2,1)S(1)}, bf16[64,192]{1,0:T(8,128)(2,1)S(1)}, u32[]{:S(2)}, u32[]{:S(2)}) collective-permute-start(bf16[64,192]{1,0:T(8,128)(2,1)S(1)} %collective-permute-done.1.refs_6_), channel_id=1, source_target_pairs={{0,1},{1,0},{2,3},{3,2},{4,5},{5,4},{6,7},{7,6},{8,9},{9,8},{10,11... | collective-permute-start | bytes 73736 | tf_op jit(solution)/shard_map/ppermute | solution.py:25
  27.3 4.0 %collective-permute-start.4 = (bf16[64,256]{1,0:T(8,128)(2,1)S(1)}, bf16[64,256]{1,0:T(8,128)(2,1)S(1)}, u32[]{:S(2)}, u32[]{:S(2)}) collective-permute-start(bf16[64,256]{1,0:T(8,128)(2,1)S(1)} %get-tuple-element.50), channel_id=1, source_target_pairs={{0,16},{16,0},{32,48},{48,32},{1,17},{17,1},{33,49},{49,33},{2,18}... | collective-permute-start | bytes 98312 | tf_op jit(solution)/shard_map/ppermute | solution.py:29
  35.9 14.5 %all-to-all-start.1 = ((bf16[32,16,384]{2,1,0:T(8,128)(2,1)}), bf16[32,16,384]{2,1,0:T(8,128)(2,1)S(1)}, u32[]{:S(2)}, u32[]{:S(2)}) async-start(bf16[32,16,384]{2,1,0:T(8,128)(2,1)} %get-tuple-element.51), calls=%async_computation.1 | async-start | bytes 786432 | tf_op jit(solution)/shard_map/all_to_all | solution.py:37
  41.4 10.6 %collective-permute-start.6 = (bf16[64,256]{1,0:T(8,128)(2,1)S(1)}, bf16[64,256]{1,0:T(8,128)(2,1)S(1)}, u32[]{:S(2)}, u32[]{:S(2)}) collective-permute-start(bf16[64,256]{1,0:T(8,128)(2,1)S(1)} %get-tuple-element.55), channel_id=1, source_target_pairs={{0,16},{16,0},{32,48},{48,32},{1,17},{17,1},{33,49},{49,33},{2,18}... | collective-permute-start | bytes 98312 | tf_op jit(solution)/shard_map/ppermute | solution.py:29
  50.5 4.7 %collective-permute-start.5 = (bf16[32,256]{1,0:T(8,128)(2,1)S(1)}, bf16[32,256]{1,0:T(8,128)(2,1)S(1)}, u32[]{:S(2)}, u32[]{:S(2)}) collective-permute-start(bf16[32,256]{1,0:T(8,128)(2,1)S(1)} %get-tuple-element.53), channel_id=1, source_target_pairs={{0,32},{16,48},{32,0},{48,16},{1,33},{17,49},{33,1},{49,17},{2,34}... | collective-permute-start | bytes 49160 | tf_op jit(solution)/shard_map/ppermute | solution.py:29
  52.1 3.2 %copy-start.5 = (bf16[16,192]{1,0:T(8,128)(2,1)S(1)}, bf16[16,192]{1,0:T(8,128)(2,1)}, u32[]{:S(2)}) copy-start(bf16[16,192]{1,0:T(8,128)(2,1)} %key_taps.1) | copy-start | bytes 18436
  52.1 3.2 %copy-start.6 = (bf16[16,192]{1,0:T(8,128)(2,1)S(1)}, bf16[16,192]{1,0:T(8,128)(2,1)}, u32[]{:S(2)}) copy-start(bf16[16,192]{1,0:T(8,128)(2,1)} %value_taps.1) | copy-start | bytes 18436
  56.4 15.8 %all-to-all-start.2 = ((bf16[32,96,128]{2,1,0:T(8,128)(2,1)}), bf16[32,96,128]{2,1,0:T(8,128)(2,1)S(1)}, u32[]{:S(2)}, u32[]{:S(2)}) async-start(bf16[32,96,128]{2,1,0:T(8,128)(2,1)} %get-tuple-element.58), calls=%async_computation.2 | async-start | bytes 1572864 | tf_op jit(solution)/shard_map/all_to_all | solution.py:37
  62.5 1.5 %collective-permute-start.7 = (bf16[192,384]{1,0:T(8,128)(2,1)S(1)}, bf16[192,384]{1,0:T(8,128)(2,1)S(1)}, u32[]{:S(2)}, u32[]{:S(2)}) collective-permute-start(bf16[192,384]{1,0:T(8,128)(2,1)S(1)} %get-tuple-element.65), channel_id=1, source_target_pairs={{0,1},{1,0},{2,3},{3,2},{4,5},{5,4},{6,7},{7,6},{8,9},{9,8},{10,11... | collective-permute-start | bytes 442376 | tf_op jit(solution)/shard_map/ppermute | solution.py:25
  64.2 19.0 %collective-permute-start.8 = (bf16[160,384]{1,0:T(8,128)(2,1)S(1)}, bf16[160,384]{1,0:T(8,128)(2,1)S(1)}, u32[]{:S(2)}, u32[]{:S(2)}) collective-permute-start(bf16[160,384]{1,0:T(8,128)(2,1)S(1)} %get-tuple-element.68), channel_id=1, source_target_pairs={{0,2},{2,0},{1,3},{3,1},{4,6},{6,4},{5,7},{7,5},{8,10},{10,8},{9,1... | collective-permute-start | bytes 368648 | tf_op jit(solution)/shard_map/ppermute | solution.py:25
  72.3 5.2 %collective-permute-start.10 = (bf16[96,128]{1,0:T(8,128)(2,1)S(1)}, bf16[96,128]{1,0:T(8,128)(2,1)S(1)}, u32[]{:S(2)}, u32[]{:S(2)}) collective-permute-start(bf16[96,128]{1,0:T(8,128)(2,1)S(1)} %reduce_sum.12.refs_0_), channel_id=1, source_target_pairs={{0,32},{16,48},{32,0},{48,16},{1,33},{17,49},{33,1},{49,17},{2,34}... | collective-permute-start | bytes 73736 | tf_op jit(solution)/shard_map/ppermute | solution.py:29
  78.5 16.8 %all-to-all-start.3 = ((bf16[32,96,128]{2,1,0:T(8,128)(2,1)}), bf16[32,96,128]{2,1,0:T(8,128)(2,1)S(1)}, u32[]{:S(2)}, u32[]{:S(2)}) async-start(bf16[32,96,128]{2,1,0:T(8,128)(2,1)} %settle.1), calls=%async_computation.3 | async-start | bytes 1572864 | tf_op jit(solution)/shard_map/all_to_all | solution.py:37
  83.9 1.3 %collective-permute-start.9 = (bf16[128,384]{1,0:T(8,128)(2,1)S(1)}, bf16[128,384]{1,0:T(8,128)(2,1)S(1)}, u32[]{:S(2)}, u32[]{:S(2)}) collective-permute-start(bf16[128,384]{1,0:T(8,128)(2,1)S(1)} %get-tuple-element.72.refs_0_), channel_id=1, source_target_pairs={{0,1},{1,0},{2,3},{3,2},{4,5},{5,4},{6,7},{7,6},{8,9},{9,8},{10,11... | collective-permute-start | bytes 294920 | tf_op jit(solution)/shard_map/ppermute | solution.py:25
  (2 other events, 1.4 us)
